TPU v7x, 32 devices: a whole 2x2x4 slice. The times are simulated.
32 devices in a mesh: paths: 2 (over x), node: 16 (over z, y, core).
Axes of the slice: x: 2, y: 2, z: 4, core: 2. Of those that a mesh axis runs over, the one named last changes fastest.
Arguments:
- amplitudes: float32 [2, 2097152], P(None, ('paths', 'node')), parts along dimension 1, may hold values from -6 to 6
- gates: float32 [2, 12, 128, 128], replicated, may hold values from -0.375 to 0.375
Outputs:
- final_state: float32 [2, 2097152], P(None, ('paths', 'node')), parts along dimension 1
There are 2 independent parts, one for each index of `paths`. A program takes and returns all parts, laid end to end along the dimension named above; an argument that names none is the same for every part. Nothing has to cross between parts.
All inputs are finite; a program needn't handle non-finite values.
Results may differ from a plain program's by a relative error of at most 0.0001.
Values sent between devices are 32-bit elements; how exact they have to be, the bound alone decides.
No kernel may reach another device: no remote copies, remote signals or barrier semaphores. Data moves between devices by JAX's collectives and lax.ppermute only.
A program may use at most 64 MiB of HBM per device.

v0:
```python
import functools

import jax
import jax.numpy as jnp
from jax import lax
from jax.experimental import pallas as pl
from jax.experimental.pallas import tpu as pltpu
from jax.sharding import PartitionSpec as P

F32, BF16 = jnp.float32, jnp.bfloat16
LANES = 128
PAIR = 2 * LANES
NT = (((1,), (1,)), ((), ()))
NN = (((1,), (0,)), ((), ()))
PORTS = (4, 2, 6)
VMEM = pl.BlockSpec(memory_space=pltpu.VMEM)
ANY = pl.BlockSpec(memory_space=pl.ANY)
HBM = pl.BlockSpec(memory_space=pltpu.HBM)


def halves(x):
    high = x.astype(BF16)
    return high, (x - high.astype(F32)).astype(BF16)


def product(a, b, dims):
    (ah, al), (bh, bl) = a, b
    dot = functools.partial(lax.dot_general, dimension_numbers=dims, preferred_element_type=F32)
    return dot(ah, bh) + (dot(al, bh) + dot(ah, bl))


def natural_gate(g):
    return g[0], g[1]


def regrouped_gate(g):
    order = lax.broadcasted_iota(jnp.int32, (LANES, LANES), 1)
    order = (order % 16) * 8 + order // 16
    out = []
    for c in range(2):
        rows = jnp.concatenate([g[c, pl.ds(m, 16, stride=8), :] for m in range(8)], 0)
        out.append(jnp.take_along_axis(rows, order, axis=1))
    return out


def prepare(g, regroup, mh, ml):
    re, im = regrouped_gate(g) if regroup else natural_gate(g)
    for r, row in enumerate(((re, -im), (im, re))):
        for c, part in enumerate(row):
            high, low = halves(part)
            at = (pl.ds(r * LANES, LANES), pl.ds(c * LANES, LANES))
            mh[at] = high
            ml[at] = low


def right_gate(x_re, x_im, m):
    out = product(halves(jnp.concatenate([x_re, x_im], 1)), m, NT)
    return out[:, :LANES], out[:, LANES:]


def left_gate(x_re, x_im, m):
    out = product(m, halves(jnp.concatenate([x_re, x_im], 0)), NN)
    return out[:LANES], out[LANES:]


def exchange(blocks):
    blocks = list(blocks)
    lane = lax.broadcasted_iota(jnp.int32, blocks[0].shape, 1)
    for bit, shift in ((4, 64), (2, 32), (1, 16)):
        low = (lane & shift) == 0
        for k in range(8):
            if k & bit == 0:
                a, b = blocks[k], blocks[k | bit]
                t = jnp.where(low, b, a)
                t = pltpu.roll(t, 64, 1) if shift == 64 else jnp.take_along_axis(t, lane ^ shift, axis=1)
                blocks[k] = jnp.where(low, a, t)
                blocks[k | bit] = jnp.where(low, t, b)
    return blocks


def high_gate(s, m):
    for pair in range(2):
        bs = (2 * pair, 2 * pair + 1)
        x = [jnp.concatenate([s[c, pl.ds(b, LANES, stride=4), :] for b in bs], 1) for c in range(2)]
        y = left_gate(*x, m)
        for c in range(2):
            for k, b in enumerate(bs):
                s[c, pl.ds(b, LANES, stride=4), :] = y[c][:, k * LANES : (k + 1) * LANES]


def upper_gate(s, m, store):
    for pair in range(2):
        bs = (2 * pair, 2 * pair + 1)
        x = [jnp.concatenate([s[c, pl.ds(b * LANES, LANES), :] for b in bs], 1) for c in range(2)]
        y = left_gate(*x, m)
        for c in range(2):
            for k, b in enumerate(bs):
                store(c, b * LANES, y[c][:, k * LANES : (k + 1) * LANES])


def middle_gate(s, m):
    count = s.shape[1] // LANES
    for first in range(0, count, 2):
        bs = tuple(range(first, min(first + 2, count)))
        x = [
            jnp.concatenate(
                [
                    jnp.concatenate(exchange([s[c, pl.ds(b * LANES + 16 * k, 16), :] for k in range(8)]), 0)
                    for b in bs
                ],
                1,
            )
            for c in range(2)
        ]
        y = left_gate(*x, m)
        for c in range(2):
            for n, b in enumerate(bs):
                part = y[c][:, n * LANES : (n + 1) * LANES]
                back = exchange([part[16 * k : 16 * k + 16] for k in range(8)])
                s[c, pl.ds(b * LANES, LANES), :] = jnp.concatenate(back, 0)


def low_gate(s, m):
    count = s.shape[1]
    for first in range(0, count, PAIR):
        at = pl.ds(first, min(PAIR, count - first))
        y = right_gate(s[0, at, :], s[1, at, :], m)
        for c in range(2):
            s[c, at, :] = y[c]


def keeper(s):
    def store(c, row, value):
        s[c, pl.ds(row, LANES), :] = value

    return store


def reversed3(v):
    return ((v & 1) << 2) | (v & 2) | ((v >> 2) & 1)


def rows_of(block, size):
    return pl.ds(pl.multiple_of(block * size, size), size)


def split(ref):
    return ref.at[0], ref.at[1]


class Gates:
    def __init__(self, source, scratch, indices):
        self.own, self.sems, self.mh, self.ml = scratch
        self.indices = indices
        self.copies = [
            pltpu.make_async_copy(source.at[:, g], self.own.at[k], self.sems.at[k]) for k, g in enumerate(indices)
        ]

    def start(self, ks):
        for k in ks:
            self.copies[k].start()

    def ready(self, ks):
        for k in ks:
            self.copies[k].wait()
        for k in ks:
            prepare(self.own.at[k], self.indices[k] % 4 == 1, self.mh.at[k], self.ml.at[k])

    def __getitem__(self, g):
        k = self.indices.index(g)
        return self.mh[k], self.ml[k]


def first_kernel(indices, me_ref, amps, gates, keep, send, s, own, sems, mh, ml, x, xsems):
    g = Gates(gates, (own, sems, mh, ml), indices)
    parts = []
    for b in range(2):
        at = pl.ds(2 * PAIR * b, 2 * PAIR)
        parts.append(pltpu.make_async_copy(amps.at[at], x.at[at], xsems.at[b]))
    g.start([0])
    for part in parts:
        part.start()
    g.start(range(1, len(indices)))
    low3 = me_ref[0] & 7
    g.ready([0])
    for b in range(2):
        parts[b].wait()
        y = right_gate(*[x[pl.ds(2 * PAIR * b + c, PAIR, stride=2), :] for c in range(2)], g[0])
        for c in range(2):
            s[c, pl.ds(b * PAIR, PAIR), :] = y[c]
    g.ready(range(1, len(indices)))
    middle_gate(s, g[1])
    high_gate(s, g[2])
    upper_gate(s, g[3], keeper(s))
    low_gate(s, g[4])
    middle_gate(s, g[5])
    for core, out in ((0, keep), (1, send)):
        ats = [rows_of(reversed3(low3 ^ (2 * p + core)), 64) for p in range(4)]
        y = right_gate(*[jnp.concatenate([s[c, at, :] for at in ats], 0) for c in range(2)], g[8])
        for p in range(4):
            for c in range(2):
                out[p, c] = y[c][64 * p : 64 * p + 64]


def second_kernel(indices, me_ref, keep0, recv0, r1, r2, r3, gates, own6, give, y1, self0, s, own, sems, mh, ml):
    g = Gates(gates, (own, sems, mh, ml), indices)
    g.start(range(3))
    me = me_ref[0]
    low3, core = me & 7, me & 1
    for p, part in enumerate(((keep0, recv0), split(r1), split(r2), split(r3))):
        for e in range(2):
            at = rows_of(reversed3(low3 ^ (2 * p + e)), 64)
            for c in range(2):
                s[c, at, :] = part[e][c]
    g.ready(range(3))
    high_gate(s, g[6])
    upper_gate(s, g[7], keeper(s))
    middle_gate(s, g[9])

    def write(out, first, mask, parts=(0, 1)):
        at = rows_of(me ^ mask, 32)
        for n, c in enumerate(parts):
            out[first + n] = s[c, at, :]

    for i, base in enumerate(PORTS):
        for f in range(2):
            write(own6.at[i, f], 0, 2 * (base + core) + f)
            write(give, 4 * i + 2 * f, 2 * (base + 1 - core) + (1 - f))
    write(give, 12, 3, (0,))
    write(give, 13, 1)
    write(y1, 0, 2)
    write(y1, 2, 3, (1,))
    write(self0, 0, 0)


def third_kernel(indices, me_ref, a0, a1, a2, y1, other, early, late, self0, gates, out, s, own, sems, mh, ml, y, ysems):
    g = Gates(gates, (own, sems, mh, ml), indices)
    g.start(range(2))
    me = me_ref[0]
    core = me & 1

    def place(part, first, mask, parts=(0, 1)):
        at = rows_of(me ^ mask, 32)
        for n, c in enumerate(parts):
            s[c, at, :] = part[first + n]

    for i, (base, arrived) in enumerate(zip(PORTS, (a0, a1, a2))):
        for src in range(2):
            place(arrived.at[0, src], 0, 2 * (base + core) + src)
            post, first = (early, 4 * i) if i < 2 else (late, 0)
            place(post, first + 2 * src, 2 * (base + 1 - core) + (1 - src))
    place(y1, 0, 2)
    place(y1, 3, 3, (0,))
    place(early, 8, 3, (1,))
    place(other, 0, 1)
    place(self0, 0, 0)
    g.ready(range(2))
    high_gate(s, g[10])
    copies = []

    def store(c, row, value):
        y[pl.ds(2 * row + c, LANES, stride=2), :] = value
        if c == 1 and row % PAIR == LANES:
            at = pl.ds(2 * (row - LANES), 2 * PAIR)
            copies.append(pltpu.make_async_copy(y.at[at], out.at[at], ysems.at[len(copies)]))
            copies[-1].start()

    upper_gate(s, g[11], store)
    for copy in copies:
        copy.wait()


def shape(*dims):
    return jax.ShapeDtypeStruct(dims, F32)


def call(kernel, indices, outs, rows, operands, specs, scratch=(), out_specs=None, limit=32 << 20):
    n = len(indices)
    return pl.pallas_call(
        functools.partial(kernel, indices),
        out_shape=outs,
        in_specs=[pl.BlockSpec(memory_space=pltpu.SMEM)] + specs,
        out_specs=out_specs or [VMEM] * len(outs),
        scratch_shapes=[
            pltpu.VMEM((2, rows, LANES), F32),
            pltpu.VMEM((n, 2, LANES, LANES), F32),
            pltpu.SemaphoreType.DMA((n,)),
            pltpu.VMEM((n, PAIR, PAIR), BF16),
            pltpu.VMEM((n, PAIR, PAIR), BF16),
            *scratch,
        ],
        compiler_params=pltpu.CompilerParams(vmem_limit_bytes=limit),
        name=kernel.__name__,
    )(*operands)


def flipped(block, mask, port=0):
    route = [(i, i ^ mask ^ (port if i & 1 else 0)) for i in range(lax.axis_size("node"))]
    return lax.ppermute(block, "node", route)


def fast_body(amplitudes, gates):
    total = amplitudes.shape[1]
    rows = total // LANES
    eighth, part16 = rows // 8, rows // 16
    me = lax.axis_index("node").astype(jnp.int32).reshape(1)
    x = amplitudes.reshape(2, rows, LANES).transpose(1, 0, 2).reshape(2 * rows, LANES)
    interleaved = (pltpu.VMEM((2 * rows, LANES), F32), pltpu.SemaphoreType.DMA((2,)))
    half = shape(4, 2, eighth, LANES)
    keep, send = call(
        first_kernel, (0, 1, 2, 3, 4, 5, 8), [half] * 2, rows, [me, x, gates], [HBM] * 2, interleaved, limit=532 * 104858
    )
    recv = flipped(send, 1)
    far = [flipped(jnp.stack([keep[p], recv[p]]), 2 * p) for p in (1, 2, 3)]
    block = (part16, LANES)
    own, give, y1, self0 = call(
        second_kernel,
        (6, 7, 9),
        [shape(3, 2, 2, *block), shape(15, *block), shape(3, *block), shape(2, *block)],
        rows,
        [me, keep[0], recv[0], *far, gates],
        [VMEM] * 5 + [HBM],
    )
    recv = flipped(give, 1)
    arrived = [
        flipped(jnp.stack([own[i], recv[4 * i : 4 * i + 4].reshape(2, 2, *block)], 1), 2 * base, 2)
        for i, base in enumerate(PORTS)
    ]
    y1 = flipped(jnp.concatenate([y1, recv[12:13]]), 2)
    early = [a[1].reshape(4, *block) for a in arrived]
    late = flipped(early[2], 1)
    early = flipped(jnp.concatenate(early[:2] + [y1[2:3]]), 1)
    out = call(
        third_kernel,
        (10, 11),
        [shape(2 * rows, LANES)],
        rows,
        [me, *arrived, y1, recv[13:], early, late, self0, gates],
        [VMEM] * 8 + [HBM],
        interleaved,
        [HBM],
    )[0]
    return out.reshape(rows, 2, LANES).transpose(1, 0, 2).reshape(2, total)


def swapped(block, axis, apart):
    count = lax.axis_size(axis)
    route = []
    for low in range(count):
        high = low | 1 << apart
        if high != low and high < count:
            route += [(low, high), (high, low)]
    return lax.ppermute(block, axis, route)


def apply_gate(state, gate_pair, offset):
    total = state.shape[1]
    real_g, imag_g = (gate_pair[0], gate_pair[1])
    hp = lax.Precision.HIGHEST
    if offset == 0:
        view = state.reshape(2, total // 128, 128)
        real_in, imag_in = (view[0], view[1])
        real_out = jnp.einsum("ij,aj->ai", real_g, real_in, precision=hp) - jnp.einsum(
            "ij,aj->ai", imag_g, imag_in, precision=hp
        )
        imag_out = jnp.einsum("ij,aj->ai", real_g, imag_in, precision=hp) + jnp.einsum(
            "ij,aj->ai", imag_g, real_in, precision=hp
        )
        return jnp.stack([real_out, imag_out], 0).reshape(2, total)
    inner = 1 << offset
    outer = total // (128 * inner)
    folded = 1
    if inner < 128:
        folded = min(128 // inner, outer)
    view = state.reshape(2, outer // folded, folded, 128, inner)
    view = jnp.transpose(view, (0, 1, 3, 2, 4)).reshape(2, outer // folded, 128, folded * inner)
    real_in, imag_in = (view[0], view[1])
    real_out = jnp.einsum("ij,ajb->aib", real_g, real_in, precision=hp) - jnp.einsum(
        "ij,ajb->aib", imag_g, imag_in, precision=hp
    )
    imag_out = jnp.einsum("ij,ajb->aib", real_g, imag_in, precision=hp) + jnp.einsum(
        "ij,ajb->aib", imag_g, real_in, precision=hp
    )
    result = jnp.stack([real_out, imag_out], 0).reshape(2, outer // folded, 128, folded, inner)
    return jnp.transpose(result, (0, 1, 3, 2, 4)).reshape(2, total)


def run_gates(state, gates, indices, offsets):
    distinct = gates.shape[1]
    for index, offset in zip(indices, offsets):
        state = apply_gate(state, gates[:, index % distinct], offset)
    return state


def leave_alone(half):
    return half


def split_halves(state, position, bit):
    total = state.shape[1]
    mine = lax.axis_index("node") // (1 << bit) % 2
    view = state.reshape(2, total >> position + 1, 2, 1 << position)
    keep = lax.dynamic_index_in_dim(view, mine, 2, keepdims=False)
    other = lax.dynamic_index_in_dim(view, 1 - mine, 2, keepdims=False)
    return (mine, keep, other)


def join_halves(mine, keep, arrived, total):
    lower = jnp.where(mine == 0, keep, arrived)
    upper = jnp.where(mine == 0, arrived, keep)
    return jnp.stack([lower, upper], 2).reshape(2, total)


def enter_bit(state, position, bit, prepare):
    total = state.shape[1]
    mine, keep, other = split_halves(state, position, bit)
    other = prepare(other.reshape(2, total // 2)).reshape(keep.shape)
    arrived = swapped(other, "node", bit)
    keep = prepare(keep.reshape(2, total // 2)).reshape(arrived.shape)
    return join_halves(mine, keep, arrived, total)


def general_body(amplitudes, gates):
    total = amplitudes.shape[1]
    locq = total.bit_length() - 1
    devices_node = lax.axis_size("node")
    offsets = [0, (locq - 7) // 2, locq - 7, locq - 9]
    state = run_gates(amplitudes, gates, [0, 1, 2, 3], offsets)

    def early_gates(half):
        return run_gates(half, gates, [4, 5], offsets[:2])

    state = enter_bit(state, locq - 1, 0, early_gates)
    for bit in range(1, 3):
        state = enter_bit(state, locq - 1 - bit, bit, leave_alone)
    state = run_gates(state, gates, [6, 7], offsets[2:])
    blocks = state.reshape(2, devices_node, total // devices_node)
    blocks = lax.all_to_all(blocks, "node", split_axis=1, concat_axis=1, tiled=True)
    state = blocks.reshape(2, total)
    return run_gates(state, gates, [8, 9, 10, 11], offsets)


def body(amplitudes, gates):
    if amplitudes.shape[1] == 65536 and lax.axis_size("node") == 16 and gates.shape[1] == 12:
        return fast_body(amplitudes, gates)
    return general_body(amplitudes, gates)


def solution(mesh):
    in_specs = (P(None, ("paths", "node")), P())
    out_specs = P(None, ("paths", "node"))
    return jax.shard_map(body, mesh=mesh, in_specs=in_specs, out_specs=out_specs, check_vma=False)
```

profile of v0, /device:TPU:19, one launch (start us, length us, event | category | flops | bytes accessed | tf_op | source)
XLA Modules:
  0.0 39.5 jit_solution(7686525666491299152)
XLA Ops:
  0.0 0.0 copy-start
  0.0 5.4 %first_kernel.1 = (f32[4,2,64,128]{3,2,1,0:T(8,128)S(1)}, f32[4,2,64,128]{3,2,1,0:T(8,128)S(1)}) custom-call(s32[1]{0:T(128)} %bitcast.me_ref, f32[1024,128]{1,0:T(8,128)} %bitcast.33, f32[2,12,128,128]{3,2,1,0:T(8,128)} %gates.5), custom_call_target="tpu_custom_call" | custom-call | tf_op jit(solution)/shard_map/first_kernel/pallas_call | solution.py:279
  5.4 0.7 %collective-permute-start = (f32[4,2,64,128]{3,2,1,0:T(8,128)S(1)}, f32[4,2,64,128]{3,2,1,0:T(8,128)S(1)}, u32[]{:S(2)}, u32[]{:S(2)}) collective-permute-start(f32[4,2,64,128]{3,2,1,0:T(8,128)S(1)} %get-tuple-element.12), channel_id=1, source_target_pairs={{0,1},{1,0},{2,3},{3,2},{4,5},{5,4},{6,7},{7,6},{8,9},{9,8},{10,11... | collective-permute-start | bytes 786440 | tf_op jit(solution)/shard_map/ppermute | solution.py:299
  6.2 1.1 %collective-permute-done = f32[4,2,64,128]{3,2,1,0:T(8,128)S(1)} collective-permute-done((f32[4,2,64,128]{3,2,1,0:T(8,128)S(1)}, f32[4,2,64,128]{3,2,1,0:T(8,128)S(1)}, u32[]{:S(2)}, u32[]{:S(2)}) %collective-permute-start) | collective-permute-done | bytes 262176 | tf_op jit(solution)/shard_map/ppermute | solution.py:299
  7.4 1.3 %collective-permute-start.1 = (f32[2,2,64,128]{3,2,1,0:T(8,128)S(1)}, f32[2,2,64,128]{3,2,1,0:T(8,128)S(1)}, u32[]{:S(2)}, u32[]{:S(2)}) collective-permute-start(f32[2,2,64,128]{3,2,1,0:T(8,128)S(1)} %pad_maximum_fusion.1), channel_id=1, source_target_pairs={{0,2},{1,3},{2,0},{3,1},{4,6},{5,7},{6,4},{7,5},{8,10},{9,11},{10,... | collective-permute-start | bytes 393224 | tf_op jit(solution)/shard_map/ppermute | solution.py:299
  8.7 1.4 %collective-permute-start.2 = (f32[2,2,64,128]{3,2,1,0:T(8,128)S(1)}, f32[2,2,64,128]{3,2,1,0:T(8,128)S(1)}, u32[]{:S(2)}, u32[]{:S(2)}) collective-permute-start(f32[2,2,64,128]{3,2,1,0:T(8,128)S(1)} %pad_maximum_fusion.2), channel_id=1, source_target_pairs={{0,4},{1,5},{2,6},{3,7},{4,0},{5,1},{6,2},{7,3},{8,12},{9,13},{10,... | collective-permute-start | bytes 393224 | tf_op jit(solution)/shard_map/ppermute | solution.py:299
  10.1 0.2 collective-permute-start.3
  10.2 1.9 %collective-permute-done.1.r1 = f32[2,2,64,128]{3,2,1,0:T(8,128)S(1)} collective-permute-done((f32[2,2,64,128]{3,2,1,0:T(8,128)S(1)}, f32[2,2,64,128]{3,2,1,0:T(8,128)S(1)}, u32[]{:S(2)}, u32[]{:S(2)}) %collective-permute-start.1) | collective-permute-done | bytes 131104 | tf_op jit(solution)/shard_map/ppermute | solution.py:299
  12.1 1.0 %collective-permute-done.2.r2 = f32[2,2,64,128]{3,2,1,0:T(8,128)S(1)} collective-permute-done((f32[2,2,64,128]{3,2,1,0:T(8,128)S(1)}, f32[2,2,64,128]{3,2,1,0:T(8,128)S(1)}, u32[]{:S(2)}, u32[]{:S(2)}) %collective-permute-start.2) | collective-permute-done | bytes 131104 | tf_op jit(solution)/shard_map/ppermute | solution.py:299
  13.1 2.9 %collective-permute-done.3.r3 = f32[2,2,64,128]{3,2,1,0:T(8,128)S(1)} collective-permute-done((f32[2,2,64,128]{3,2,1,0:T(8,128)S(1)}, f32[2,2,64,128]{3,2,1,0:T(8,128)S(1)}, u32[]{:S(2)}, u32[]{:S(2)}) %collective-permute-start.3) | collective-permute-done | bytes 131104 | tf_op jit(solution)/shard_map/ppermute | solution.py:299
  16.0 0.0 copy-done
  16.0 2.0 %second_kernel.1 = (f32[3,2,2,32,128]{4,3,2,1,0:T(8,128)S(1)}, f32[15,32,128]{2,1,0:T(8,128)S(1)}, f32[3,32,128]{2,1,0:T(8,128)S(1)}, f32[2,32,128]{2,1,0:T(8,128)S(1)}) custom-call(s32[1]{0:T(128)} %bitcast.me_ref, f32[2,64,128]{2,1,0:T(8,128)S(1)} %get-tuple-element.20.keep0, f32[2,64,128]{2,1,0:T(8,128)S(1)} %get-tuple-element.24.recv0, ...), custom_call_target="tpu_custom_call" | custom-call | tf_op jit(solution)/shard_map/second_kernel/pallas_call | solution.py:279
  18.0 1.4 %collective-permute-start.4 = (f32[15,32,128]{2,1,0:T(8,128)S(1)}, f32[15,32,128]{2,1,0:T(8,128)S(1)}, u32[]{:S(2)}, u32[]{:S(2)}) collective-permute-start(f32[15,32,128]{2,1,0:T(8,128)S(1)} %get-tuple-element.14), channel_id=1, source_target_pairs={{0,1},{1,0},{2,3},{3,2},{4,5},{5,4},{6,7},{7,6},{8,9},{9,8},{10,11... | collective-permute-start | bytes 737288 | tf_op jit(solution)/shard_map/ppermute | solution.py:299
  19.5 1.1 %collective-permute-done.4 = f32[15,32,128]{2,1,0:T(8,128)S(1)} collective-permute-done((f32[15,32,128]{2,1,0:T(8,128)S(1)}, f32[15,32,128]{2,1,0:T(8,128)S(1)}, u32[]{:S(2)}, u32[]{:S(2)}) %collective-permute-start.4) | collective-permute-done | bytes 245792 | tf_op jit(solution)/shard_map/ppermute | solution.py:299
  20.6 1.1 %collective-permute-start.5 = (f32[2,2,2,32,128]{4,3,2,1,0:T(8,128)S(1)}, f32[2,2,2,32,128]{4,3,2,1,0:T(8,128)S(1)}, u32[]{:S(2)}, u32[]{:S(2)}) collective-permute-start(f32[2,2,2,32,128]{4,3,2,1,0:T(8,128)S(1)} %pad_maximum_fusion.4), channel_id=1, source_target_pairs={{0,8},{1,11},{2,10},{3,9},{4,12},{5,15},{6,14},{7,13},{8,0},{9,3},... | collective-permute-start | bytes 393224 | tf_op jit(solution)/shard_map/ppermute | solution.py:299
  21.7 1.3 %collective-permute-start.6 = (f32[2,2,2,32,128]{4,3,2,1,0:T(8,128)S(1)}, f32[2,2,2,32,128]{4,3,2,1,0:T(8,128)S(1)}, u32[]{:S(2)}, u32[]{:S(2)}) collective-permute-start(f32[2,2,2,32,128]{4,3,2,1,0:T(8,128)S(1)} %pad_maximum_fusion.5), channel_id=1, source_target_pairs={{0,4},{1,7},{2,6},{3,5},{4,0},{5,3},{6,2},{7,1},{8,12},{9,15},{10,... | collective-permute-start | bytes 393224 | tf_op jit(solution)/shard_map/ppermute | solution.py:299
  23.1 1.3 %collective-permute-start.8 = (f32[4,32,128]{2,1,0:T(8,128)S(1)}, f32[4,32,128]{2,1,0:T(8,128)S(1)}, u32[]{:S(2)}, u32[]{:S(2)}) collective-permute-start(f32[4,32,128]{2,1,0:T(8,128)S(1)} %pad_maximum_fusion.7), channel_id=1, source_target_pairs={{0,2},{1,3},{2,0},{3,1},{4,6},{5,7},{6,4},{7,5},{8,10},{9,11},{10,... | collective-permute-start | bytes 196616 | tf_op jit(solution)/shard_map/ppermute | solution.py:299
  24.4 1.3 %collective-permute-start.7 = (f32[2,2,2,32,128]{4,3,2,1,0:T(8,128)S(1)}, f32[2,2,2,32,128]{4,3,2,1,0:T(8,128)S(1)}, u32[]{:S(2)}, u32[]{:S(2)}) collective-permute-start(f32[2,2,2,32,128]{4,3,2,1,0:T(8,128)S(1)} %pad_maximum_fusion.6), channel_id=1, source_target_pairs={{0,12},{1,15},{2,14},{3,13},{4,8},{5,11},{6,10},{7,9},{8,4},{9,7},... | collective-permute-start | bytes 393224 | tf_op jit(solution)/shard_map/ppermute | solution.py:299
  25.7 3.7 %collective-permute-done.8.y1 = f32[4,32,128]{2,1,0:T(8,128)S(1)} collective-permute-done((f32[4,32,128]{2,1,0:T(8,128)S(1)}, f32[4,32,128]{2,1,0:T(8,128)S(1)}, u32[]{:S(2)}, u32[]{:S(2)}) %collective-permute-start.8) | collective-permute-done | bytes 65568 | tf_op jit(solution)/shard_map/ppermute | solution.py:299
  29.4 0.0 collective-permute-done.5.a0
  29.4 0.0 collective-permute-done.6.a1
  29.4 0.7 %collective-permute-start.9 = (f32[9,32,128]{2,1,0:T(8,128)S(1)}, f32[9,32,128]{2,1,0:T(8,128)S(1)}, u32[]{:S(2)}, u32[]{:S(2)}) collective-permute-start(f32[9,32,128]{2,1,0:T(8,128)S(1)} %pad_maximum_fusion), channel_id=1, source_target_pairs={{0,1},{1,0},{2,3},{3,2},{4,5},{5,4},{6,7},{7,6},{8,9},{9,8},{10,11... | collective-permute-start | bytes 442376 | tf_op jit(solution)/shard_map/ppermute | solution.py:299
  30.1 6.0 %collective-permute-done.7.a2 = f32[2,2,2,32,128]{4,3,2,1,0:T(8,128)S(1)} collective-permute-done((f32[2,2,2,32,128]{4,3,2,1,0:T(8,128)S(1)}, f32[2,2,2,32,128]{4,3,2,1,0:T(8,128)S(1)}, u32[]{:S(2)}, u32[]{:S(2)}) %collective-permute-start.7) | collective-permute-done | bytes 131104 | tf_op jit(solution)/shard_map/ppermute | solution.py:299
  36.1 0.7 %collective-permute-start.10 = (f32[4,32,128]{2,1,0:T(8,128)S(1)}, f32[4,32,128]{2,1,0:T(8,128)S(1)}, u32[]{:S(2)}, u32[]{:S(2)}) collective-permute-start(f32[4,32,128]{2,1,0:T(8,128)S(1)} %bitcast.39), channel_id=1, source_target_pairs={{0,1},{1,0},{2,3},{3,2},{4,5},{5,4},{6,7},{7,6},{8,9},{9,8},{10,11... | collective-permute-start | bytes 196616 | tf_op jit(solution)/shard_map/ppermute | solution.py:299
  36.8 0.9 %collective-permute-done.10.late = f32[4,32,128]{2,1,0:T(8,128)S(1)} collective-permute-done((f32[4,32,128]{2,1,0:T(8,128)S(1)}, f32[4,32,128]{2,1,0:T(8,128)S(1)}, u32[]{:S(2)}, u32[]{:S(2)}) %collective-permute-start.10) | collective-permute-done | bytes 65568 | tf_op jit(solution)/shard_map/ppermute | solution.py:299
  37.7 0.0 collective-permute-done.9.early
  37.7 1.8 %third_kernel.1 = f32[1024,128]{1,0:T(8,128)} custom-call(s32[1]{0:T(128)} %bitcast.me_ref, f32[2,2,2,32,128]{4,3,2,1,0:T(8,128)S(1)} %collective-permute-done.5.a0, f32[2,2,2,32,128]{4,3,2,1,0:T(8,128)S(1)} %collective-permute-done.6.a1, f32[2,2,2,32,128]{4,3,2,1,0:T(8,128)S(1)} %collective-permute-done.7.a2, f32[4,32,128]{2,1,0:T(8,128)S(1)} %collective-permute-done.8.y1, ...), custom_call_target="tpu_custom_call" | custom-call | tf_op jit(solution)/shard_map/third_kernel/pallas_call | solution.py:279
  (18 shorter events, 0.2 us)
Async XLA Ops:
  0.0 16.0 %copy-start = (f32[2,12,128,128]{3,2,1,0:T(8,128)S(1)}, f32[2,12,128,128]{3,2,1,0:T(8,128)}, u32[]{:S(2)}) copy-start(f32[2,12,128,128]{3,2,1,0:T(8,128)} %gates.5) | copy-start | bytes 4718596
  5.4 1.9 %collective-permute-start = (f32[4,2,64,128]{3,2,1,0:T(8,128)S(1)}, f32[4,2,64,128]{3,2,1,0:T(8,128)S(1)}, u32[]{:S(2)}, u32[]{:S(2)}) collective-permute-start(f32[4,2,64,128]{3,2,1,0:T(8,128)S(1)} %get-tuple-element.12), channel_id=1, source_target_pairs={{0,1},{1,0},{2,3},{3,2},{4,5},{5,4},{6,7},{7,6},{8,9},{9,8},{10,11... | collective-permute-start | bytes 786440 | tf_op jit(solution)/shard_map/ppermute | solution.py:299
  7.4 4.8 %collective-permute-start.1 = (f32[2,2,64,128]{3,2,1,0:T(8,128)S(1)}, f32[2,2,64,128]{3,2,1,0:T(8,128)S(1)}, u32[]{:S(2)}, u32[]{:S(2)}) collective-permute-start(f32[2,2,64,128]{3,2,1,0:T(8,128)S(1)} %pad_maximum_fusion.1), channel_id=1, source_target_pairs={{0,2},{1,3},{2,0},{3,1},{4,6},{5,7},{6,4},{7,5},{8,10},{9,11},{10,... | collective-permute-start | bytes 393224 | tf_op jit(solution)/shard_map/ppermute | solution.py:299
  8.7 4.5 %collective-permute-start.2 = (f32[2,2,64,128]{3,2,1,0:T(8,128)S(1)}, f32[2,2,64,128]{3,2,1,0:T(8,128)S(1)}, u32[]{:S(2)}, u32[]{:S(2)}) collective-permute-start(f32[2,2,64,128]{3,2,1,0:T(8,128)S(1)} %pad_maximum_fusion.2), channel_id=1, source_target_pairs={{0,4},{1,5},{2,6},{3,7},{4,0},{5,1},{6,2},{7,3},{8,12},{9,13},{10,... | collective-permute-start | bytes 393224 | tf_op jit(solution)/shard_map/ppermute | solution.py:299
  10.1 6.0 %collective-permute-start.3 = (f32[2,2,64,128]{3,2,1,0:T(8,128)S(1)}, f32[2,2,64,128]{3,2,1,0:T(8,128)S(1)}, u32[]{:S(2)}, u32[]{:S(2)}) collective-permute-start(f32[2,2,64,128]{3,2,1,0:T(8,128)S(1)} %pad_maximum_fusion.3), channel_id=1, source_target_pairs={{0,6},{1,7},{2,4},{3,5},{4,2},{5,3},{6,0},{7,1},{8,14},{9,15},{10,... | collective-permute-start | bytes 393224 | tf_op jit(solution)/shard_map/ppermute | solution.py:299
  18.0 2.6 %collective-permute-start.4 = (f32[15,32,128]{2,1,0:T(8,128)S(1)}, f32[15,32,128]{2,1,0:T(8,128)S(1)}, u32[]{:S(2)}, u32[]{:S(2)}) collective-permute-start(f32[15,32,128]{2,1,0:T(8,128)S(1)} %get-tuple-element.14), channel_id=1, source_target_pairs={{0,1},{1,0},{2,3},{3,2},{4,5},{5,4},{6,7},{7,6},{8,9},{9,8},{10,11... | collective-permute-start | bytes 737288 | tf_op jit(solution)/shard_map/ppermute | solution.py:299
  20.6 8.7 %collective-permute-start.5 = (f32[2,2,2,32,128]{4,3,2,1,0:T(8,128)S(1)}, f32[2,2,2,32,128]{4,3,2,1,0:T(8,128)S(1)}, u32[]{:S(2)}, u32[]{:S(2)}) collective-permute-start(f32[2,2,2,32,128]{4,3,2,1,0:T(8,128)S(1)} %pad_maximum_fusion.4), channel_id=1, source_target_pairs={{0,8},{1,11},{2,10},{3,9},{4,12},{5,15},{6,14},{7,13},{8,0},{9,3},... | collective-permute-start | bytes 393224 | tf_op jit(solution)/shard_map/ppermute | solution.py:299
  21.7 7.6 %collective-permute-start.6 = (f32[2,2,2,32,128]{4,3,2,1,0:T(8,128)S(1)}, f32[2,2,2,32,128]{4,3,2,1,0:T(8,128)S(1)}, u32[]{:S(2)}, u32[]{:S(2)}) collective-permute-start(f32[2,2,2,32,128]{4,3,2,1,0:T(8,128)S(1)} %pad_maximum_fusion.5), channel_id=1, source_target_pairs={{0,4},{1,7},{2,6},{3,5},{4,0},{5,3},{6,2},{7,1},{8,12},{9,15},{10,... | collective-permute-start | bytes 393224 | tf_op jit(solution)/shard_map/ppermute | solution.py:299
  23.1 6.3 %collective-permute-start.8 = (f32[4,32,128]{2,1,0:T(8,128)S(1)}, f32[4,32,128]{2,1,0:T(8,128)S(1)}, u32[]{:S(2)}, u32[]{:S(2)}) collective-permute-start(f32[4,32,128]{2,1,0:T(8,128)S(1)} %pad_maximum_fusion.7), channel_id=1, source_target_pairs={{0,2},{1,3},{2,0},{3,1},{4,6},{5,7},{6,4},{7,5},{8,10},{9,11},{10,... | collective-permute-start | bytes 196616 | tf_op jit(solution)/shard_map/ppermute | solution.py:299
  24.4 11.7 %collective-permute-start.7 = (f32[2,2,2,32,128]{4,3,2,1,0:T(8,128)S(1)}, f32[2,2,2,32,128]{4,3,2,1,0:T(8,128)S(1)}, u32[]{:S(2)}, u32[]{:S(2)}) collective-permute-start(f32[2,2,2,32,128]{4,3,2,1,0:T(8,128)S(1)} %pad_maximum_fusion.6), channel_id=1, source_target_pairs={{0,12},{1,15},{2,14},{3,13},{4,8},{5,11},{6,10},{7,9},{8,4},{9,7},... | collective-permute-start | bytes 393224 | tf_op jit(solution)/shard_map/ppermute | solution.py:299
  29.4 8.3 %collective-permute-start.9 = (f32[9,32,128]{2,1,0:T(8,128)S(1)}, f32[9,32,128]{2,1,0:T(8,128)S(1)}, u32[]{:S(2)}, u32[]{:S(2)}) collective-permute-start(f32[9,32,128]{2,1,0:T(8,128)S(1)} %pad_maximum_fusion), channel_id=1, source_target_pairs={{0,1},{1,0},{2,3},{3,2},{4,5},{5,4},{6,7},{7,6},{8,9},{9,8},{10,11... | collective-permute-start | bytes 442376 | tf_op jit(solution)/shard_map/ppermute | solution.py:299
  36.1 1.6 %collective-permute-start.10 = (f32[4,32,128]{2,1,0:T(8,128)S(1)}, f32[4,32,128]{2,1,0:T(8,128)S(1)}, u32[]{:S(2)}, u32[]{:S(2)}) collective-permute-start(f32[4,32,128]{2,1,0:T(8,128)S(1)} %bitcast.39), channel_id=1, source_target_pairs={{0,1},{1,0},{2,3},{3,2},{4,5},{5,4},{6,7},{7,6},{8,9},{9,8},{10,11... | collective-permute-start | bytes 196616 | tf_op jit(solution)/shard_map/ppermute | solution.py:299
where the time goes:
time: 39.6 us; the launch traced here: 39.5 us
  waiting for transfers between devices  18.6 us (47%)
  starting transfers between devices  11.4 us (29%)
  Pallas kernels  9.17 us (23%)
    ppermute x11, waiting for transfers between devices, flipped(): return lax.ppermute(block, 'node', route)  18.6 us
    ppermute x11, starting transfers between devices, flipped(): return lax.ppermute(block, 'node', route)  11.4 us
    pallas_call x3, Pallas kernels, call(): pl.pallas_call(functools.partial(kernel, indices), out_shape=outs, in_spe...  9.17 us
  transfers between devices with their start and end apart: 11, of which 8 were waited for; matrix products, arithmetic and copies ran while one was open for 0% of the time, Pallas kernels for 0%

commit v1 on v0

--- a/solution.py
+++ b/solution.py
@@ -171,7 +171,19 @@
         return self.mh[k], self.ml[k]
 
 
-def first_kernel(indices, me_ref, amps, gates, keep, send, s, own, sems, mh, ml, x, xsems):
+class Ready:
+    def __init__(self, source, scratch, indices):
+        self.mh, self.ml = scratch
+        self.indices = indices
+        for k, g in enumerate(indices):
+            prepare(source.at[:, g], g % 4 == 1, self.mh.at[k], self.ml.at[k])
+
+    def __getitem__(self, g):
+        k = self.indices.index(g)
+        return self.mh[k], self.ml[k]
+
+
+def first_kernel(indices, me_ref, amps, gates, q1, q2, own3, own0, give, s, own, sems, mh, ml, x, xsems):
     g = Gates(gates, (own, sems, mh, ml), indices)
     parts = []
     for b in range(2):
@@ -194,25 +206,23 @@
     upper_gate(s, g[3], keeper(s))
     low_gate(s, g[4])
     middle_gate(s, g[5])
-    for core, out in ((0, keep), (1, send)):
-        ats = [rows_of(reversed3(low3 ^ (2 * p + core)), 64) for p in range(4)]
+    outs = ((own0, give.at[0]), split(q1), split(q2), (own3, give.at[1]))
+    for e in range(2):
+        ats = [rows_of(reversed3(low3 ^ (2 * p + e)), 64) for p in range(4)]
         y = right_gate(*[jnp.concatenate([s[c, at, :] for at in ats], 0) for c in range(2)], g[8])
         for p in range(4):
             for c in range(2):
-                out[p, c] = y[c][64 * p : 64 * p + 64]
-
-
-def second_kernel(indices, me_ref, keep0, recv0, r1, r2, r3, gates, own6, give, y1, self0, s, own, sems, mh, ml):
-    g = Gates(gates, (own, sems, mh, ml), indices)
-    g.start(range(3))
+                outs[p][e][c] = y[c][64 * p : 64 * p + 64]
+
+
+def second_kernel(indices, me_ref, own0, other0, r1, r2, r3, post1, post2, gates, own6, give, y1, self0, s, mh, ml):
+    g = Ready(gates, (mh, ml), indices)
     me = me_ref[0]
     low3, core = me & 7, me & 1
-    for p, part in enumerate(((keep0, recv0), split(r1), split(r2), split(r3))):
-        for e in range(2):
-            at = rows_of(reversed3(low3 ^ (2 * p + e)), 64)
-            for c in range(2):
-                s[c, at, :] = part[e][c]
-    g.ready(range(3))
+    for mask, part in enumerate((own0, other0, r1.at[0], post1, r2.at[0], post2, r3.at[0], r3.at[1])):
+        at = rows_of(reversed3(low3 ^ mask), 64)
+        for c in range(2):
+            s[c, at, :] = part[c]
     high_gate(s, g[6])
     upper_gate(s, g[7], keeper(s))
     middle_gate(s, g[9])
@@ -233,9 +243,8 @@
     write(self0, 0, 0)
 
 
-def third_kernel(indices, me_ref, a0, a1, a2, y1, other, early, late, self0, gates, out, s, own, sems, mh, ml, y, ysems):
-    g = Gates(gates, (own, sems, mh, ml), indices)
-    g.start(range(2))
+def third_kernel(indices, me_ref, a0, a1, a2, y1, other, early, late, self0, gates, out, s, mh, ml, y, ysems):
+    g = Ready(gates, (mh, ml), indices)
     me = me_ref[0]
     core = me & 1
 
@@ -254,7 +263,6 @@
     place(early, 8, 3, (1,))
     place(other, 0, 1)
     place(self0, 0, 0)
-    g.ready(range(2))
     high_gate(s, g[10])
     copies = []
 
@@ -276,6 +284,7 @@
 
 def call(kernel, indices, outs, rows, operands, specs, scratch=(), out_specs=None, limit=32 << 20):
     n = len(indices)
+    fetch = [pltpu.VMEM((n, 2, LANES, LANES), F32), pltpu.SemaphoreType.DMA((n,))] if specs[-1] is HBM else []
     return pl.pallas_call(
         functools.partial(kernel, indices),
         out_shape=outs,
@@ -283,8 +292,7 @@
         out_specs=out_specs or [VMEM] * len(outs),
         scratch_shapes=[
             pltpu.VMEM((2, rows, LANES), F32),
-            pltpu.VMEM((n, 2, LANES, LANES), F32),
-            pltpu.SemaphoreType.DMA((n,)),
+            *fetch,
             pltpu.VMEM((n, PAIR, PAIR), BF16),
             pltpu.VMEM((n, PAIR, PAIR), BF16),
             *scratch,
@@ -306,20 +314,29 @@
     me = lax.axis_index("node").astype(jnp.int32).reshape(1)
     x = amplitudes.reshape(2, rows, LANES).transpose(1, 0, 2).reshape(2 * rows, LANES)
     interleaved = (pltpu.VMEM((2 * rows, LANES), F32), pltpu.SemaphoreType.DMA((2,)))
-    half = shape(4, 2, eighth, LANES)
-    keep, send = call(
-        first_kernel, (0, 1, 2, 3, 4, 5, 8), [half] * 2, rows, [me, x, gates], [HBM] * 2, interleaved, limit=532 * 104858
+    one, two = shape(2, eighth, LANES), shape(2, 2, eighth, LANES)
+    q1, q2, own3, own0, give = call(
+        first_kernel,
+        (0, 1, 2, 3, 4, 5, 8),
+        [two, two, one, one, two],
+        rows,
+        [me, x, gates],
+        [HBM] * 2,
+        interleaved,
+        limit=532 * 104858,
     )
-    recv = flipped(send, 1)
-    far = [flipped(jnp.stack([keep[p], recv[p]]), 2 * p) for p in (1, 2, 3)]
+    recv = flipped(give, 1)
+    r1, r2 = flipped(q1, 2), flipped(q2, 4)
+    r3 = flipped(jnp.stack([own3, recv[1]]), 6)
+    post1, post2 = flipped(r1[1], 1), flipped(r2[1], 1)
     block = (part16, LANES)
     own, give, y1, self0 = call(
         second_kernel,
         (6, 7, 9),
         [shape(3, 2, 2, *block), shape(15, *block), shape(3, *block), shape(2, *block)],
         rows,
-        [me, keep[0], recv[0], *far, gates],
-        [VMEM] * 5 + [HBM],
+        [me, own0, recv[0], r1, r2, r3, post1, post2, gates],
+        [VMEM] * 8,
     )
     recv = flipped(give, 1)
     arrived = [
@@ -336,7 +353,7 @@
         [shape(2 * rows, LANES)],
         rows,
         [me, *arrived, y1, recv[13:], early, late, self0, gates],
-        [VMEM] * 8 + [HBM],
+        [VMEM] * 9,
         interleaved,
         [HBM],
     )[0]

time: 39.6 us -> 37.8 us (0.955)
  waiting for transfers between devices: 18.6 us -> 14.4 us
  starting transfers between devices: 11.4 us -> 14.3 us
  Pallas kernels: 9.17 us -> 8.72 us
    ppermute x11 -> x13, waiting for transfers between devices: 18.6 us -> 14.4 us  [flipped(): return lax.ppermute(block, 'node', route)]
    ppermute x11 -> x13, starting transfers between devices: 11.4 us -> 14.3 us  [flipped(): return lax.ppermute(block, 'node', route)]
    pallas_call x3, Pallas kernels: 9.17 us -> 8.72 us  [call(): pl.pallas_call(functools.partial(kernel, indices), out_shape=outs, in_spe...]
  transfers between devices with their start and end apart: 11 -> 13, of which waited for: 8 -> 7; matrix products, arithmetic and copies ran while one was open for 0% -> 0% of each run, Pallas kernels for 0% -> 0%
where the time goes in v1:
time: 37.8 us; the launch traced here: 37.7 us
  waiting for transfers between devices  14.4 us (38%)
  starting transfers between devices  14.3 us (38%)
  Pallas kernels  8.72 us (23%)
    ppermute x13, waiting for transfers between devices, flipped(): return lax.ppermute(block, 'node', route)  14.4 us
    ppermute x13, starting transfers between devices, flipped(): return lax.ppermute(block, 'node', route)  14.3 us
    pallas_call x3, Pallas kernels, call(): pl.pallas_call(functools.partial(kernel, indices), out_shape=outs, in_spe...  8.72 us
  transfers between devices with their start and end apart: 13, of which 7 were waited for; matrix products, arithmetic and copies ran while one was open for 0% of the time, Pallas kernels for 0%

profile of v1, /device:TPU:19, one launch (start us, length us, event | category | flops | bytes accessed | tf_op | source)
XLA Modules:
  0.0 37.7 jit_solution(14983048588367124251)
XLA Ops:
  0.0 0.0 copy-start
  0.0 5.4 %first_kernel.1 = (f32[2,2,64,128]{3,2,1,0:T(8,128)S(1)}, f32[2,2,64,128]{3,2,1,0:T(8,128)S(1)}, f32[2,64,128]{2,1,0:T(8,128)S(1)}, f32[2,64,128]{2,1,0:T(8,128)S(1)}, f32[2,2,64,128]{3,2,1,0:T(8,128)S(1)}) custom-call(s32[1]{0:T(128)} %bitcast.me_ref, f32[1024,128]{1,0:T(8,128)} %bitcast.37, f32[2,12,128,128]{3,2,1,0:T(8,128)} %gates.5), custom_call_target="tpu_custom_call" | custom-call | tf_op jit(solution)/shard_map/first_kernel/pallas_call | solution.py:288
  5.4 0.7 %collective-permute-start = (f32[2,2,64,128]{3,2,1,0:T(8,128)S(1)}, f32[2,2,64,128]{3,2,1,0:T(8,128)S(1)}, u32[]{:S(2)}, u32[]{:S(2)}) collective-permute-start(f32[2,2,64,128]{3,2,1,0:T(8,128)S(1)} %get-tuple-element.15), channel_id=1, source_target_pairs={{0,1},{1,0},{2,3},{3,2},{4,5},{5,4},{6,7},{7,6},{8,9},{9,8},{10,11... | collective-permute-start | bytes 393224 | tf_op jit(solution)/shard_map/ppermute | solution.py:307
  6.2 1.3 %collective-permute-start.1 = (f32[2,2,64,128]{3,2,1,0:T(8,128)S(1)}, f32[2,2,64,128]{3,2,1,0:T(8,128)S(1)}, u32[]{:S(2)}, u32[]{:S(2)}) collective-permute-start(f32[2,2,64,128]{3,2,1,0:T(8,128)S(1)} %get-tuple-element.16), channel_id=1, source_target_pairs={{0,2},{1,3},{2,0},{3,1},{4,6},{5,7},{6,4},{7,5},{8,10},{9,11},{10,... | collective-permute-start | bytes 393224 | tf_op jit(solution)/shard_map/ppermute | solution.py:307
  7.4 1.3 %collective-permute-start.2 = (f32[2,2,64,128]{3,2,1,0:T(8,128)S(1)}, f32[2,2,64,128]{3,2,1,0:T(8,128)S(1)}, u32[]{:S(2)}, u32[]{:S(2)}) collective-permute-start(f32[2,2,64,128]{3,2,1,0:T(8,128)S(1)} %get-tuple-element.17), channel_id=1, source_target_pairs={{0,4},{1,5},{2,6},{3,7},{4,0},{5,1},{6,2},{7,3},{8,12},{9,13},{10,... | collective-permute-start | bytes 393224 | tf_op jit(solution)/shard_map/ppermute | solution.py:307
  8.7 0.0 collective-permute-done
  8.8 0.7 %collective-permute-start.3 = (f32[2,2,64,128]{3,2,1,0:T(8,128)S(1)}, f32[2,2,64,128]{3,2,1,0:T(8,128)S(1)}, u32[]{:S(2)}, u32[]{:S(2)}) collective-permute-start(f32[2,2,64,128]{3,2,1,0:T(8,128)S(1)} %pad_maximum_fusion.1), channel_id=1, source_target_pairs={{0,6},{1,7},{2,4},{3,5},{4,2},{5,3},{6,0},{7,1},{8,14},{9,15},{10,... | collective-permute-start | bytes 393224 | tf_op jit(solution)/shard_map/ppermute | solution.py:307
  9.5 1.7 %collective-permute-done.1.r1 = f32[2,2,64,128]{3,2,1,0:T(8,128)S(1)} collective-permute-done((f32[2,2,64,128]{3,2,1,0:T(8,128)S(1)}, f32[2,2,64,128]{3,2,1,0:T(8,128)S(1)}, u32[]{:S(2)}, u32[]{:S(2)}) %collective-permute-start.1) | collective-permute-done | bytes 131104 | tf_op jit(solution)/shard_map/ppermute | solution.py:307
  11.3 0.8 %collective-permute-start.4 = (f32[2,64,128]{2,1,0:T(8,128)S(1)}, f32[2,64,128]{2,1,0:T(8,128)S(1)}, u32[]{:S(2)}, u32[]{:S(2)}) collective-permute-start(f32[2,64,128]{2,1,0:T(8,128)S(1)} %slice_bitcast_fusion.1), channel_id=1, source_target_pairs={{0,1},{1,0},{2,3},{3,2},{4,5},{5,4},{6,7},{7,6},{8,9},{9,8},{10,11... | collective-permute-start | bytes 196616 | tf_op jit(solution)/shard_map/ppermute | solution.py:307
  12.1 0.1 collective-permute-done.2.r2
  12.2 1.9 %collective-permute-start.5 = (f32[2,64,128]{2,1,0:T(8,128)S(1)}, f32[2,64,128]{2,1,0:T(8,128)S(1)}, u32[]{:S(2)}, u32[]{:S(2)}) collective-permute-start(f32[2,64,128]{2,1,0:T(8,128)S(1)} %slice_bitcast_fusion), channel_id=1, source_target_pairs={{0,1},{1,0},{2,3},{3,2},{4,5},{5,4},{6,7},{7,6},{8,9},{9,8},{10,11... | collective-permute-start | bytes 196616 | tf_op jit(solution)/shard_map/ppermute | solution.py:307
  14.1 0.0 collective-permute-done.4.post1
  14.1 0.9 %collective-permute-done.5.post2 = f32[2,64,128]{2,1,0:T(8,128)S(1)} collective-permute-done((f32[2,64,128]{2,1,0:T(8,128)S(1)}, f32[2,64,128]{2,1,0:T(8,128)S(1)}, u32[]{:S(2)}, u32[]{:S(2)}) %collective-permute-start.5) | collective-permute-done | bytes 65568 | tf_op jit(solution)/shard_map/ppermute | solution.py:307
  15.0 0.0 collective-permute-done.3.r3
  15.0 0.0 copy-done
  15.0 1.7 %second_kernel.1 = (f32[3,2,2,32,128]{4,3,2,1,0:T(8,128)S(1)}, f32[15,32,128]{2,1,0:T(8,128)S(1)}, f32[3,32,128]{2,1,0:T(8,128)S(1)}, f32[2,32,128]{2,1,0:T(8,128)S(1)}) custom-call(s32[1]{0:T(128)} %bitcast.me_ref, f32[2,64,128]{2,1,0:T(8,128)S(1)} %get-tuple-element.14.own0, f32[2,64,128]{2,1,0:T(8,128)S(1)} %get-tuple-element.30.other0, ...), custom_call_target="tpu_custom_call" | custom-call | tf_op jit(solution)/shard_map/second_kernel/pallas_call | solution.py:288
  16.7 1.1 %collective-permute-start.6 = (f32[15,32,128]{2,1,0:T(8,128)S(1)}, f32[15,32,128]{2,1,0:T(8,128)S(1)}, u32[]{:S(2)}, u32[]{:S(2)}) collective-permute-start(f32[15,32,128]{2,1,0:T(8,128)S(1)} %get-tuple-element.20), channel_id=1, source_target_pairs={{0,1},{1,0},{2,3},{3,2},{4,5},{5,4},{6,7},{7,6},{8,9},{9,8},{10,11... | collective-permute-start | bytes 737288 | tf_op jit(solution)/shard_map/ppermute | solution.py:307
  17.9 1.1 %collective-permute-done.6 = f32[15,32,128]{2,1,0:T(8,128)S(1)} collective-permute-done((f32[15,32,128]{2,1,0:T(8,128)S(1)}, f32[15,32,128]{2,1,0:T(8,128)S(1)}, u32[]{:S(2)}, u32[]{:S(2)}) %collective-permute-start.6) | collective-permute-done | bytes 245792 | tf_op jit(solution)/shard_map/ppermute | solution.py:307
  19.0 1.1 %collective-permute-start.7 = (f32[2,2,2,32,128]{4,3,2,1,0:T(8,128)S(1)}, f32[2,2,2,32,128]{4,3,2,1,0:T(8,128)S(1)}, u32[]{:S(2)}, u32[]{:S(2)}) collective-permute-start(f32[2,2,2,32,128]{4,3,2,1,0:T(8,128)S(1)} %pad_maximum_fusion.2), channel_id=1, source_target_pairs={{0,8},{1,11},{2,10},{3,9},{4,12},{5,15},{6,14},{7,13},{8,0},{9,3},... | collective-permute-start | bytes 393224 | tf_op jit(solution)/shard_map/ppermute | solution.py:307
  20.1 1.3 %collective-permute-start.8 = (f32[2,2,2,32,128]{4,3,2,1,0:T(8,128)S(1)}, f32[2,2,2,32,128]{4,3,2,1,0:T(8,128)S(1)}, u32[]{:S(2)}, u32[]{:S(2)}) collective-permute-start(f32[2,2,2,32,128]{4,3,2,1,0:T(8,128)S(1)} %pad_maximum_fusion.3), channel_id=1, source_target_pairs={{0,4},{1,7},{2,6},{3,5},{4,0},{5,3},{6,2},{7,1},{8,12},{9,15},{10,... | collective-permute-start | bytes 393224 | tf_op jit(solution)/shard_map/ppermute | solution.py:307
  21.5 1.3 %collective-permute-start.10 = (f32[4,32,128]{2,1,0:T(8,128)S(1)}, f32[4,32,128]{2,1,0:T(8,128)S(1)}, u32[]{:S(2)}, u32[]{:S(2)}) collective-permute-start(f32[4,32,128]{2,1,0:T(8,128)S(1)} %pad_maximum_fusion.5), channel_id=1, source_target_pairs={{0,2},{1,3},{2,0},{3,1},{4,6},{5,7},{6,4},{7,5},{8,10},{9,11},{10,... | collective-permute-start | bytes 196616 | tf_op jit(solution)/shard_map/ppermute | solution.py:307
  22.7 1.3 %collective-permute-start.9 = (f32[2,2,2,32,128]{4,3,2,1,0:T(8,128)S(1)}, f32[2,2,2,32,128]{4,3,2,1,0:T(8,128)S(1)}, u32[]{:S(2)}, u32[]{:S(2)}) collective-permute-start(f32[2,2,2,32,128]{4,3,2,1,0:T(8,128)S(1)} %pad_maximum_fusion.4), channel_id=1, source_target_pairs={{0,12},{1,15},{2,14},{3,13},{4,8},{5,11},{6,10},{7,9},{8,4},{9,7},... | collective-permute-start | bytes 393224 | tf_op jit(solution)/shard_map/ppermute | solution.py:307
  24.0 3.7 %collective-permute-done.10.y1 = f32[4,32,128]{2,1,0:T(8,128)S(1)} collective-permute-done((f32[4,32,128]{2,1,0:T(8,128)S(1)}, f32[4,32,128]{2,1,0:T(8,128)S(1)}, u32[]{:S(2)}, u32[]{:S(2)}) %collective-permute-start.10) | collective-permute-done | bytes 65568 | tf_op jit(solution)/shard_map/ppermute | solution.py:307
  27.8 0.0 collective-permute-done.7.a0
  27.8 0.0 collective-permute-done.8.a1
  27.8 0.7 %collective-permute-start.11 = (f32[9,32,128]{2,1,0:T(8,128)S(1)}, f32[9,32,128]{2,1,0:T(8,128)S(1)}, u32[]{:S(2)}, u32[]{:S(2)}) collective-permute-start(f32[9,32,128]{2,1,0:T(8,128)S(1)} %pad_maximum_fusion), channel_id=1, source_target_pairs={{0,1},{1,0},{2,3},{3,2},{4,5},{5,4},{6,7},{7,6},{8,9},{9,8},{10,11... | collective-permute-start | bytes 442376 | tf_op jit(solution)/shard_map/ppermute | solution.py:307
  28.5 6.0 %collective-permute-done.9.a2 = f32[2,2,2,32,128]{4,3,2,1,0:T(8,128)S(1)} collective-permute-done((f32[2,2,2,32,128]{4,3,2,1,0:T(8,128)S(1)}, f32[2,2,2,32,128]{4,3,2,1,0:T(8,128)S(1)}, u32[]{:S(2)}, u32[]{:S(2)}) %collective-permute-start.9) | collective-permute-done | bytes 131104 | tf_op jit(solution)/shard_map/ppermute | solution.py:307
  34.5 0.7 %collective-permute-start.12 = (f32[4,32,128]{2,1,0:T(8,128)S(1)}, f32[4,32,128]{2,1,0:T(8,128)S(1)}, u32[]{:S(2)}, u32[]{:S(2)}) collective-permute-start(f32[4,32,128]{2,1,0:T(8,128)S(1)} %bitcast.43), channel_id=1, source_target_pairs={{0,1},{1,0},{2,3},{3,2},{4,5},{5,4},{6,7},{7,6},{8,9},{9,8},{10,11... | collective-permute-start | bytes 196616 | tf_op jit(solution)/shard_map/ppermute | solution.py:307
  35.2 0.9 %collective-permute-done.12.late = f32[4,32,128]{2,1,0:T(8,128)S(1)} collective-permute-done((f32[4,32,128]{2,1,0:T(8,128)S(1)}, f32[4,32,128]{2,1,0:T(8,128)S(1)}, u32[]{:S(2)}, u32[]{:S(2)}) %collective-permute-start.12) | collective-permute-done | bytes 65568 | tf_op jit(solution)/shard_map/ppermute | solution.py:307
  36.1 0.0 collective-permute-done.11.early
  36.1 1.6 %third_kernel.1 = f32[1024,128]{1,0:T(8,128)} custom-call(s32[1]{0:T(128)} %bitcast.me_ref, f32[2,2,2,32,128]{4,3,2,1,0:T(8,128)S(1)} %collective-permute-done.7.a0, f32[2,2,2,32,128]{4,3,2,1,0:T(8,128)S(1)} %collective-permute-done.8.a1, f32[2,2,2,32,128]{4,3,2,1,0:T(8,128)S(1)} %collective-permute-done.9.a2, f32[4,32,128]{2,1,0:T(8,128)S(1)} %collective-permute-done.10.y1, ...), custom_call_target="tpu_custom_call" | custom-call | tf_op jit(solution)/shard_map/third_kernel/pallas_call | solution.py:288
  (17 shorter events, 0.1 us)
Async XLA Ops:
  0.0 15.0 %copy-start = (f32[2,12,128,128]{3,2,1,0:T(8,128)S(1)}, f32[2,12,128,128]{3,2,1,0:T(8,128)}, u32[]{:S(2)}) copy-start(f32[2,12,128,128]{3,2,1,0:T(8,128)} %gates.5) | copy-start | bytes 4718596
  5.4 3.3 %collective-permute-start = (f32[2,2,64,128]{3,2,1,0:T(8,128)S(1)}, f32[2,2,64,128]{3,2,1,0:T(8,128)S(1)}, u32[]{:S(2)}, u32[]{:S(2)}) collective-permute-start(f32[2,2,64,128]{3,2,1,0:T(8,128)S(1)} %get-tuple-element.15), channel_id=1, source_target_pairs={{0,1},{1,0},{2,3},{3,2},{4,5},{5,4},{6,7},{7,6},{8,9},{9,8},{10,11... | collective-permute-start | bytes 393224 | tf_op jit(solution)/shard_map/ppermute | solution.py:307
  6.2 5.1 %collective-permute-start.1 = (f32[2,2,64,128]{3,2,1,0:T(8,128)S(1)}, f32[2,2,64,128]{3,2,1,0:T(8,128)S(1)}, u32[]{:S(2)}, u32[]{:S(2)}) collective-permute-start(f32[2,2,64,128]{3,2,1,0:T(8,128)S(1)} %get-tuple-element.16), channel_id=1, source_target_pairs={{0,2},{1,3},{2,0},{3,1},{4,6},{5,7},{6,4},{7,5},{8,10},{9,11},{10,... | collective-permute-start | bytes 393224 | tf_op jit(solution)/shard_map/ppermute | solution.py:307
  7.4 4.7 %collective-permute-start.2 = (f32[2,2,64,128]{3,2,1,0:T(8,128)S(1)}, f32[2,2,64,128]{3,2,1,0:T(8,128)S(1)}, u32[]{:S(2)}, u32[]{:S(2)}) collective-permute-start(f32[2,2,64,128]{3,2,1,0:T(8,128)S(1)} %get-tuple-element.17), channel_id=1, source_target_pairs={{0,4},{1,5},{2,6},{3,7},{4,0},{5,1},{6,2},{7,3},{8,12},{9,13},{10,... | collective-permute-start | bytes 393224 | tf_op jit(solution)/shard_map/ppermute | solution.py:307
  8.8 6.3 %collective-permute-start.3 = (f32[2,2,64,128]{3,2,1,0:T(8,128)S(1)}, f32[2,2,64,128]{3,2,1,0:T(8,128)S(1)}, u32[]{:S(2)}, u32[]{:S(2)}) collective-permute-start(f32[2,2,64,128]{3,2,1,0:T(8,128)S(1)} %pad_maximum_fusion.1), channel_id=1, source_target_pairs={{0,6},{1,7},{2,4},{3,5},{4,2},{5,3},{6,0},{7,1},{8,14},{9,15},{10,... | collective-permute-start | bytes 393224 | tf_op jit(solution)/shard_map/ppermute | solution.py:307
  11.3 2.9 %collective-permute-start.4 = (f32[2,64,128]{2,1,0:T(8,128)S(1)}, f32[2,64,128]{2,1,0:T(8,128)S(1)}, u32[]{:S(2)}, u32[]{:S(2)}) collective-permute-start(f32[2,64,128]{2,1,0:T(8,128)S(1)} %slice_bitcast_fusion.1), channel_id=1, source_target_pairs={{0,1},{1,0},{2,3},{3,2},{4,5},{5,4},{6,7},{7,6},{8,9},{9,8},{10,11... | collective-permute-start | bytes 196616 | tf_op jit(solution)/shard_map/ppermute | solution.py:307
  12.2 2.9 %collective-permute-start.5 = (f32[2,64,128]{2,1,0:T(8,128)S(1)}, f32[2,64,128]{2,1,0:T(8,128)S(1)}, u32[]{:S(2)}, u32[]{:S(2)}) collective-permute-start(f32[2,64,128]{2,1,0:T(8,128)S(1)} %slice_bitcast_fusion), channel_id=1, source_target_pairs={{0,1},{1,0},{2,3},{3,2},{4,5},{5,4},{6,7},{7,6},{8,9},{9,8},{10,11... | collective-permute-start | bytes 196616 | tf_op jit(solution)/shard_map/ppermute | solution.py:307
  16.7 2.2 %collective-permute-start.6 = (f32[15,32,128]{2,1,0:T(8,128)S(1)}, f32[15,32,128]{2,1,0:T(8,128)S(1)}, u32[]{:S(2)}, u32[]{:S(2)}) collective-permute-start(f32[15,32,128]{2,1,0:T(8,128)S(1)} %get-tuple-element.20), channel_id=1, source_target_pairs={{0,1},{1,0},{2,3},{3,2},{4,5},{5,4},{6,7},{7,6},{8,9},{9,8},{10,11... | collective-permute-start | bytes 737288 | tf_op jit(solution)/shard_map/ppermute | solution.py:307
  19.0 8.8 %collective-permute-start.7 = (f32[2,2,2,32,128]{4,3,2,1,0:T(8,128)S(1)}, f32[2,2,2,32,128]{4,3,2,1,0:T(8,128)S(1)}, u32[]{:S(2)}, u32[]{:S(2)}) collective-permute-start(f32[2,2,2,32,128]{4,3,2,1,0:T(8,128)S(1)} %pad_maximum_fusion.2), channel_id=1, source_target_pairs={{0,8},{1,11},{2,10},{3,9},{4,12},{5,15},{6,14},{7,13},{8,0},{9,3},... | collective-permute-start | bytes 393224 | tf_op jit(solution)/shard_map/ppermute | solution.py:307
  20.1 7.7 %collective-permute-start.8 = (f32[2,2,2,32,128]{4,3,2,1,0:T(8,128)S(1)}, f32[2,2,2,32,128]{4,3,2,1,0:T(8,128)S(1)}, u32[]{:S(2)}, u32[]{:S(2)}) collective-permute-start(f32[2,2,2,32,128]{4,3,2,1,0:T(8,128)S(1)} %pad_maximum_fusion.3), channel_id=1, source_target_pairs={{0,4},{1,7},{2,6},{3,5},{4,0},{5,3},{6,2},{7,1},{8,12},{9,15},{10,... | collective-permute-start | bytes 393224 | tf_op jit(solution)/shard_map/ppermute | solution.py:307
  21.5 6.3 %collective-permute-start.10 = (f32[4,32,128]{2,1,0:T(8,128)S(1)}, f32[4,32,128]{2,1,0:T(8,128)S(1)}, u32[]{:S(2)}, u32[]{:S(2)}) collective-permute-start(f32[4,32,128]{2,1,0:T(8,128)S(1)} %pad_maximum_fusion.5), channel_id=1, source_target_pairs={{0,2},{1,3},{2,0},{3,1},{4,6},{5,7},{6,4},{7,5},{8,10},{9,11},{10,... | collective-permute-start | bytes 196616 | tf_op jit(solution)/shard_map/ppermute | solution.py:307
  22.7 11.7 %collective-permute-start.9 = (f32[2,2,2,32,128]{4,3,2,1,0:T(8,128)S(1)}, f32[2,2,2,32,128]{4,3,2,1,0:T(8,128)S(1)}, u32[]{:S(2)}, u32[]{:S(2)}) collective-permute-start(f32[2,2,2,32,128]{4,3,2,1,0:T(8,128)S(1)} %pad_maximum_fusion.4), channel_id=1, source_target_pairs={{0,12},{1,15},{2,14},{3,13},{4,8},{5,11},{6,10},{7,9},{8,4},{9,7},... | collective-permute-start | bytes 393224 | tf_op jit(solution)/shard_map/ppermute | solution.py:307
  27.8 8.2 %collective-permute-start.11 = (f32[9,32,128]{2,1,0:T(8,128)S(1)}, f32[9,32,128]{2,1,0:T(8,128)S(1)}, u32[]{:S(2)}, u32[]{:S(2)}) collective-permute-start(f32[9,32,128]{2,1,0:T(8,128)S(1)} %pad_maximum_fusion), channel_id=1, source_target_pairs={{0,1},{1,0},{2,3},{3,2},{4,5},{5,4},{6,7},{7,6},{8,9},{9,8},{10,11... | collective-permute-start | bytes 442376 | tf_op jit(solution)/shard_map/ppermute | solution.py:307
  34.5 1.6 %collective-permute-start.12 = (f32[4,32,128]{2,1,0:T(8,128)S(1)}, f32[4,32,128]{2,1,0:T(8,128)S(1)}, u32[]{:S(2)}, u32[]{:S(2)}) collective-permute-start(f32[4,32,128]{2,1,0:T(8,128)S(1)} %bitcast.43), channel_id=1, source_target_pairs={{0,1},{1,0},{2,3},{3,2},{4,5},{5,4},{6,7},{7,6},{8,9},{9,8},{10,11... | collective-permute-start | bytes 196616 | tf_op jit(solution)/shard_map/ppermute | solution.py:307

commit v2 on v1

--- a/solution.py
+++ b/solution.py
@@ -13,6 +13,7 @@
 NT = (((1,), (1,)), ((), ()))
 NN = (((1,), (0,)), ((), ()))
 PORTS = (4, 2, 6)
+SMEM = pl.BlockSpec(memory_space=pltpu.SMEM)
 VMEM = pl.BlockSpec(memory_space=pltpu.VMEM)
 ANY = pl.BlockSpec(memory_space=pl.ANY)
 HBM = pl.BlockSpec(memory_space=pltpu.HBM)
@@ -183,15 +184,21 @@
         return self.mh[k], self.ml[k]
 
 
-def first_kernel(indices, me_ref, amps, gates, q1, q2, own3, own0, give, s, own, sems, mh, ml, x, xsems):
+def lower_gates(s, g):
+    low_gate(s, g[4])
+    middle_gate(s, g[5])
+    low_gate(s, g[8])
+
+
+def first_kernel(indices, me_ref, amps, gates, q1, q2, own3, own0, give, s, own, sems, mh, ml, x, xsems, part):
     g = Gates(gates, (own, sems, mh, ml), indices)
     parts = []
     for b in range(2):
         at = pl.ds(2 * PAIR * b, 2 * PAIR)
         parts.append(pltpu.make_async_copy(amps.at[at], x.at[at], xsems.at[b]))
     g.start([0])
-    for part in parts:
-        part.start()
+    for copy in parts:
+        copy.start()
     g.start(range(1, len(indices)))
     low3 = me_ref[0] & 7
     g.ready([0])
@@ -204,65 +211,97 @@
     middle_gate(s, g[1])
     high_gate(s, g[2])
     upper_gate(s, g[3], keeper(s))
-    low_gate(s, g[4])
-    middle_gate(s, g[5])
-    outs = ((own0, give.at[0]), split(q1), split(q2), (own3, give.at[1]))
-    for e in range(2):
-        ats = [rows_of(reversed3(low3 ^ (2 * p + e)), 64) for p in range(4)]
-        y = right_gate(*[jnp.concatenate([s[c, at, :] for at in ats], 0) for c in range(2)], g[8])
-        for p in range(4):
-            for c in range(2):
-                outs[p][e][c] = y[c][64 * p : 64 * p + 64]
-
-
-def second_kernel(indices, me_ref, own0, other0, r1, r2, r3, post1, post2, gates, own6, give, y1, self0, s, mh, ml):
+    sent = [(4, q2.at[0]), (5, q2.at[1]), (6, own3), (7, give.at[1])]
+    for n, (mask, _) in enumerate(sent):
+        at = rows_of(reversed3(low3 ^ mask), 64)
+        for c in range(2):
+            part[c, pl.ds(64 * n, 64), :] = s[c, at, :]
+    for mask, out in ((0, own0), (1, give.at[0]), (2, q1.at[0]), (3, q1.at[1])):
+        at = rows_of(reversed3(low3 ^ mask), 64)
+        for c in range(2):
+            out[c] = s[c, at, :]
+    lower_gates(part, g)
+    for n, (_, out) in enumerate(sent):
+        for c in range(2):
+            out[c] = part[c, pl.ds(64 * n, 64), :]
+
+
+def near_kernel(indices, own0, other0, r1, gates, keep, send, s, mh, ml):
+    g = Ready(gates, (mh, ml), indices)
+    for n, block in enumerate((own0, other0, r1.at[0], r1.at[1])):
+        for c in range(2):
+            s[c, pl.ds(64 * n, 64), :] = block[c]
+    lower_gates(s, g)
+    for n, out in enumerate((keep.at[0], keep.at[1], keep.at[2], send)):
+        for c in range(2):
+            out[c] = s[c, pl.ds(64 * n, 64), :]
+
+
+def second_kernel(indices, me_ref, near, r2, r3, post1, post2, gates, own, give, y1, self0, s, mh, ml):
     g = Ready(gates, (mh, ml), indices)
     me = me_ref[0]
     low3, core = me & 7, me & 1
-    for mask, part in enumerate((own0, other0, r1.at[0], post1, r2.at[0], post2, r3.at[0], r3.at[1])):
+    blocks = (near.at[0], near.at[1], near.at[2], post1, r2.at[0], post2, r3.at[0], r3.at[1])
+    for mask, block in enumerate(blocks):
         at = rows_of(reversed3(low3 ^ mask), 64)
         for c in range(2):
-            s[c, at, :] = part[c]
+            s[c, at, :] = block[c]
     high_gate(s, g[6])
     upper_gate(s, g[7], keeper(s))
-    middle_gate(s, g[9])
-
-    def write(out, first, mask, parts=(0, 1)):
+
+    def write(out, mask):
         at = rows_of(me ^ mask, 32)
-        for n, c in enumerate(parts):
-            out[first + n] = s[c, at, :]
+        for c in range(2):
+            out[c] = s[c, at, :]
 
     for i, base in enumerate(PORTS):
         for f in range(2):
-            write(own6.at[i, f], 0, 2 * (base + core) + f)
-            write(give, 4 * i + 2 * f, 2 * (base + 1 - core) + (1 - f))
-    write(give, 12, 3, (0,))
-    write(give, 13, 1)
-    write(y1, 0, 2)
-    write(y1, 2, 3, (1,))
-    write(self0, 0, 0)
-
-
-def third_kernel(indices, me_ref, a0, a1, a2, y1, other, early, late, self0, gates, out, s, mh, ml, y, ysems):
+            write(own.at[i, f], 2 * (base + core) + f)
+            write(give.at[2 * i + f], 2 * (base + 1 - core) + (1 - f))
+    write(give.at[6], 3)
+    write(give.at[7], 1)
+    write(y1, 2)
+    write(self0, 0)
+
+
+def gate_nine(s, g, blocks, outs):
+    for n, block in enumerate(blocks):
+        for c in range(2):
+            s[c, pl.ds(32 * n, 32), :] = block[c]
+    middle_gate(s, g[9])
+    for n, out in enumerate(outs):
+        for c in range(2):
+            out[c] = s[c, pl.ds(32 * n, 32), :]
+
+
+def before_kernel(indices, own, recv, gates, out, s, mh, ml):
+    g = Ready(gates, (mh, ml), indices)
+    gate_nine(s, g, (*split(own), *split(recv)), [out.at[f, src] for src in range(2) for f in range(2)])
+
+
+def after_kernel(indices, a0, a1, y1, self0, other, gates, keep, send, s, mh, ml):
+    g = Ready(gates, (mh, ml), indices)
+    blocks = [a.at[f, src] for f in range(2) for a in (a0, a1) for src in range(2)]
+    blocks = blocks[:4] + [y1.at[0], y1.at[1], self0, other] + blocks[4:]
+    gate_nine(s, g, blocks, [keep.at[n] for n in range(8)] + [send.at[n] for n in range(4)])
+
+
+def third_kernel(indices, me_ref, keep, early, a2, late, gates, out, s, mh, ml, y, ysems):
     g = Ready(gates, (mh, ml), indices)
     me = me_ref[0]
     core = me & 1
 
-    def place(part, first, mask, parts=(0, 1)):
+    def place(block, mask):
         at = rows_of(me ^ mask, 32)
-        for n, c in enumerate(parts):
-            s[c, at, :] = part[first + n]
-
-    for i, (base, arrived) in enumerate(zip(PORTS, (a0, a1, a2))):
+        for c in range(2):
+            s[c, at, :] = block[c]
+
+    for i, base in enumerate(PORTS):
         for src in range(2):
-            place(arrived.at[0, src], 0, 2 * (base + core) + src)
-            post, first = (early, 4 * i) if i < 2 else (late, 0)
-            place(post, first + 2 * src, 2 * (base + 1 - core) + (1 - src))
-    place(y1, 0, 2)
-    place(y1, 3, 3, (0,))
-    place(early, 8, 3, (1,))
-    place(other, 0, 1)
-    place(self0, 0, 0)
+            place(keep.at[2 * i + src] if i < 2 else a2.at[0, src], 2 * (base + core) + src)
+            place(early.at[2 * i + src] if i < 2 else late.at[src], 2 * (base + 1 - core) + (1 - src))
+    for n, mask in ((4, 2), (5, 3), (6, 0), (7, 1)):
+        place(keep.at[n], mask)
     high_gate(s, g[10])
     copies = []
 
@@ -288,7 +327,7 @@
     return pl.pallas_call(
         functools.partial(kernel, indices),
         out_shape=outs,
-        in_specs=[pl.BlockSpec(memory_space=pltpu.SMEM)] + specs,
+        in_specs=specs,
         out_specs=out_specs or [VMEM] * len(outs),
         scratch_shapes=[
             pltpu.VMEM((2, rows, LANES), F32),
@@ -321,39 +360,54 @@
         [two, two, one, one, two],
         rows,
         [me, x, gates],
-        [HBM] * 2,
-        interleaved,
+        [SMEM, HBM, HBM],
+        (*interleaved, pltpu.VMEM((2, 4 * eighth, LANES), F32)),
         limit=532 * 104858,
     )
     recv = flipped(give, 1)
     r1, r2 = flipped(q1, 2), flipped(q2, 4)
     r3 = flipped(jnp.stack([own3, recv[1]]), 6)
-    post1, post2 = flipped(r1[1], 1), flipped(r2[1], 1)
-    block = (part16, LANES)
+    near, send = call(
+        near_kernel,
+        (4, 5, 8),
+        [shape(3, 2, eighth, LANES), one],
+        4 * eighth,
+        [own0, recv[0], r1, gates],
+        [VMEM] * 4,
+    )
+    post1, post2 = flipped(send, 1), flipped(r2[1], 1)
+    block = (2, part16, LANES)
     own, give, y1, self0 = call(
         second_kernel,
-        (6, 7, 9),
-        [shape(3, 2, 2, *block), shape(15, *block), shape(3, *block), shape(2, *block)],
+        (6, 7),
+        [shape(3, 2, *block), shape(8, *block), shape(*block), shape(*block)],
         rows,
-        [me, own0, recv[0], r1, r2, r3, post1, post2, gates],
-        [VMEM] * 8,
+        [me, near, r2, r3, post1, post2, gates],
+        [SMEM] + [VMEM] * 6,
     )
     recv = flipped(give, 1)
-    arrived = [
-        flipped(jnp.stack([own[i], recv[4 * i : 4 * i + 4].reshape(2, 2, *block)], 1), 2 * base, 2)
-        for i, base in enumerate(PORTS)
-    ]
-    y1 = flipped(jnp.concatenate([y1, recv[12:13]]), 2)
-    early = [a[1].reshape(4, *block) for a in arrived]
-    late = flipped(early[2], 1)
-    early = flipped(jnp.concatenate(early[:2] + [y1[2:3]]), 1)
+    ready = call(
+        before_kernel, (9,), [shape(2, 2, *block)], 4 * part16, [own[2], recv[4:6], gates], [VMEM] * 3
+    )[0]
+    payloads = [jnp.stack([own[i], recv[2 * i : 2 * i + 2]], 1) for i in range(2)] + [ready]
+    a0, a1, a2 = [flipped(payload, 2 * base, 2) for base, payload in zip(PORTS, payloads)]
+    y1 = flipped(jnp.stack([y1, recv[6]]), 2)
+    keep, send = call(
+        after_kernel,
+        (9,),
+        [shape(8, *block), shape(4, *block)],
+        12 * part16,
+        [a0, a1, y1, self0, recv[7], gates],
+        [VMEM] * 6,
+    )
+    early, late = flipped(send, 1), flipped(a2[1], 1)
     out = call(
         third_kernel,
         (10, 11),
         [shape(2 * rows, LANES)],
         rows,
-        [me, *arrived, y1, recv[13:], early, late, self0, gates],
-        [VMEM] * 9,
+        [me, keep, early, a2, late, gates],
+        [SMEM] + [VMEM] * 5,
         interleaved,
         [HBM],
     )[0]

time: 37.8 us -> 37 us (0.979)
  Pallas kernels: 8.72 us -> 11 us
  starting transfers between devices: 14.3 us -> 12.6 us
  waiting for transfers between devices: 14.4 us -> 13.1 us
    pallas_call x3 -> x6, Pallas kernels: 8.72 us -> 11 us  [call(): pl.pallas_call(functools.partial(kernel, indices), out_shape=outs, in_spe...]
    ppermute x13, starting transfers between devices: 14.3 us -> 12.6 us  [flipped(): return lax.ppermute(block, 'node', route)]
    ppermute x13, waiting for transfers between devices: 14.4 us -> 13.1 us  [flipped(): return lax.ppermute(block, 'node', route)]
  transfers between devices with their start and end apart: 13 -> 13, of which waited for: 7 -> 9; matrix products, arithmetic and copies ran while one was open for 0% -> 0% of each run, Pallas kernels for 0% -> 8%
where the time goes in v2:
time: 37 us; the launch traced here: 36.9 us
  waiting for transfers between devices  13.1 us (35%)
  starting transfers between devices  12.6 us (34%)
  Pallas kernels  11 us (30%)
    ppermute x13, waiting for transfers between devices, flipped(): return lax.ppermute(block, 'node', route)  13.1 us
    ppermute x13, starting transfers between devices, flipped(): return lax.ppermute(block, 'node', route)  12.6 us
    pallas_call x6, Pallas kernels, call(): pl.pallas_call(functools.partial(kernel, indices), out_shape=outs, in_spe...  11 us
  transfers between devices with their start and end apart: 13, of which 9 were waited for; matrix products, arithmetic and copies ran while one was open for 0% of the time, Pallas kernels for 8%

profile of v2, /device:TPU:19, one launch (start us, length us, event | category | flops | bytes accessed | tf_op | source)
XLA Modules:
  0.0 36.9 jit_solution(13711540922400023234)
XLA Ops:
  0.0 5.4 %first_kernel.1 = (f32[2,2,64,128]{3,2,1,0:T(8,128)S(1)}, f32[2,2,64,128]{3,2,1,0:T(8,128)S(1)}, f32[2,64,128]{2,1,0:T(8,128)S(1)}, f32[2,64,128]{2,1,0:T(8,128)S(1)}, f32[2,2,64,128]{3,2,1,0:T(8,128)S(1)}) custom-call(s32[1]{0:T(128)} %bitcast.me_ref, f32[1024,128]{1,0:T(8,128)} %bitcast.33, f32[2,12,128,128]{3,2,1,0:T(8,128)} %gates.11), custom_call_target="tpu_custom_call" | custom-call | tf_op jit(solution)/shard_map/first_kernel/pallas_call | solution.py:327
  5.4 0.7 %collective-permute-start = (f32[2,2,64,128]{3,2,1,0:T(8,128)S(1)}, f32[2,2,64,128]{3,2,1,0:T(8,128)S(1)}, u32[]{:S(2)}, u32[]{:S(2)}) collective-permute-start(f32[2,2,64,128]{3,2,1,0:T(8,128)S(1)} %get-tuple-element.19), channel_id=1, source_target_pairs={{0,1},{1,0},{2,3},{3,2},{4,5},{5,4},{6,7},{7,6},{8,9},{9,8},{10,11... | collective-permute-start | bytes 393224 | tf_op jit(solution)/shard_map/ppermute | solution.py:346
  6.2 1.3 %collective-permute-start.1 = (f32[2,2,64,128]{3,2,1,0:T(8,128)S(1)}, f32[2,2,64,128]{3,2,1,0:T(8,128)S(1)}, u32[]{:S(2)}, u32[]{:S(2)}) collective-permute-start(f32[2,2,64,128]{3,2,1,0:T(8,128)S(1)} %get-tuple-element.20), channel_id=1, source_target_pairs={{0,2},{1,3},{2,0},{3,1},{4,6},{5,7},{6,4},{7,5},{8,10},{9,11},{10,... | collective-permute-start | bytes 393224 | tf_op jit(solution)/shard_map/ppermute | solution.py:346
  7.4 1.3 %collective-permute-start.2 = (f32[2,2,64,128]{3,2,1,0:T(8,128)S(1)}, f32[2,2,64,128]{3,2,1,0:T(8,128)S(1)}, u32[]{:S(2)}, u32[]{:S(2)}) collective-permute-start(f32[2,2,64,128]{3,2,1,0:T(8,128)S(1)} %get-tuple-element.22), channel_id=1, source_target_pairs={{0,4},{1,5},{2,6},{3,7},{4,0},{5,1},{6,2},{7,3},{8,12},{9,13},{10,... | collective-permute-start | bytes 393224 | tf_op jit(solution)/shard_map/ppermute | solution.py:346
  8.7 0.0 collective-permute-done
  8.8 0.7 %collective-permute-start.3 = (f32[2,2,64,128]{3,2,1,0:T(8,128)S(1)}, f32[2,2,64,128]{3,2,1,0:T(8,128)S(1)}, u32[]{:S(2)}, u32[]{:S(2)}) collective-permute-start(f32[2,2,64,128]{3,2,1,0:T(8,128)S(1)} %pad_maximum_fusion), channel_id=1, source_target_pairs={{0,6},{1,7},{2,4},{3,5},{4,2},{5,3},{6,0},{7,1},{8,14},{9,15},{10,... | collective-permute-start | bytes 393224 | tf_op jit(solution)/shard_map/ppermute | solution.py:346
  9.5 1.7 %collective-permute-done.1.r1 = f32[2,2,64,128]{3,2,1,0:T(8,128)S(1)} collective-permute-done((f32[2,2,64,128]{3,2,1,0:T(8,128)S(1)}, f32[2,2,64,128]{3,2,1,0:T(8,128)S(1)}, u32[]{:S(2)}, u32[]{:S(2)}) %collective-permute-start.1) | collective-permute-done | bytes 131104 | tf_op jit(solution)/shard_map/ppermute | solution.py:346
  11.3 1.5 %near_kernel.1 = (f32[3,2,64,128]{3,2,1,0:T(8,128)S(1)}, f32[2,64,128]{2,1,0:T(8,128)S(1)}) custom-call(f32[2,64,128]{2,1,0:T(8,128)S(1)} %get-tuple-element.18.own0, f32[2,64,128]{2,1,0:T(8,128)S(1)} %get-tuple-element.40.other0, f32[2,2,64,128]{3,2,1,0:T(8,128)S(1)} %collective-permute-done.1.r1, f32[2,12,128,128]{3,2,1,0:T(8,128)S(1)} %copy-done), custom_call_target="tpu_custom_call" | custom-call | tf_op jit(solution)/shard_map/near_kernel/pallas_call | solution.py:327
  12.8 0.9 %collective-permute-start.4 = (f32[2,64,128]{2,1,0:T(8,128)S(1)}, f32[2,64,128]{2,1,0:T(8,128)S(1)}, u32[]{:S(2)}, u32[]{:S(2)}) collective-permute-start(f32[2,64,128]{2,1,0:T(8,128)S(1)} %get-tuple-element.24), channel_id=1, source_target_pairs={{0,1},{1,0},{2,3},{3,2},{4,5},{5,4},{6,7},{7,6},{8,9},{9,8},{10,11... | collective-permute-start | bytes 196616 | tf_op jit(solution)/shard_map/ppermute | solution.py:346
  13.7 0.0 collective-permute-done.2.r2
  13.7 0.5 %collective-permute-start.5 = (f32[2,64,128]{2,1,0:T(8,128)S(1)}, f32[2,64,128]{2,1,0:T(8,128)S(1)}, u32[]{:S(2)}, u32[]{:S(2)}) collective-permute-start(f32[2,64,128]{2,1,0:T(8,128)S(1)} %slice_bitcast_fusion.3), channel_id=1, source_target_pairs={{0,1},{1,0},{2,3},{3,2},{4,5},{5,4},{6,7},{7,6},{8,9},{9,8},{10,11... | collective-permute-start | bytes 196616 | tf_op jit(solution)/shard_map/ppermute | solution.py:346
  14.1 0.4 %collective-permute-done.4.post1 = f32[2,64,128]{2,1,0:T(8,128)S(1)} collective-permute-done((f32[2,64,128]{2,1,0:T(8,128)S(1)}, f32[2,64,128]{2,1,0:T(8,128)S(1)}, u32[]{:S(2)}, u32[]{:S(2)}) %collective-permute-start.4) | collective-permute-done | bytes 65568 | tf_op jit(solution)/shard_map/ppermute | solution.py:346
  14.6 0.5 %collective-permute-done.5.post2 = f32[2,64,128]{2,1,0:T(8,128)S(1)} collective-permute-done((f32[2,64,128]{2,1,0:T(8,128)S(1)}, f32[2,64,128]{2,1,0:T(8,128)S(1)}, u32[]{:S(2)}, u32[]{:S(2)}) %collective-permute-start.5) | collective-permute-done | bytes 65568 | tf_op jit(solution)/shard_map/ppermute | solution.py:346
  15.0 0.0 collective-permute-done.3.r3
  15.1 0.9 %second_kernel.1 = (f32[3,2,2,32,128]{4,3,2,1,0:T(8,128)S(1)}, f32[8,2,32,128]{3,2,1,0:T(8,128)S(1)}, f32[2,32,128]{2,1,0:T(8,128)S(1)}, f32[2,32,128]{2,1,0:T(8,128)S(1)}) custom-call(s32[1]{0:T(128)} %bitcast.me_ref, f32[3,2,64,128]{3,2,1,0:T(8,128)S(1)} %get-tuple-element.21.near, f32[2,2,64,128]{3,2,1,0:T(8,128)S(1)} %collective-permute-done.2.r2, ...), custom_call_target="tpu_custom_call" | custom-call | tf_op jit(solution)/shard_map/second_kernel/pallas_call | solution.py:327
  15.9 1.1 %collective-permute-start.6 = (f32[8,2,32,128]{3,2,1,0:T(8,128)S(1)}, f32[8,2,32,128]{3,2,1,0:T(8,128)S(1)}, u32[]{:S(2)}, u32[]{:S(2)}) collective-permute-start(f32[8,2,32,128]{3,2,1,0:T(8,128)S(1)} %get-tuple-element.26), channel_id=1, source_target_pairs={{0,1},{1,0},{2,3},{3,2},{4,5},{5,4},{6,7},{7,6},{8,9},{9,8},{10,11... | collective-permute-start | bytes 786440 | tf_op jit(solution)/shard_map/ppermute | solution.py:346
  17.1 1.1 %collective-permute-done.6 = f32[8,2,32,128]{3,2,1,0:T(8,128)S(1)} collective-permute-done((f32[8,2,32,128]{3,2,1,0:T(8,128)S(1)}, f32[8,2,32,128]{3,2,1,0:T(8,128)S(1)}, u32[]{:S(2)}, u32[]{:S(2)}) %collective-permute-start.6) | collective-permute-done | bytes 262176 | tf_op jit(solution)/shard_map/ppermute | solution.py:346
  18.2 1.1 %collective-permute-start.7 = (f32[2,2,2,32,128]{4,3,2,0,1:T(8,128)S(1)}, f32[2,2,2,32,128]{4,3,2,0,1:T(8,128)S(1)}, u32[]{:S(2)}, u32[]{:S(2)}) collective-permute-start(f32[2,2,2,32,128]{4,3,2,0,1:T(8,128)S(1)} %pad_maximum_fusion.1), channel_id=1, source_target_pairs={{0,8},{1,11},{2,10},{3,9},{4,12},{5,15},{6,14},{7,13},{8,0},{9,3},... | collective-permute-start | bytes 393224 | tf_op jit(solution)/shard_map/ppermute | solution.py:346
  19.3 1.3 %collective-permute-start.8 = (f32[2,2,2,32,128]{4,3,2,0,1:T(8,128)S(1)}, f32[2,2,2,32,128]{4,3,2,0,1:T(8,128)S(1)}, u32[]{:S(2)}, u32[]{:S(2)}) collective-permute-start(f32[2,2,2,32,128]{4,3,2,0,1:T(8,128)S(1)} %pad_maximum_fusion.2), channel_id=1, source_target_pairs={{0,4},{1,7},{2,6},{3,5},{4,0},{5,3},{6,2},{7,1},{8,12},{9,15},{10,... | collective-permute-start | bytes 393224 | tf_op jit(solution)/shard_map/ppermute | solution.py:346
  20.7 0.7 %before_kernel.1 = f32[2,2,2,32,128]{4,3,2,1,0:T(8,128)S(1)} custom-call(f32[2,2,32,128]{3,2,1,0:T(8,128)S(1)} %get-tuple-element.36.own, f32[2,2,32,128]{3,2,1,0:T(8,128)S(1)} %get-tuple-element.31.recv, f32[2,12,128,128]{3,2,1,0:T(8,128)S(1)} %copy-done), custom_call_target="tpu_custom_call" | custom-call | tf_op jit(solution)/shard_map/before_kernel/pallas_call | solution.py:327
  21.4 2.3 %collective-permute-start.11 = (f32[2,2,2,32,128]{4,3,2,1,0:T(8,128)S(1)}, f32[2,2,2,32,128]{4,3,2,1,0:T(8,128)S(1)}, u32[]{:S(2)}, u32[]{:S(2)}) collective-permute-start(f32[2,2,2,32,128]{4,3,2,1,0:T(8,128)S(1)} %before_kernel.1), channel_id=1, source_target_pairs={{0,12},{1,15},{2,14},{3,13},{4,8},{5,11},{6,10},{7,9},{8,4},{9,7},... | collective-permute-start | bytes 393224 | tf_op jit(solution)/shard_map/ppermute | solution.py:346
  23.7 0.3 collective-permute-start.9
  24.0 1.5 %collective-permute-done.7 = f32[2,2,2,32,128]{4,3,2,0,1:T(8,128)S(1)} collective-permute-done((f32[2,2,2,32,128]{4,3,2,0,1:T(8,128)S(1)}, f32[2,2,2,32,128]{4,3,2,0,1:T(8,128)S(1)}, u32[]{:S(2)}, u32[]{:S(2)}) %collective-permute-start.7) | collective-permute-done | bytes 131104 | tf_op jit(solution)/shard_map/ppermute | solution.py:346
  25.5 0.8 %collective-permute-done.8 = f32[2,2,2,32,128]{4,3,2,0,1:T(8,128)S(1)} collective-permute-done((f32[2,2,2,32,128]{4,3,2,0,1:T(8,128)S(1)}, f32[2,2,2,32,128]{4,3,2,0,1:T(8,128)S(1)}, u32[]{:S(2)}, u32[]{:S(2)}) %collective-permute-start.8) | collective-permute-done | bytes 131104 | tf_op jit(solution)/shard_map/ppermute | solution.py:346
  26.3 1.4 %collective-permute-done.9.y1 = f32[2,2,32,128]{3,2,1,0:T(8,128)S(1)} collective-permute-done((f32[2,2,32,128]{3,2,1,0:T(8,128)S(1)}, f32[2,2,32,128]{3,2,1,0:T(8,128)S(1)}, u32[]{:S(2)}, u32[]{:S(2)}) %collective-permute-start.9) | collective-permute-done | bytes 65568 | tf_op jit(solution)/shard_map/ppermute | solution.py:346
  27.8 0.9 %after_kernel.1 = (f32[8,2,32,128]{3,2,1,0:T(8,128)S(1)}, f32[4,2,32,128]{3,2,1,0:T(8,128)S(1)}) custom-call(f32[2,2,2,32,128]{4,3,2,1,0:T(8,128)S(1)} %copy.4.a0, f32[2,2,2,32,128]{4,3,2,1,0:T(8,128)S(1)} %copy.5.a1, f32[2,2,32,128]{3,2,1,0:T(8,128)S(1)} %collective-permute-done.9.y1, f32[2,32,128]{2,1,0:T(8,128)S(1)} %get-tuple-element.28.self0, ...), custom_call_target="tpu_custom_call" | custom-call | tf_op jit(solution)/shard_map/after_kernel/pallas_call | solution.py:327
  28.7 0.5 %collective-permute-start.10 = (f32[4,2,32,128]{3,2,1,0:T(8,128)S(1)}, f32[4,2,32,128]{3,2,1,0:T(8,128)S(1)}, u32[]{:S(2)}, u32[]{:S(2)}) collective-permute-start(f32[4,2,32,128]{3,2,1,0:T(8,128)S(1)} %get-tuple-element.30), channel_id=1, source_target_pairs={{0,1},{1,0},{2,3},{3,2},{4,5},{5,4},{6,7},{7,6},{8,9},{9,8},{10,11... | collective-permute-start | bytes 393224 | tf_op jit(solution)/shard_map/ppermute | solution.py:346
  29.1 4.6 %collective-permute-done.11.a2 = f32[2,2,2,32,128]{4,3,2,1,0:T(8,128)S(1)} collective-permute-done((f32[2,2,2,32,128]{4,3,2,1,0:T(8,128)S(1)}, f32[2,2,2,32,128]{4,3,2,1,0:T(8,128)S(1)}, u32[]{:S(2)}, u32[]{:S(2)}) %collective-permute-start.11) | collective-permute-done | bytes 131104 | tf_op jit(solution)/shard_map/ppermute | solution.py:346
  33.7 0.7 %collective-permute-start.12 = (f32[2,2,32,128]{3,2,1,0:T(8,128)S(1)}, f32[2,2,32,128]{3,2,1,0:T(8,128)S(1)}, u32[]{:S(2)}, u32[]{:S(2)}) collective-permute-start(f32[2,2,32,128]{3,2,1,0:T(8,128)S(1)} %slice_bitcast_fusion), channel_id=1, source_target_pairs={{0,1},{1,0},{2,3},{3,2},{4,5},{5,4},{6,7},{7,6},{8,9},{9,8},{10,11... | collective-permute-start | bytes 196616 | tf_op jit(solution)/shard_map/ppermute | solution.py:346
  34.4 0.9 %collective-permute-done.12.late = f32[2,2,32,128]{3,2,1,0:T(8,128)S(1)} collective-permute-done((f32[2,2,32,128]{3,2,1,0:T(8,128)S(1)}, f32[2,2,32,128]{3,2,1,0:T(8,128)S(1)}, u32[]{:S(2)}, u32[]{:S(2)}) %collective-permute-start.12) | collective-permute-done | bytes 65568 | tf_op jit(solution)/shard_map/ppermute | solution.py:346
  35.3 0.0 collective-permute-done.10.early
  35.3 1.6 %third_kernel.1 = f32[1024,128]{1,0:T(8,128)} custom-call(s32[1]{0:T(128)} %bitcast.me_ref, f32[8,2,32,128]{3,2,1,0:T(8,128)S(1)} %get-tuple-element.29.keep, f32[4,2,32,128]{3,2,1,0:T(8,128)S(1)} %collective-permute-done.10.early, f32[2,2,2,32,128]{4,3,2,1,0:T(8,128)S(1)} %collective-permute-done.11.a2, f32[2,2,32,128]{3,2,1,0:T(8,128)S(1)} %collective-permute-done.12.late, ...), custom_call_target="tpu_custom_call" | custom-call | tf_op jit(solution)/shard_map/third_kernel/pallas_call | solution.py:327
  (14 shorter events, 0.1 us)
Async XLA Ops:
  0.0 11.3 %copy-start = (f32[2,12,128,128]{3,2,1,0:T(8,128)S(1)}, f32[2,12,128,128]{3,2,1,0:T(8,128)}, u32[]{:S(2)}) copy-start(f32[2,12,128,128]{3,2,1,0:T(8,128)} %gates.11) | copy-start | bytes 4718596
  5.4 3.3 %collective-permute-start = (f32[2,2,64,128]{3,2,1,0:T(8,128)S(1)}, f32[2,2,64,128]{3,2,1,0:T(8,128)S(1)}, u32[]{:S(2)}, u32[]{:S(2)}) collective-permute-start(f32[2,2,64,128]{3,2,1,0:T(8,128)S(1)} %get-tuple-element.19), channel_id=1, source_target_pairs={{0,1},{1,0},{2,3},{3,2},{4,5},{5,4},{6,7},{7,6},{8,9},{9,8},{10,11... | collective-permute-start | bytes 393224 | tf_op jit(solution)/shard_map/ppermute | solution.py:346
  6.2 5.1 %collective-permute-start.1 = (f32[2,2,64,128]{3,2,1,0:T(8,128)S(1)}, f32[2,2,64,128]{3,2,1,0:T(8,128)S(1)}, u32[]{:S(2)}, u32[]{:S(2)}) collective-permute-start(f32[2,2,64,128]{3,2,1,0:T(8,128)S(1)} %get-tuple-element.20), channel_id=1, source_target_pairs={{0,2},{1,3},{2,0},{3,1},{4,6},{5,7},{6,4},{7,5},{8,10},{9,11},{10,... | collective-permute-start | bytes 393224 | tf_op jit(solution)/shard_map/ppermute | solution.py:346
  7.4 6.2 %collective-permute-start.2 = (f32[2,2,64,128]{3,2,1,0:T(8,128)S(1)}, f32[2,2,64,128]{3,2,1,0:T(8,128)S(1)}, u32[]{:S(2)}, u32[]{:S(2)}) collective-permute-start(f32[2,2,64,128]{3,2,1,0:T(8,128)S(1)} %get-tuple-element.22), channel_id=1, source_target_pairs={{0,4},{1,5},{2,6},{3,7},{4,0},{5,1},{6,2},{7,3},{8,12},{9,13},{10,... | collective-permute-start | bytes 393224 | tf_op jit(solution)/shard_map/ppermute | solution.py:346
  8.8 6.3 %collective-permute-start.3 = (f32[2,2,64,128]{3,2,1,0:T(8,128)S(1)}, f32[2,2,64,128]{3,2,1,0:T(8,128)S(1)}, u32[]{:S(2)}, u32[]{:S(2)}) collective-permute-start(f32[2,2,64,128]{3,2,1,0:T(8,128)S(1)} %pad_maximum_fusion), channel_id=1, source_target_pairs={{0,6},{1,7},{2,4},{3,5},{4,2},{5,3},{6,0},{7,1},{8,14},{9,15},{10,... | collective-permute-start | bytes 393224 | tf_op jit(solution)/shard_map/ppermute | solution.py:346
  12.8 1.8 %collective-permute-start.4 = (f32[2,64,128]{2,1,0:T(8,128)S(1)}, f32[2,64,128]{2,1,0:T(8,128)S(1)}, u32[]{:S(2)}, u32[]{:S(2)}) collective-permute-start(f32[2,64,128]{2,1,0:T(8,128)S(1)} %get-tuple-element.24), channel_id=1, source_target_pairs={{0,1},{1,0},{2,3},{3,2},{4,5},{5,4},{6,7},{7,6},{8,9},{9,8},{10,11... | collective-permute-start | bytes 196616 | tf_op jit(solution)/shard_map/ppermute | solution.py:346
  13.7 1.4 %collective-permute-start.5 = (f32[2,64,128]{2,1,0:T(8,128)S(1)}, f32[2,64,128]{2,1,0:T(8,128)S(1)}, u32[]{:S(2)}, u32[]{:S(2)}) collective-permute-start(f32[2,64,128]{2,1,0:T(8,128)S(1)} %slice_bitcast_fusion.3), channel_id=1, source_target_pairs={{0,1},{1,0},{2,3},{3,2},{4,5},{5,4},{6,7},{7,6},{8,9},{9,8},{10,11... | collective-permute-start | bytes 196616 | tf_op jit(solution)/shard_map/ppermute | solution.py:346
  15.9 2.3 %collective-permute-start.6 = (f32[8,2,32,128]{3,2,1,0:T(8,128)S(1)}, f32[8,2,32,128]{3,2,1,0:T(8,128)S(1)}, u32[]{:S(2)}, u32[]{:S(2)}) collective-permute-start(f32[8,2,32,128]{3,2,1,0:T(8,128)S(1)} %get-tuple-element.26), channel_id=1, source_target_pairs={{0,1},{1,0},{2,3},{3,2},{4,5},{5,4},{6,7},{7,6},{8,9},{9,8},{10,11... | collective-permute-start | bytes 786440 | tf_op jit(solution)/shard_map/ppermute | solution.py:346
  18.2 7.2 %collective-permute-start.7 = (f32[2,2,2,32,128]{4,3,2,0,1:T(8,128)S(1)}, f32[2,2,2,32,128]{4,3,2,0,1:T(8,128)S(1)}, u32[]{:S(2)}, u32[]{:S(2)}) collective-permute-start(f32[2,2,2,32,128]{4,3,2,0,1:T(8,128)S(1)} %pad_maximum_fusion.1), channel_id=1, source_target_pairs={{0,8},{1,11},{2,10},{3,9},{4,12},{5,15},{6,14},{7,13},{8,0},{9,3},... | collective-permute-start | bytes 393224 | tf_op jit(solution)/shard_map/ppermute | solution.py:346
  19.3 7.0 %collective-permute-start.8 = (f32[2,2,2,32,128]{4,3,2,0,1:T(8,128)S(1)}, f32[2,2,2,32,128]{4,3,2,0,1:T(8,128)S(1)}, u32[]{:S(2)}, u32[]{:S(2)}) collective-permute-start(f32[2,2,2,32,128]{4,3,2,0,1:T(8,128)S(1)} %pad_maximum_fusion.2), channel_id=1, source_target_pairs={{0,4},{1,7},{2,6},{3,5},{4,0},{5,3},{6,2},{7,1},{8,12},{9,15},{10,... | collective-permute-start | bytes 393224 | tf_op jit(solution)/shard_map/ppermute | solution.py:346
  21.4 12.4 %collective-permute-start.11 = (f32[2,2,2,32,128]{4,3,2,1,0:T(8,128)S(1)}, f32[2,2,2,32,128]{4,3,2,1,0:T(8,128)S(1)}, u32[]{:S(2)}, u32[]{:S(2)}) collective-permute-start(f32[2,2,2,32,128]{4,3,2,1,0:T(8,128)S(1)} %before_kernel.1), channel_id=1, source_target_pairs={{0,12},{1,15},{2,14},{3,13},{4,8},{5,11},{6,10},{7,9},{8,4},{9,7},... | collective-permute-start | bytes 393224 | tf_op jit(solution)/shard_map/ppermute | solution.py:346
  23.7 4.1 %collective-permute-start.9 = (f32[2,2,32,128]{3,2,1,0:T(8,128)S(1)}, f32[2,2,32,128]{3,2,1,0:T(8,128)S(1)}, u32[]{:S(2)}, u32[]{:S(2)}) collective-permute-start(f32[2,2,32,128]{3,2,1,0:T(8,128)S(1)} %pad_maximum_fusion.3), channel_id=1, source_target_pairs={{0,2},{1,3},{2,0},{3,1},{4,6},{5,7},{6,4},{7,5},{8,10},{9,11},{10,... | collective-permute-start | bytes 196616 | tf_op jit(solution)/shard_map/ppermute | solution.py:346
  28.7 6.6 %collective-permute-start.10 = (f32[4,2,32,128]{3,2,1,0:T(8,128)S(1)}, f32[4,2,32,128]{3,2,1,0:T(8,128)S(1)}, u32[]{:S(2)}, u32[]{:S(2)}) collective-permute-start(f32[4,2,32,128]{3,2,1,0:T(8,128)S(1)} %get-tuple-element.30), channel_id=1, source_target_pairs={{0,1},{1,0},{2,3},{3,2},{4,5},{5,4},{6,7},{7,6},{8,9},{9,8},{10,11... | collective-permute-start | bytes 393224 | tf_op jit(solution)/shard_map/ppermute | solution.py:346
  33.7 1.6 %collective-permute-start.12 = (f32[2,2,32,128]{3,2,1,0:T(8,128)S(1)}, f32[2,2,32,128]{3,2,1,0:T(8,128)S(1)}, u32[]{:S(2)}, u32[]{:S(2)}) collective-permute-start(f32[2,2,32,128]{3,2,1,0:T(8,128)S(1)} %slice_bitcast_fusion), channel_id=1, source_target_pairs={{0,1},{1,0},{2,3},{3,2},{4,5},{5,4},{6,7},{7,6},{8,9},{9,8},{10,11... | collective-permute-start | bytes 196616 | tf_op jit(solution)/shard_map/ppermute | solution.py:346

commit v3 on v2

--- a/solution.py
+++ b/solution.py
@@ -184,13 +184,7 @@
         return self.mh[k], self.ml[k]
 
 
-def lower_gates(s, g):
-    low_gate(s, g[4])
-    middle_gate(s, g[5])
-    low_gate(s, g[8])
-
-
-def first_kernel(indices, me_ref, amps, gates, q1, q2, own3, own0, give, s, own, sems, mh, ml, x, xsems, part):
+def first_kernel(indices, me_ref, amps, gates, q2, q1, own3, own0, give, s, own, sems, mh, ml, x, xsems):
     g = Gates(gates, (own, sems, mh, ml), indices)
     parts = []
     for b in range(2):
@@ -211,37 +205,39 @@
     middle_gate(s, g[1])
     high_gate(s, g[2])
     upper_gate(s, g[3], keeper(s))
-    sent = [(4, q2.at[0]), (5, q2.at[1]), (6, own3), (7, give.at[1])]
-    for n, (mask, _) in enumerate(sent):
+    for mask, out in enumerate((own0, give.at[0], *split(q1), *split(q2), own3, give.at[1])):
         at = rows_of(reversed3(low3 ^ mask), 64)
         for c in range(2):
-            part[c, pl.ds(64 * n, 64), :] = s[c, at, :]
-    for mask, out in ((0, own0), (1, give.at[0]), (2, q1.at[0]), (3, q1.at[1])):
-        at = rows_of(reversed3(low3 ^ mask), 64)
-        for c in range(2):
             out[c] = s[c, at, :]
-    lower_gates(part, g)
-    for n, (_, out) in enumerate(sent):
-        for c in range(2):
-            out[c] = part[c, pl.ds(64 * n, 64), :]
-
-
-def near_kernel(indices, own0, other0, r1, gates, keep, send, s, mh, ml):
+
+
+def lower_blocks(s, g, blocks, outs):
+    for n, block in enumerate(blocks):
+        for c in range(2):
+            s[c, pl.ds(64 * n, 64), :] = block[c]
+    low_gate(s, g[4])
+    middle_gate(s, g[5])
+    low_gate(s, g[8])
+    for n, out in enumerate(outs):
+        for c in range(2):
+            out[c] = s[c, pl.ds(64 * n, 64), :]
+
+
+def before_lower(indices, own0, own3, recv, gates, p0, p3, s, mh, ml):
     g = Ready(gates, (mh, ml), indices)
-    for n, block in enumerate((own0, other0, r1.at[0], r1.at[1])):
-        for c in range(2):
-            s[c, pl.ds(64 * n, 64), :] = block[c]
-    lower_gates(s, g)
-    for n, out in enumerate((keep.at[0], keep.at[1], keep.at[2], send)):
-        for c in range(2):
-            out[c] = s[c, pl.ds(64 * n, 64), :]
-
-
-def second_kernel(indices, me_ref, near, r2, r3, post1, post2, gates, own, give, y1, self0, s, mh, ml):
+    lower_blocks(s, g, (own0, recv.at[0], own3, recv.at[1]), (*split(p0), *split(p3)))
+
+
+def after_lower(indices, r1, r2, gates, keep, send1, send2, s, mh, ml):
+    g = Ready(gates, (mh, ml), indices)
+    lower_blocks(s, g, (*split(r1), *split(r2)), (keep.at[0], send1, keep.at[1], send2))
+
+
+def second_kernel(indices, me_ref, p0, near, r3, post1, post2, gates, own, give, y1, self0, s, mh, ml):
     g = Ready(gates, (mh, ml), indices)
     me = me_ref[0]
     low3, core = me & 7, me & 1
-    blocks = (near.at[0], near.at[1], near.at[2], post1, r2.at[0], post2, r3.at[0], r3.at[1])
+    blocks = (*split(p0), near.at[0], post1, near.at[1], post2, *split(r3))
     for mask, block in enumerate(blocks):
         at = rows_of(reversed3(low3 ^ mask), 64)
         for c in range(2):
@@ -319,6 +315,9 @@
 
 def shape(*dims):
     return jax.ShapeDtypeStruct(dims, F32)
+
+
+COST = {name: pl.CostEstimate(flops=n, bytes_accessed=1 << 18, transcendentals=0) for name, n in {"after_kernel": 2000000000, "after_lower": 2000000000, "before_kernel": 1000000000, "before_lower": 2000000000}.items()}
 
 
 def call(kernel, indices, outs, rows, operands, specs, scratch=(), out_specs=None, limit=32 << 20):
@@ -338,6 +337,7 @@
         ],
         compiler_params=pltpu.CompilerParams(vmem_limit_bytes=limit),
         name=kernel.__name__,
+        cost_estimate=COST.get(kernel.__name__),
     )(*operands)
 
 
@@ -354,35 +354,29 @@
     x = amplitudes.reshape(2, rows, LANES).transpose(1, 0, 2).reshape(2 * rows, LANES)
     interleaved = (pltpu.VMEM((2 * rows, LANES), F32), pltpu.SemaphoreType.DMA((2,)))
     one, two = shape(2, eighth, LANES), shape(2, 2, eighth, LANES)
-    q1, q2, own3, own0, give = call(
+    q2, q1, own3, own0, give = call(
         first_kernel,
-        (0, 1, 2, 3, 4, 5, 8),
+        (0, 1, 2, 3),
         [two, two, one, one, two],
         rows,
         [me, x, gates],
         [SMEM, HBM, HBM],
-        (*interleaved, pltpu.VMEM((2, 4 * eighth, LANES), F32)),
+        interleaved,
         limit=532 * 104858,
     )
     recv = flipped(give, 1)
     r1, r2 = flipped(q1, 2), flipped(q2, 4)
-    r3 = flipped(jnp.stack([own3, recv[1]]), 6)
-    near, send = call(
-        near_kernel,
-        (4, 5, 8),
-        [shape(3, 2, eighth, LANES), one],
-        4 * eighth,
-        [own0, recv[0], r1, gates],
-        [VMEM] * 4,
-    )
-    post1, post2 = flipped(send, 1), flipped(r2[1], 1)
+    p0, p3 = call(before_lower, (4, 5, 8), [two, two], 4 * eighth, [own0, own3, recv, gates], [VMEM] * 4)
+    r3 = flipped(p3, 6)
+    near, send1, send2 = call(after_lower, (4, 5, 8), [two, one, one], 4 * eighth, [r1, r2, gates], [VMEM] * 3)
+    post1, post2 = flipped(send1, 1), flipped(send2, 1)
     block = (2, part16, LANES)
     own, give, y1, self0 = call(
         second_kernel,
         (6, 7),
         [shape(3, 2, *block), shape(8, *block), shape(*block), shape(*block)],
         rows,
-        [me, near, r2, r3, post1, post2, gates],
+        [me, p0, near, r3, post1, post2, gates],
         [SMEM] + [VMEM] * 6,
     )
     recv = flipped(give, 1)

time: 37 us -> 36 us (0.973)
  starting transfers between devices: 12.6 us -> 12 us
    ppermute x13, starting transfers between devices: 12.6 us -> 12 us  [flipped(): return lax.ppermute(block, 'node', route)]
    pallas_call x6 -> x7, Pallas kernels: 11 us -> 10.8 us  [call(): pl.pallas_call(functools.partial(kernel, indices), out_shape=outs, in_spe...]
  transfers between devices with their start and end apart: 13 -> 13, of which waited for: 9 -> 9; matrix products, arithmetic and copies ran while one was open for 0% -> 0% of each run, Pallas kernels for 8% -> 13%
where the time goes in v3:
time: 36 us; the launch traced here: 35.8 us
  waiting for transfers between devices  12.9 us (36%)
  starting transfers between devices  12 us (33%)
  Pallas kernels  10.8 us (30%)
    ppermute x13, waiting for transfers between devices, flipped(): return lax.ppermute(block, 'node', route)  12.9 us
    ppermute x13, starting transfers between devices, flipped(): return lax.ppermute(block, 'node', route)  12 us
    pallas_call x7, Pallas kernels, call(): pl.pallas_call(functools.partial(kernel, indices), out_shape=outs, in_spe...  10.8 us
  transfers between devices with their start and end apart: 13, of which 9 were waited for; matrix products, arithmetic and copies ran while one was open for 0% of the time, Pallas kernels for 13%

profile of v3, /device:TPU:19, one launch (start us, length us, event | category | flops | bytes accessed | tf_op | source)
XLA Modules:
  0.0 35.8 jit_solution(8418527967594470651)
XLA Ops:
  0.0 3.7 %first_kernel.1 = (f32[2,2,64,128]{3,2,1,0:T(8,128)S(1)}, f32[2,2,64,128]{3,2,1,0:T(8,128)S(1)}, f32[2,64,128]{2,1,0:T(8,128)S(1)}, f32[2,64,128]{2,1,0:T(8,128)S(1)}, f32[2,2,64,128]{3,2,1,0:T(8,128)S(1)}) custom-call(s32[1]{0:T(128)} %bitcast.me_ref, f32[1024,128]{1,0:T(8,128)} %bitcast.27, f32[2,12,128,128]{3,2,1,0:T(8,128)} %gates.13), custom_call_target="tpu_custom_call" | custom-call | tf_op jit(solution)/shard_map/first_kernel/pallas_call | solution.py:326
  3.7 0.7 %collective-permute-start = (f32[2,2,64,128]{3,2,1,0:T(8,128)S(1)}, f32[2,2,64,128]{3,2,1,0:T(8,128)S(1)}, u32[]{:S(2)}, u32[]{:S(2)}) collective-permute-start(f32[2,2,64,128]{3,2,1,0:T(8,128)S(1)} %get-tuple-element.23), channel_id=1, source_target_pairs={{0,1},{1,0},{2,3},{3,2},{4,5},{5,4},{6,7},{7,6},{8,9},{9,8},{10,11... | collective-permute-start | bytes 393224 | tf_op jit(solution)/shard_map/ppermute | solution.py:346
  4.5 1.3 %collective-permute-start.1 = (f32[2,2,64,128]{3,2,1,0:T(8,128)S(1)}, f32[2,2,64,128]{3,2,1,0:T(8,128)S(1)}, u32[]{:S(2)}, u32[]{:S(2)}) collective-permute-start(f32[2,2,64,128]{3,2,1,0:T(8,128)S(1)} %get-tuple-element.25), channel_id=1, source_target_pairs={{0,2},{1,3},{2,0},{3,1},{4,6},{5,7},{6,4},{7,5},{8,10},{9,11},{10,... | collective-permute-start | bytes 393224 | tf_op jit(solution)/shard_map/ppermute | solution.py:346
  5.7 1.3 %collective-permute-start.2 = (f32[2,2,64,128]{3,2,1,0:T(8,128)S(1)}, f32[2,2,64,128]{3,2,1,0:T(8,128)S(1)}, u32[]{:S(2)}, u32[]{:S(2)}) collective-permute-start(f32[2,2,64,128]{3,2,1,0:T(8,128)S(1)} %get-tuple-element.26), channel_id=1, source_target_pairs={{0,4},{1,5},{2,6},{3,7},{4,0},{5,1},{6,2},{7,3},{8,12},{9,13},{10,... | collective-permute-start | bytes 393224 | tf_op jit(solution)/shard_map/ppermute | solution.py:346
  7.0 0.0 collective-permute-done.recv
  7.0 1.5 %before_lower.1 = (f32[2,2,64,128]{3,2,1,0:T(8,128)S(1)}, f32[2,2,64,128]{3,2,1,0:T(8,128)S(1)}) custom-call(f32[2,64,128]{2,1,0:T(8,128)S(1)} %get-tuple-element.21.own0, f32[2,64,128]{2,1,0:T(8,128)S(1)} %get-tuple-element.22.own3, f32[2,2,64,128]{3,2,1,0:T(8,128)S(1)} %collective-permute-done.recv, f32[2,12,128,128]{3,2,1,0:T(8,128)S(1)} %copy-done), custom_call_target="tpu_custom_call" | custom-call | flops 2000000000 | bytes 262144 | tf_op jit(solution)/shard_map/before_lower/pallas_call | solution.py:326
  8.5 0.7 %collective-permute-start.3 = (f32[2,2,64,128]{3,2,1,0:T(8,128)S(1)}, f32[2,2,64,128]{3,2,1,0:T(8,128)S(1)}, u32[]{:S(2)}, u32[]{:S(2)}) collective-permute-start(f32[2,2,64,128]{3,2,1,0:T(8,128)S(1)} %get-tuple-element.28), channel_id=1, source_target_pairs={{0,6},{1,7},{2,4},{3,5},{4,2},{5,3},{6,0},{7,1},{8,14},{9,15},{10,... | collective-permute-start | bytes 393224 | tf_op jit(solution)/shard_map/ppermute | solution.py:346
  9.3 0.3 collective-permute-done.1.r1
  9.6 0.9 %collective-permute-done.2.r2 = f32[2,2,64,128]{3,2,1,0:T(8,128)S(1)} collective-permute-done((f32[2,2,64,128]{3,2,1,0:T(8,128)S(1)}, f32[2,2,64,128]{3,2,1,0:T(8,128)S(1)}, u32[]{:S(2)}, u32[]{:S(2)}) %collective-permute-start.2) | collective-permute-done | bytes 131104 | tf_op jit(solution)/shard_map/ppermute | solution.py:346
  10.5 1.5 %after_lower.1 = (f32[2,2,64,128]{3,2,1,0:T(8,128)S(1)}, f32[2,64,128]{2,1,0:T(8,128)S(1)}, f32[2,64,128]{2,1,0:T(8,128)S(1)}) custom-call(f32[2,2,64,128]{3,2,1,0:T(8,128)S(1)} %collective-permute-done.1.r1, f32[2,2,64,128]{3,2,1,0:T(8,128)S(1)} %collective-permute-done.2.r2, f32[2,12,128,128]{3,2,1,0:T(8,128)S(1)} %copy-done), custom_call_target="tpu_custom_call" | custom-call | flops 2000000000 | bytes 262144 | tf_op jit(solution)/shard_map/after_lower/pallas_call | solution.py:326
  12.0 1.2 %collective-permute-start.4 = (f32[2,64,128]{2,1,0:T(8,128)S(1)}, f32[2,64,128]{2,1,0:T(8,128)S(1)}, u32[]{:S(2)}, u32[]{:S(2)}) collective-permute-start(f32[2,64,128]{2,1,0:T(8,128)S(1)} %get-tuple-element.29), channel_id=1, source_target_pairs={{0,1},{1,0},{2,3},{3,2},{4,5},{5,4},{6,7},{7,6},{8,9},{9,8},{10,11... | collective-permute-start | bytes 196616 | tf_op jit(solution)/shard_map/ppermute | solution.py:346
  13.2 0.1 collective-permute-start.5
  13.3 0.8 %collective-permute-done.4.post1 = f32[2,64,128]{2,1,0:T(8,128)S(1)} collective-permute-done((f32[2,64,128]{2,1,0:T(8,128)S(1)}, f32[2,64,128]{2,1,0:T(8,128)S(1)}, u32[]{:S(2)}, u32[]{:S(2)}) %collective-permute-start.4) | collective-permute-done | bytes 65568 | tf_op jit(solution)/shard_map/ppermute | solution.py:346
  14.1 0.4 collective-permute-done.5.post2
  14.5 0.0 collective-permute-done.3.r3
  14.5 0.9 %second_kernel.1 = (f32[3,2,2,32,128]{4,3,2,1,0:T(8,128)S(1)}, f32[8,2,32,128]{3,2,1,0:T(8,128)S(1)}, f32[2,32,128]{2,1,0:T(8,128)S(1)}, f32[2,32,128]{2,1,0:T(8,128)S(1)}) custom-call(s32[1]{0:T(128)} %bitcast.me_ref, f32[2,2,64,128]{3,2,1,0:T(8,128)S(1)} %get-tuple-element.24.p0, f32[2,2,64,128]{3,2,1,0:T(8,128)S(1)} %get-tuple-element.27.near, ...), custom_call_target="tpu_custom_call" | custom-call | tf_op jit(solution)/shard_map/second_kernel/pallas_call | solution.py:326
  15.3 1.0 %collective-permute-start.6 = (f32[8,2,32,128]{3,2,1,0:T(8,128)S(1)}, f32[8,2,32,128]{3,2,1,0:T(8,128)S(1)}, u32[]{:S(2)}, u32[]{:S(2)}) collective-permute-start(f32[8,2,32,128]{3,2,1,0:T(8,128)S(1)} %get-tuple-element.32), channel_id=1, source_target_pairs={{0,1},{1,0},{2,3},{3,2},{4,5},{5,4},{6,7},{7,6},{8,9},{9,8},{10,11... | collective-permute-start | bytes 786440 | tf_op jit(solution)/shard_map/ppermute | solution.py:346
  16.4 1.1 %collective-permute-done.6 = f32[8,2,32,128]{3,2,1,0:T(8,128)S(1)} collective-permute-done((f32[8,2,32,128]{3,2,1,0:T(8,128)S(1)}, f32[8,2,32,128]{3,2,1,0:T(8,128)S(1)}, u32[]{:S(2)}, u32[]{:S(2)}) %collective-permute-start.6) | collective-permute-done | bytes 262176 | tf_op jit(solution)/shard_map/ppermute | solution.py:346
  17.5 0.1 collective-permute-start.7
  17.6 2.2 %collective-permute-start.8 = (f32[2,2,2,32,128]{4,3,2,0,1:T(8,128)S(1)}, f32[2,2,2,32,128]{4,3,2,0,1:T(8,128)S(1)}, u32[]{:S(2)}, u32[]{:S(2)}) collective-permute-start(f32[2,2,2,32,128]{4,3,2,0,1:T(8,128)S(1)} %pad_maximum_fusion.1), channel_id=1, source_target_pairs={{0,4},{1,7},{2,6},{3,5},{4,0},{5,3},{6,2},{7,1},{8,12},{9,15},{10,... | collective-permute-start | bytes 393224 | tf_op jit(solution)/shard_map/ppermute | solution.py:346
  19.9 0.4 %collective-permute-start.9 = (f32[2,2,32,128]{3,2,1,0:T(8,128)S(1)}, f32[2,2,32,128]{3,2,1,0:T(8,128)S(1)}, u32[]{:S(2)}, u32[]{:S(2)}) collective-permute-start(f32[2,2,32,128]{3,2,1,0:T(8,128)S(1)} %pad_maximum_fusion.2), channel_id=1, source_target_pairs={{0,2},{1,3},{2,0},{3,1},{4,6},{5,7},{6,4},{7,5},{8,10},{9,11},{10,... | collective-permute-start | bytes 196616 | tf_op jit(solution)/shard_map/ppermute | solution.py:346
  20.2 0.7 %before_kernel.1 = f32[2,2,2,32,128]{4,3,2,1,0:T(8,128)S(1)} custom-call(f32[2,2,32,128]{3,2,1,0:T(8,128)S(1)} %get-tuple-element.42.own, f32[2,2,32,128]{3,2,1,0:T(8,128)S(1)} %get-tuple-element.37.recv, f32[2,12,128,128]{3,2,1,0:T(8,128)S(1)} %copy-done), custom_call_target="tpu_custom_call" | custom-call | flops 1000000000 | bytes 262144 | tf_op jit(solution)/shard_map/before_kernel/pallas_call | solution.py:326
  20.9 2.3 %collective-permute-start.11 = (f32[2,2,2,32,128]{4,3,2,1,0:T(8,128)S(1)}, f32[2,2,2,32,128]{4,3,2,1,0:T(8,128)S(1)}, u32[]{:S(2)}, u32[]{:S(2)}) collective-permute-start(f32[2,2,2,32,128]{4,3,2,1,0:T(8,128)S(1)} %before_kernel.1), channel_id=1, source_target_pairs={{0,12},{1,15},{2,14},{3,13},{4,8},{5,11},{6,10},{7,9},{8,4},{9,7},... | collective-permute-start | bytes 393224 | tf_op jit(solution)/shard_map/ppermute | solution.py:346
  23.2 1.5 %collective-permute-done.7 = f32[2,2,2,32,128]{4,3,2,0,1:T(8,128)S(1)} collective-permute-done((f32[2,2,2,32,128]{4,3,2,0,1:T(8,128)S(1)}, f32[2,2,2,32,128]{4,3,2,0,1:T(8,128)S(1)}, u32[]{:S(2)}, u32[]{:S(2)}) %collective-permute-start.7) | collective-permute-done | bytes 131104 | tf_op jit(solution)/shard_map/ppermute | solution.py:346
  24.8 1.5 %collective-permute-done.8 = f32[2,2,2,32,128]{4,3,2,0,1:T(8,128)S(1)} collective-permute-done((f32[2,2,2,32,128]{4,3,2,0,1:T(8,128)S(1)}, f32[2,2,2,32,128]{4,3,2,0,1:T(8,128)S(1)}, u32[]{:S(2)}, u32[]{:S(2)}) %collective-permute-start.8) | collective-permute-done | bytes 131104 | tf_op jit(solution)/shard_map/ppermute | solution.py:346
  26.4 0.0 collective-permute-done.9.y1
  26.4 0.9 %after_kernel.1 = (f32[8,2,32,128]{3,2,1,0:T(8,128)S(1)}, f32[4,2,32,128]{3,2,1,0:T(8,128)S(1)}) custom-call(f32[2,2,2,32,128]{4,3,2,1,0:T(8,128)S(1)} %copy.4.a0, f32[2,2,2,32,128]{4,3,2,1,0:T(8,128)S(1)} %copy.5.a1, f32[2,2,32,128]{3,2,1,0:T(8,128)S(1)} %collective-permute-done.9.y1, f32[2,32,128]{2,1,0:T(8,128)S(1)} %get-tuple-element.34.self0, ...), custom_call_target="tpu_custom_call" | custom-call | flops 2000000000 | bytes 262144 | tf_op jit(solution)/shard_map/after_kernel/pallas_call | solution.py:326
  27.3 0.6 %collective-permute-start.10 = (f32[4,2,32,128]{3,2,1,0:T(8,128)S(1)}, f32[4,2,32,128]{3,2,1,0:T(8,128)S(1)}, u32[]{:S(2)}, u32[]{:S(2)}) collective-permute-start(f32[4,2,32,128]{3,2,1,0:T(8,128)S(1)} %get-tuple-element.36), channel_id=1, source_target_pairs={{0,1},{1,0},{2,3},{3,2},{4,5},{5,4},{6,7},{7,6},{8,9},{9,8},{10,11... | collective-permute-start | bytes 393224 | tf_op jit(solution)/shard_map/ppermute | solution.py:346
  27.9 5.0 %collective-permute-done.11.a2 = f32[2,2,2,32,128]{4,3,2,1,0:T(8,128)S(1)} collective-permute-done((f32[2,2,2,32,128]{4,3,2,1,0:T(8,128)S(1)}, f32[2,2,2,32,128]{4,3,2,1,0:T(8,128)S(1)}, u32[]{:S(2)}, u32[]{:S(2)}) %collective-permute-start.11) | collective-permute-done | bytes 131104 | tf_op jit(solution)/shard_map/ppermute | solution.py:346
  32.9 0.0 collective-permute-start.12
  32.9 1.2 %collective-permute-done.12.late = f32[2,2,32,128]{3,2,1,0:T(8,128)S(1)} collective-permute-done((f32[2,2,32,128]{3,2,1,0:T(8,128)S(1)}, f32[2,2,32,128]{3,2,1,0:T(8,128)S(1)}, u32[]{:S(2)}, u32[]{:S(2)}) %collective-permute-start.12) | collective-permute-done | bytes 65568 | tf_op jit(solution)/shard_map/ppermute | solution.py:346
  34.2 1.6 %third_kernel.1 = f32[1024,128]{1,0:T(8,128)} custom-call(s32[1]{0:T(128)} %bitcast.me_ref, f32[8,2,32,128]{3,2,1,0:T(8,128)S(1)} %get-tuple-element.35.keep, f32[4,2,32,128]{3,2,1,0:T(8,128)S(1)} %collective-permute-done.10.early, f32[2,2,2,32,128]{4,3,2,1,0:T(8,128)S(1)} %collective-permute-done.11.a2, f32[2,2,32,128]{3,2,1,0:T(8,128)S(1)} %collective-permute-done.12.late, ...), custom_call_target="tpu_custom_call" | custom-call | tf_op jit(solution)/shard_map/third_kernel/pallas_call | solution.py:326
  (12 shorter events, 0.1 us)
Async XLA Ops:
  0.0 7.0 %copy-start = (f32[2,12,128,128]{3,2,1,0:T(8,128)S(1)}, f32[2,12,128,128]{3,2,1,0:T(8,128)}, u32[]{:S(2)}) copy-start(f32[2,12,128,128]{3,2,1,0:T(8,128)} %gates.13) | copy-start | bytes 4718596
  3.7 3.3 %collective-permute-start = (f32[2,2,64,128]{3,2,1,0:T(8,128)S(1)}, f32[2,2,64,128]{3,2,1,0:T(8,128)S(1)}, u32[]{:S(2)}, u32[]{:S(2)}) collective-permute-start(f32[2,2,64,128]{3,2,1,0:T(8,128)S(1)} %get-tuple-element.23), channel_id=1, source_target_pairs={{0,1},{1,0},{2,3},{3,2},{4,5},{5,4},{6,7},{7,6},{8,9},{9,8},{10,11... | collective-permute-start | bytes 393224 | tf_op jit(solution)/shard_map/ppermute | solution.py:346
  4.5 5.1 %collective-permute-start.1 = (f32[2,2,64,128]{3,2,1,0:T(8,128)S(1)}, f32[2,2,64,128]{3,2,1,0:T(8,128)S(1)}, u32[]{:S(2)}, u32[]{:S(2)}) collective-permute-start(f32[2,2,64,128]{3,2,1,0:T(8,128)S(1)} %get-tuple-element.25), channel_id=1, source_target_pairs={{0,2},{1,3},{2,0},{3,1},{4,6},{5,7},{6,4},{7,5},{8,10},{9,11},{10,... | collective-permute-start | bytes 393224 | tf_op jit(solution)/shard_map/ppermute | solution.py:346
  5.7 4.7 %collective-permute-start.2 = (f32[2,2,64,128]{3,2,1,0:T(8,128)S(1)}, f32[2,2,64,128]{3,2,1,0:T(8,128)S(1)}, u32[]{:S(2)}, u32[]{:S(2)}) collective-permute-start(f32[2,2,64,128]{3,2,1,0:T(8,128)S(1)} %get-tuple-element.26), channel_id=1, source_target_pairs={{0,4},{1,5},{2,6},{3,7},{4,0},{5,1},{6,2},{7,3},{8,12},{9,13},{10,... | collective-permute-start | bytes 393224 | tf_op jit(solution)/shard_map/ppermute | solution.py:346
  8.5 5.9 %collective-permute-start.3 = (f32[2,2,64,128]{3,2,1,0:T(8,128)S(1)}, f32[2,2,64,128]{3,2,1,0:T(8,128)S(1)}, u32[]{:S(2)}, u32[]{:S(2)}) collective-permute-start(f32[2,2,64,128]{3,2,1,0:T(8,128)S(1)} %get-tuple-element.28), channel_id=1, source_target_pairs={{0,6},{1,7},{2,4},{3,5},{4,2},{5,3},{6,0},{7,1},{8,14},{9,15},{10,... | collective-permute-start | bytes 393224 | tf_op jit(solution)/shard_map/ppermute | solution.py:346
  12.0 2.1 %collective-permute-start.4 = (f32[2,64,128]{2,1,0:T(8,128)S(1)}, f32[2,64,128]{2,1,0:T(8,128)S(1)}, u32[]{:S(2)}, u32[]{:S(2)}) collective-permute-start(f32[2,64,128]{2,1,0:T(8,128)S(1)} %get-tuple-element.29), channel_id=1, source_target_pairs={{0,1},{1,0},{2,3},{3,2},{4,5},{5,4},{6,7},{7,6},{8,9},{9,8},{10,11... | collective-permute-start | bytes 196616 | tf_op jit(solution)/shard_map/ppermute | solution.py:346
  13.2 1.3 %collective-permute-start.5 = (f32[2,64,128]{2,1,0:T(8,128)S(1)}, f32[2,64,128]{2,1,0:T(8,128)S(1)}, u32[]{:S(2)}, u32[]{:S(2)}) collective-permute-start(f32[2,64,128]{2,1,0:T(8,128)S(1)} %get-tuple-element.30), channel_id=1, source_target_pairs={{0,1},{1,0},{2,3},{3,2},{4,5},{5,4},{6,7},{7,6},{8,9},{9,8},{10,11... | collective-permute-start | bytes 196616 | tf_op jit(solution)/shard_map/ppermute | solution.py:346
  15.3 2.2 %collective-permute-start.6 = (f32[8,2,32,128]{3,2,1,0:T(8,128)S(1)}, f32[8,2,32,128]{3,2,1,0:T(8,128)S(1)}, u32[]{:S(2)}, u32[]{:S(2)}) collective-permute-start(f32[8,2,32,128]{3,2,1,0:T(8,128)S(1)} %get-tuple-element.32), channel_id=1, source_target_pairs={{0,1},{1,0},{2,3},{3,2},{4,5},{5,4},{6,7},{7,6},{8,9},{9,8},{10,11... | collective-permute-start | bytes 786440 | tf_op jit(solution)/shard_map/ppermute | solution.py:346
  17.5 7.3 %collective-permute-start.7 = (f32[2,2,2,32,128]{4,3,2,0,1:T(8,128)S(1)}, f32[2,2,2,32,128]{4,3,2,0,1:T(8,128)S(1)}, u32[]{:S(2)}, u32[]{:S(2)}) collective-permute-start(f32[2,2,2,32,128]{4,3,2,0,1:T(8,128)S(1)} %pad_maximum_fusion), channel_id=1, source_target_pairs={{0,8},{1,11},{2,10},{3,9},{4,12},{5,15},{6,14},{7,13},{8,0},{9,3},... | collective-permute-start | bytes 393224 | tf_op jit(solution)/shard_map/ppermute | solution.py:346
  17.6 8.7 %collective-permute-start.8 = (f32[2,2,2,32,128]{4,3,2,0,1:T(8,128)S(1)}, f32[2,2,2,32,128]{4,3,2,0,1:T(8,128)S(1)}, u32[]{:S(2)}, u32[]{:S(2)}) collective-permute-start(f32[2,2,2,32,128]{4,3,2,0,1:T(8,128)S(1)} %pad_maximum_fusion.1), channel_id=1, source_target_pairs={{0,4},{1,7},{2,6},{3,5},{4,0},{5,3},{6,2},{7,1},{8,12},{9,15},{10,... | collective-permute-start | bytes 393224 | tf_op jit(solution)/shard_map/ppermute | solution.py:346
  19.9 6.5 %collective-permute-start.9 = (f32[2,2,32,128]{3,2,1,0:T(8,128)S(1)}, f32[2,2,32,128]{3,2,1,0:T(8,128)S(1)}, u32[]{:S(2)}, u32[]{:S(2)}) collective-permute-start(f32[2,2,32,128]{3,2,1,0:T(8,128)S(1)} %pad_maximum_fusion.2), channel_id=1, source_target_pairs={{0,2},{1,3},{2,0},{3,1},{4,6},{5,7},{6,4},{7,5},{8,10},{9,11},{10,... | collective-permute-start | bytes 196616 | tf_op jit(solution)/shard_map/ppermute | solution.py:346
  20.9 12.0 %collective-permute-start.11 = (f32[2,2,2,32,128]{4,3,2,1,0:T(8,128)S(1)}, f32[2,2,2,32,128]{4,3,2,1,0:T(8,128)S(1)}, u32[]{:S(2)}, u32[]{:S(2)}) collective-permute-start(f32[2,2,2,32,128]{4,3,2,1,0:T(8,128)S(1)} %before_kernel.1), channel_id=1, source_target_pairs={{0,12},{1,15},{2,14},{3,13},{4,8},{5,11},{6,10},{7,9},{8,4},{9,7},... | collective-permute-start | bytes 393224 | tf_op jit(solution)/shard_map/ppermute | solution.py:346
  27.3 6.9 %collective-permute-start.10 = (f32[4,2,32,128]{3,2,1,0:T(8,128)S(1)}, f32[4,2,32,128]{3,2,1,0:T(8,128)S(1)}, u32[]{:S(2)}, u32[]{:S(2)}) collective-permute-start(f32[4,2,32,128]{3,2,1,0:T(8,128)S(1)} %get-tuple-element.36), channel_id=1, source_target_pairs={{0,1},{1,0},{2,3},{3,2},{4,5},{5,4},{6,7},{7,6},{8,9},{9,8},{10,11... | collective-permute-start | bytes 393224 | tf_op jit(solution)/shard_map/ppermute | solution.py:346
  32.9 1.3 %collective-permute-start.12 = (f32[2,2,32,128]{3,2,1,0:T(8,128)S(1)}, f32[2,2,32,128]{3,2,1,0:T(8,128)S(1)}, u32[]{:S(2)}, u32[]{:S(2)}) collective-permute-start(f32[2,2,32,128]{3,2,1,0:T(8,128)S(1)} %slice_bitcast_fusion), channel_id=1, source_target_pairs={{0,1},{1,0},{2,3},{3,2},{4,5},{5,4},{6,7},{7,6},{8,9},{9,8},{10,11... | collective-permute-start | bytes 196616 | tf_op jit(solution)/shard_map/ppermute | solution.py:346

commit v4 on v3

--- a/solution.py
+++ b/solution.py
@@ -270,9 +270,9 @@
             out[c] = s[c, pl.ds(32 * n, 32), :]
 
 
-def before_kernel(indices, own, recv, gates, out, s, mh, ml):
+def before_kernel(indices, own, recv, gates, out0, out1, s, mh, ml):
     g = Ready(gates, (mh, ml), indices)
-    gate_nine(s, g, (*split(own), *split(recv)), [out.at[f, src] for src in range(2) for f in range(2)])
+    gate_nine(s, g, (*split(own), *split(recv)), [out.at[src] for src in range(2) for out in (out0, out1)])
 
 
 def after_kernel(indices, a0, a1, y1, self0, other, gates, keep, send, s, mh, ml):
@@ -282,7 +282,13 @@
     gate_nine(s, g, blocks, [keep.at[n] for n in range(8)] + [send.at[n] for n in range(4)])
 
 
-def third_kernel(indices, me_ref, keep, early, a2, late, gates, out, s, mh, ml, y, ysems):
+def join_kernel(indices, mine, late, out, s, mh, ml):
+    for n, block in enumerate((*split(mine), *split(late))):
+        for c in range(2):
+            out[n, c] = block[c]
+
+
+def third_kernel(indices, me_ref, keep, early, far, gates, out, s, mh, ml, y, ysems):
     g = Ready(gates, (mh, ml), indices)
     me = me_ref[0]
     core = me & 1
@@ -294,8 +300,8 @@
 
     for i, base in enumerate(PORTS):
         for src in range(2):
-            place(keep.at[2 * i + src] if i < 2 else a2.at[0, src], 2 * (base + core) + src)
-            place(early.at[2 * i + src] if i < 2 else late.at[src], 2 * (base + 1 - core) + (1 - src))
+            place(keep.at[2 * i + src] if i < 2 else far.at[src], 2 * (base + core) + src)
+            place(early.at[2 * i + src] if i < 2 else far.at[2 + src], 2 * (base + 1 - core) + (1 - src))
     for n, mask in ((4, 2), (5, 3), (6, 0), (7, 1)):
         place(keep.at[n], mask)
     high_gate(s, g[10])
@@ -317,7 +323,7 @@
     return jax.ShapeDtypeStruct(dims, F32)
 
 
-COST = {name: pl.CostEstimate(flops=n, bytes_accessed=1 << 18, transcendentals=0) for name, n in {"after_kernel": 2000000000, "after_lower": 2000000000, "before_kernel": 1000000000, "before_lower": 2000000000}.items()}
+COST = {name: pl.CostEstimate(flops=n, bytes_accessed=1 << 18, transcendentals=0) for name, n in {"join_kernel": 2000000000, "after_kernel": 2000000000, "after_lower": 2000000000, "before_kernel": 1000000000, "before_lower": 2000000000}.items()}
 
 
 def call(kernel, indices, outs, rows, operands, specs, scratch=(), out_specs=None, limit=32 << 20):
@@ -381,10 +387,11 @@
     )
     recv = flipped(give, 1)
     ready = call(
-        before_kernel, (9,), [shape(2, 2, *block)], 4 * part16, [own[2], recv[4:6], gates], [VMEM] * 3
-    )[0]
-    payloads = [jnp.stack([own[i], recv[2 * i : 2 * i + 2]], 1) for i in range(2)] + [ready]
-    a0, a1, a2 = [flipped(payload, 2 * base, 2) for base, payload in zip(PORTS, payloads)]
+        before_kernel, (9,), [shape(2, *block)] * 2, 4 * part16, [own[2], recv[4:6], gates], [VMEM] * 3
+    )
+    payloads = [jnp.stack([own[i], recv[2 * i : 2 * i + 2]], 1) for i in range(2)]
+    a0, a1 = [flipped(payload, 2 * base, 2) for base, payload in zip(PORTS, payloads)]
+    mine, late = [flipped(payload, 2 * PORTS[2] + f, 2) for f, payload in enumerate(ready)]
     y1 = flipped(jnp.stack([y1, recv[6]]), 2)
     keep, send = call(
         after_kernel,
@@ -394,14 +401,15 @@
         [a0, a1, y1, self0, recv[7], gates],
         [VMEM] * 6,
     )
-    early, late = flipped(send, 1), flipped(a2[1], 1)
+    early = flipped(send, 1)
+    far = call(join_kernel, (9,), [shape(4, *block)], 8, [mine, late], [VMEM] * 2)[0]
     out = call(
         third_kernel,
         (10, 11),
         [shape(2 * rows, LANES)],
         rows,
-        [me, keep, early, a2, late, gates],
-        [SMEM] + [VMEM] * 5,
+        [me, keep, early, far, gates],
+        [SMEM] + [VMEM] * 4,
         interleaved,
         [HBM],
     )[0]

time: 36 us -> 34.7 us (0.964); the launches traced: 35.8 us -> 34.1 us
  waiting for transfers between devices: 12.9 us -> 10.8 us
    ppermute x13, waiting for transfers between devices: 12.9 us -> 10.8 us  [flipped(): return lax.ppermute(block, 'node', route)]
    ppermute x13, starting transfers between devices: 12 us -> 12.3 us  [flipped(): return lax.ppermute(block, 'node', route)]
    pallas_call x7 -> x8, Pallas kernels: 10.8 us -> 10.8 us  [call(): pl.pallas_call(functools.partial(kernel, indices), out_shape=outs, in_spe...]
where the time goes in v4:
time: 34.7 us; the launch traced here: 34.1 us
  starting transfers between devices  12.3 us (35%)
  Pallas kernels  10.8 us (31%)
  waiting for transfers between devices  10.8 us (31%)
    ppermute x13, starting transfers between devices, flipped(): return lax.ppermute(block, 'node', route)  12.3 us
    pallas_call x8, Pallas kernels, call(): pl.pallas_call(functools.partial(kernel, indices), out_shape=outs, in_spe...  10.8 us
    ppermute x13, waiting for transfers between devices, flipped(): return lax.ppermute(block, 'node', route)  10.8 us
  transfers between devices with their start and end apart: 13, of which 9 were waited for; matrix products, arithmetic and copies ran while one was open for 0% of the time, Pallas kernels for 13%

profile of v4, /device:TPU:19, one launch (start us, length us, event | category | flops | bytes accessed | tf_op | source)
XLA Modules:
  0.0 34.1 jit_solution(12811070678140653757)
XLA Ops:
  0.0 3.7 %first_kernel.1 = (f32[2,2,64,128]{3,2,1,0:T(8,128)S(1)}, f32[2,2,64,128]{3,2,1,0:T(8,128)S(1)}, f32[2,64,128]{2,1,0:T(8,128)S(1)}, f32[2,64,128]{2,1,0:T(8,128)S(1)}, f32[2,2,64,128]{3,2,1,0:T(8,128)S(1)}) custom-call(s32[1]{0:T(128)} %bitcast.me_ref, f32[1024,128]{1,0:T(8,128)} %bitcast.25, f32[2,12,128,128]{3,2,1,0:T(8,128)} %gates.13), custom_call_target="tpu_custom_call" | custom-call | tf_op jit(solution)/shard_map/first_kernel/pallas_call | solution.py:332
  3.7 0.7 %collective-permute-start = (f32[2,2,64,128]{3,2,1,0:T(8,128)S(1)}, f32[2,2,64,128]{3,2,1,0:T(8,128)S(1)}, u32[]{:S(2)}, u32[]{:S(2)}) collective-permute-start(f32[2,2,64,128]{3,2,1,0:T(8,128)S(1)} %get-tuple-element.25), channel_id=1, source_target_pairs={{0,1},{1,0},{2,3},{3,2},{4,5},{5,4},{6,7},{7,6},{8,9},{9,8},{10,11... | collective-permute-start | bytes 393224 | tf_op jit(solution)/shard_map/ppermute | solution.py:352
  4.5 1.3 %collective-permute-start.1 = (f32[2,2,64,128]{3,2,1,0:T(8,128)S(1)}, f32[2,2,64,128]{3,2,1,0:T(8,128)S(1)}, u32[]{:S(2)}, u32[]{:S(2)}) collective-permute-start(f32[2,2,64,128]{3,2,1,0:T(8,128)S(1)} %get-tuple-element.27), channel_id=1, source_target_pairs={{0,2},{1,3},{2,0},{3,1},{4,6},{5,7},{6,4},{7,5},{8,10},{9,11},{10,... | collective-permute-start | bytes 393224 | tf_op jit(solution)/shard_map/ppermute | solution.py:352
  5.7 1.3 %collective-permute-start.2 = (f32[2,2,64,128]{3,2,1,0:T(8,128)S(1)}, f32[2,2,64,128]{3,2,1,0:T(8,128)S(1)}, u32[]{:S(2)}, u32[]{:S(2)}) collective-permute-start(f32[2,2,64,128]{3,2,1,0:T(8,128)S(1)} %get-tuple-element.28), channel_id=1, source_target_pairs={{0,4},{1,5},{2,6},{3,7},{4,0},{5,1},{6,2},{7,3},{8,12},{9,13},{10,... | collective-permute-start | bytes 393224 | tf_op jit(solution)/shard_map/ppermute | solution.py:352
  7.0 0.0 collective-permute-done.recv
  7.0 1.5 %before_lower.1 = (f32[2,2,64,128]{3,2,1,0:T(8,128)S(1)}, f32[2,2,64,128]{3,2,1,0:T(8,128)S(1)}) custom-call(f32[2,64,128]{2,1,0:T(8,128)S(1)} %get-tuple-element.23.own0, f32[2,64,128]{2,1,0:T(8,128)S(1)} %get-tuple-element.24.own3, f32[2,2,64,128]{3,2,1,0:T(8,128)S(1)} %collective-permute-done.recv, f32[2,12,128,128]{3,2,1,0:T(8,128)S(1)} %copy-done), custom_call_target="tpu_custom_call" | custom-call | flops 2000000000 | bytes 262144 | tf_op jit(solution)/shard_map/before_lower/pallas_call | solution.py:332
  8.5 0.7 %collective-permute-start.3 = (f32[2,2,64,128]{3,2,1,0:T(8,128)S(1)}, f32[2,2,64,128]{3,2,1,0:T(8,128)S(1)}, u32[]{:S(2)}, u32[]{:S(2)}) collective-permute-start(f32[2,2,64,128]{3,2,1,0:T(8,128)S(1)} %get-tuple-element.30), channel_id=1, source_target_pairs={{0,6},{1,7},{2,4},{3,5},{4,2},{5,3},{6,0},{7,1},{8,14},{9,15},{10,... | collective-permute-start | bytes 393224 | tf_op jit(solution)/shard_map/ppermute | solution.py:352
  9.3 0.3 collective-permute-done.1.r1
  9.6 0.9 %collective-permute-done.2.r2 = f32[2,2,64,128]{3,2,1,0:T(8,128)S(1)} collective-permute-done((f32[2,2,64,128]{3,2,1,0:T(8,128)S(1)}, f32[2,2,64,128]{3,2,1,0:T(8,128)S(1)}, u32[]{:S(2)}, u32[]{:S(2)}) %collective-permute-start.2) | collective-permute-done | bytes 131104 | tf_op jit(solution)/shard_map/ppermute | solution.py:352
  10.5 1.5 %after_lower.1 = (f32[2,2,64,128]{3,2,1,0:T(8,128)S(1)}, f32[2,64,128]{2,1,0:T(8,128)S(1)}, f32[2,64,128]{2,1,0:T(8,128)S(1)}) custom-call(f32[2,2,64,128]{3,2,1,0:T(8,128)S(1)} %collective-permute-done.1.r1, f32[2,2,64,128]{3,2,1,0:T(8,128)S(1)} %collective-permute-done.2.r2, f32[2,12,128,128]{3,2,1,0:T(8,128)S(1)} %copy-done), custom_call_target="tpu_custom_call" | custom-call | flops 2000000000 | bytes 262144 | tf_op jit(solution)/shard_map/after_lower/pallas_call | solution.py:332
  12.0 1.2 %collective-permute-start.4 = (f32[2,64,128]{2,1,0:T(8,128)S(1)}, f32[2,64,128]{2,1,0:T(8,128)S(1)}, u32[]{:S(2)}, u32[]{:S(2)}) collective-permute-start(f32[2,64,128]{2,1,0:T(8,128)S(1)} %get-tuple-element.31), channel_id=1, source_target_pairs={{0,1},{1,0},{2,3},{3,2},{4,5},{5,4},{6,7},{7,6},{8,9},{9,8},{10,11... | collective-permute-start | bytes 196616 | tf_op jit(solution)/shard_map/ppermute | solution.py:352
  13.2 0.1 collective-permute-start.5
  13.3 0.8 %collective-permute-done.4.post1 = f32[2,64,128]{2,1,0:T(8,128)S(1)} collective-permute-done((f32[2,64,128]{2,1,0:T(8,128)S(1)}, f32[2,64,128]{2,1,0:T(8,128)S(1)}, u32[]{:S(2)}, u32[]{:S(2)}) %collective-permute-start.4) | collective-permute-done | bytes 65568 | tf_op jit(solution)/shard_map/ppermute | solution.py:352
  14.1 0.4 %collective-permute-done.5.post2 = f32[2,64,128]{2,1,0:T(8,128)S(1)} collective-permute-done((f32[2,64,128]{2,1,0:T(8,128)S(1)}, f32[2,64,128]{2,1,0:T(8,128)S(1)}, u32[]{:S(2)}, u32[]{:S(2)}) %collective-permute-start.5) | collective-permute-done | bytes 65568 | tf_op jit(solution)/shard_map/ppermute | solution.py:352
  14.5 0.0 collective-permute-done.3.r3
  14.5 0.9 %second_kernel.1 = (f32[3,2,2,32,128]{4,3,2,1,0:T(8,128)S(1)}, f32[8,2,32,128]{3,2,1,0:T(8,128)S(1)}, f32[2,32,128]{2,1,0:T(8,128)S(1)}, f32[2,32,128]{2,1,0:T(8,128)S(1)}) custom-call(s32[1]{0:T(128)} %bitcast.me_ref, f32[2,2,64,128]{3,2,1,0:T(8,128)S(1)} %get-tuple-element.26.p0, f32[2,2,64,128]{3,2,1,0:T(8,128)S(1)} %get-tuple-element.29.near, ...), custom_call_target="tpu_custom_call" | custom-call | tf_op jit(solution)/shard_map/second_kernel/pallas_call | solution.py:332
  15.3 1.0 %collective-permute-start.6 = (f32[8,2,32,128]{3,2,1,0:T(8,128)S(1)}, f32[8,2,32,128]{3,2,1,0:T(8,128)S(1)}, u32[]{:S(2)}, u32[]{:S(2)}) collective-permute-start(f32[8,2,32,128]{3,2,1,0:T(8,128)S(1)} %get-tuple-element.34), channel_id=1, source_target_pairs={{0,1},{1,0},{2,3},{3,2},{4,5},{5,4},{6,7},{7,6},{8,9},{9,8},{10,11... | collective-permute-start | bytes 786440 | tf_op jit(solution)/shard_map/ppermute | solution.py:352
  16.4 1.1 %collective-permute-done.6 = f32[8,2,32,128]{3,2,1,0:T(8,128)S(1)} collective-permute-done((f32[8,2,32,128]{3,2,1,0:T(8,128)S(1)}, f32[8,2,32,128]{3,2,1,0:T(8,128)S(1)}, u32[]{:S(2)}, u32[]{:S(2)}) %collective-permute-start.6) | collective-permute-done | bytes 262176 | tf_op jit(solution)/shard_map/ppermute | solution.py:352
  17.5 0.1 collective-permute-start.7
  17.6 2.2 %collective-permute-start.8 = (f32[2,2,2,32,128]{4,3,2,0,1:T(8,128)S(1)}, f32[2,2,2,32,128]{4,3,2,0,1:T(8,128)S(1)}, u32[]{:S(2)}, u32[]{:S(2)}) collective-permute-start(f32[2,2,2,32,128]{4,3,2,0,1:T(8,128)S(1)} %pad_maximum_fusion.1), channel_id=1, source_target_pairs={{0,4},{1,7},{2,6},{3,5},{4,0},{5,3},{6,2},{7,1},{8,12},{9,15},{10,... | collective-permute-start | bytes 393224 | tf_op jit(solution)/shard_map/ppermute | solution.py:352
  19.9 0.4 %collective-permute-start.9 = (f32[2,2,32,128]{3,2,1,0:T(8,128)S(1)}, f32[2,2,32,128]{3,2,1,0:T(8,128)S(1)}, u32[]{:S(2)}, u32[]{:S(2)}) collective-permute-start(f32[2,2,32,128]{3,2,1,0:T(8,128)S(1)} %pad_maximum_fusion.2), channel_id=1, source_target_pairs={{0,2},{1,3},{2,0},{3,1},{4,6},{5,7},{6,4},{7,5},{8,10},{9,11},{10,... | collective-permute-start | bytes 196616 | tf_op jit(solution)/shard_map/ppermute | solution.py:352
  20.2 0.7 %before_kernel.1 = (f32[2,2,32,128]{3,2,1,0:T(8,128)S(1)}, f32[2,2,32,128]{3,2,1,0:T(8,128)S(1)}) custom-call(f32[2,2,32,128]{3,2,1,0:T(8,128)S(1)} %get-tuple-element.46.own, f32[2,2,32,128]{3,2,1,0:T(8,128)S(1)} %get-tuple-element.41.recv, f32[2,12,128,128]{3,2,1,0:T(8,128)S(1)} %copy-done), custom_call_target="tpu_custom_call" | custom-call | flops 1000000000 | bytes 262144 | tf_op jit(solution)/shard_map/before_kernel/pallas_call | solution.py:332
  20.9 2.3 %collective-permute-start.11 = (f32[2,2,32,128]{3,2,1,0:T(8,128)S(1)}, f32[2,2,32,128]{3,2,1,0:T(8,128)S(1)}, u32[]{:S(2)}, u32[]{:S(2)}) collective-permute-start(f32[2,2,32,128]{3,2,1,0:T(8,128)S(1)} %get-tuple-element.39), channel_id=1, source_target_pairs={{0,12},{1,15},{2,14},{3,13},{4,8},{5,11},{6,10},{7,9},{8,4},{9,7},... | collective-permute-start | bytes 196616 | tf_op jit(solution)/shard_map/ppermute | solution.py:352
  23.2 0.4 %collective-permute-start.12 = (f32[2,2,32,128]{3,2,1,0:T(8,128)S(1)}, f32[2,2,32,128]{3,2,1,0:T(8,128)S(1)}, u32[]{:S(2)}, u32[]{:S(2)}) collective-permute-start(f32[2,2,32,128]{3,2,1,0:T(8,128)S(1)} %get-tuple-element.40), channel_id=1, source_target_pairs={{0,13},{1,14},{2,15},{3,12},{4,9},{5,10},{6,11},{7,8},{8,5},{9,6},... | collective-permute-start | bytes 196616 | tf_op jit(solution)/shard_map/ppermute | solution.py:352
  23.6 1.2 %collective-permute-done.7 = f32[2,2,2,32,128]{4,3,2,0,1:T(8,128)S(1)} collective-permute-done((f32[2,2,2,32,128]{4,3,2,0,1:T(8,128)S(1)}, f32[2,2,2,32,128]{4,3,2,0,1:T(8,128)S(1)}, u32[]{:S(2)}, u32[]{:S(2)}) %collective-permute-start.7) | collective-permute-done | bytes 131104 | tf_op jit(solution)/shard_map/ppermute | solution.py:352
  24.8 1.5 %collective-permute-done.8 = f32[2,2,2,32,128]{4,3,2,0,1:T(8,128)S(1)} collective-permute-done((f32[2,2,2,32,128]{4,3,2,0,1:T(8,128)S(1)}, f32[2,2,2,32,128]{4,3,2,0,1:T(8,128)S(1)}, u32[]{:S(2)}, u32[]{:S(2)}) %collective-permute-start.8) | collective-permute-done | bytes 131104 | tf_op jit(solution)/shard_map/ppermute | solution.py:352
  26.4 0.0 collective-permute-done.9.y1
  26.4 0.9 %after_kernel.1 = (f32[8,2,32,128]{3,2,1,0:T(8,128)S(1)}, f32[4,2,32,128]{3,2,1,0:T(8,128)S(1)}) custom-call(f32[2,2,2,32,128]{4,3,2,1,0:T(8,128)S(1)} %copy.4.a0, f32[2,2,2,32,128]{4,3,2,1,0:T(8,128)S(1)} %copy.5.a1, f32[2,2,32,128]{3,2,1,0:T(8,128)S(1)} %collective-permute-done.9.y1, f32[2,32,128]{2,1,0:T(8,128)S(1)} %get-tuple-element.36.self0, ...), custom_call_target="tpu_custom_call" | custom-call | flops 2000000000 | bytes 262144 | tf_op jit(solution)/shard_map/after_kernel/pallas_call | solution.py:332
  27.3 0.6 %collective-permute-start.10 = (f32[4,2,32,128]{3,2,1,0:T(8,128)S(1)}, f32[4,2,32,128]{3,2,1,0:T(8,128)S(1)}, u32[]{:S(2)}, u32[]{:S(2)}) collective-permute-start(f32[4,2,32,128]{3,2,1,0:T(8,128)S(1)} %get-tuple-element.38), channel_id=1, source_target_pairs={{0,1},{1,0},{2,3},{3,2},{4,5},{5,4},{6,7},{7,6},{8,9},{9,8},{10,11... | collective-permute-start | bytes 393224 | tf_op jit(solution)/shard_map/ppermute | solution.py:352
  27.9 3.6 %collective-permute-done.11.mine = f32[2,2,32,128]{3,2,1,0:T(8,128)S(1)} collective-permute-done((f32[2,2,32,128]{3,2,1,0:T(8,128)S(1)}, f32[2,2,32,128]{3,2,1,0:T(8,128)S(1)}, u32[]{:S(2)}, u32[]{:S(2)}) %collective-permute-start.11) | collective-permute-done | bytes 65568 | tf_op jit(solution)/shard_map/ppermute | solution.py:352
  31.5 0.9 %collective-permute-done.12.late = f32[2,2,32,128]{3,2,1,0:T(8,128)S(1)} collective-permute-done((f32[2,2,32,128]{3,2,1,0:T(8,128)S(1)}, f32[2,2,32,128]{3,2,1,0:T(8,128)S(1)}, u32[]{:S(2)}, u32[]{:S(2)}) %collective-permute-start.12) | collective-permute-done | bytes 65568 | tf_op jit(solution)/shard_map/ppermute | solution.py:352
  32.5 1.6 %third_kernel.1 = f32[1024,128]{1,0:T(8,128)} custom-call(s32[1]{0:T(128)} %bitcast.me_ref, f32[8,2,32,128]{3,2,1,0:T(8,128)S(1)} %get-tuple-element.37.keep, f32[4,2,32,128]{3,2,1,0:T(8,128)S(1)} %collective-permute-done.10.early, f32[4,2,32,128]{3,2,1,0:T(8,128)S(1)} %join_kernel.1.far, f32[2,12,128,128]{3,2,1,0:T(8,128)S(1)} %copy-done), custom_call_target="tpu_custom_call" | custom-call | tf_op jit(solution)/shard_map/third_kernel/pallas_call | solution.py:332
  (12 shorter events, 0.1 us)
Async XLA Ops:
  0.0 7.0 %copy-start = (f32[2,12,128,128]{3,2,1,0:T(8,128)S(1)}, f32[2,12,128,128]{3,2,1,0:T(8,128)}, u32[]{:S(2)}) copy-start(f32[2,12,128,128]{3,2,1,0:T(8,128)} %gates.13) | copy-start | bytes 4718596
  3.7 3.3 %collective-permute-start = (f32[2,2,64,128]{3,2,1,0:T(8,128)S(1)}, f32[2,2,64,128]{3,2,1,0:T(8,128)S(1)}, u32[]{:S(2)}, u32[]{:S(2)}) collective-permute-start(f32[2,2,64,128]{3,2,1,0:T(8,128)S(1)} %get-tuple-element.25), channel_id=1, source_target_pairs={{0,1},{1,0},{2,3},{3,2},{4,5},{5,4},{6,7},{7,6},{8,9},{9,8},{10,11... | collective-permute-start | bytes 393224 | tf_op jit(solution)/shard_map/ppermute | solution.py:352
  4.5 5.1 %collective-permute-start.1 = (f32[2,2,64,128]{3,2,1,0:T(8,128)S(1)}, f32[2,2,64,128]{3,2,1,0:T(8,128)S(1)}, u32[]{:S(2)}, u32[]{:S(2)}) collective-permute-start(f32[2,2,64,128]{3,2,1,0:T(8,128)S(1)} %get-tuple-element.27), channel_id=1, source_target_pairs={{0,2},{1,3},{2,0},{3,1},{4,6},{5,7},{6,4},{7,5},{8,10},{9,11},{10,... | collective-permute-start | bytes 393224 | tf_op jit(solution)/shard_map/ppermute | solution.py:352
  5.7 4.7 %collective-permute-start.2 = (f32[2,2,64,128]{3,2,1,0:T(8,128)S(1)}, f32[2,2,64,128]{3,2,1,0:T(8,128)S(1)}, u32[]{:S(2)}, u32[]{:S(2)}) collective-permute-start(f32[2,2,64,128]{3,2,1,0:T(8,128)S(1)} %get-tuple-element.28), channel_id=1, source_target_pairs={{0,4},{1,5},{2,6},{3,7},{4,0},{5,1},{6,2},{7,3},{8,12},{9,13},{10,... | collective-permute-start | bytes 393224 | tf_op jit(solution)/shard_map/ppermute | solution.py:352
  8.5 5.9 %collective-permute-start.3 = (f32[2,2,64,128]{3,2,1,0:T(8,128)S(1)}, f32[2,2,64,128]{3,2,1,0:T(8,128)S(1)}, u32[]{:S(2)}, u32[]{:S(2)}) collective-permute-start(f32[2,2,64,128]{3,2,1,0:T(8,128)S(1)} %get-tuple-element.30), channel_id=1, source_target_pairs={{0,6},{1,7},{2,4},{3,5},{4,2},{5,3},{6,0},{7,1},{8,14},{9,15},{10,... | collective-permute-start | bytes 393224 | tf_op jit(solution)/shard_map/ppermute | solution.py:352
  12.0 2.1 %collective-permute-start.4 = (f32[2,64,128]{2,1,0:T(8,128)S(1)}, f32[2,64,128]{2,1,0:T(8,128)S(1)}, u32[]{:S(2)}, u32[]{:S(2)}) collective-permute-start(f32[2,64,128]{2,1,0:T(8,128)S(1)} %get-tuple-element.31), channel_id=1, source_target_pairs={{0,1},{1,0},{2,3},{3,2},{4,5},{5,4},{6,7},{7,6},{8,9},{9,8},{10,11... | collective-permute-start | bytes 196616 | tf_op jit(solution)/shard_map/ppermute | solution.py:352
  13.2 1.3 %collective-permute-start.5 = (f32[2,64,128]{2,1,0:T(8,128)S(1)}, f32[2,64,128]{2,1,0:T(8,128)S(1)}, u32[]{:S(2)}, u32[]{:S(2)}) collective-permute-start(f32[2,64,128]{2,1,0:T(8,128)S(1)} %get-tuple-element.32), channel_id=1, source_target_pairs={{0,1},{1,0},{2,3},{3,2},{4,5},{5,4},{6,7},{7,6},{8,9},{9,8},{10,11... | collective-permute-start | bytes 196616 | tf_op jit(solution)/shard_map/ppermute | solution.py:352
  15.3 2.2 %collective-permute-start.6 = (f32[8,2,32,128]{3,2,1,0:T(8,128)S(1)}, f32[8,2,32,128]{3,2,1,0:T(8,128)S(1)}, u32[]{:S(2)}, u32[]{:S(2)}) collective-permute-start(f32[8,2,32,128]{3,2,1,0:T(8,128)S(1)} %get-tuple-element.34), channel_id=1, source_target_pairs={{0,1},{1,0},{2,3},{3,2},{4,5},{5,4},{6,7},{7,6},{8,9},{9,8},{10,11... | collective-permute-start | bytes 786440 | tf_op jit(solution)/shard_map/ppermute | solution.py:352
  17.5 7.3 %collective-permute-start.7 = (f32[2,2,2,32,128]{4,3,2,0,1:T(8,128)S(1)}, f32[2,2,2,32,128]{4,3,2,0,1:T(8,128)S(1)}, u32[]{:S(2)}, u32[]{:S(2)}) collective-permute-start(f32[2,2,2,32,128]{4,3,2,0,1:T(8,128)S(1)} %pad_maximum_fusion), channel_id=1, source_target_pairs={{0,8},{1,11},{2,10},{3,9},{4,12},{5,15},{6,14},{7,13},{8,0},{9,3},... | collective-permute-start | bytes 393224 | tf_op jit(solution)/shard_map/ppermute | solution.py:352
  17.6 8.7 %collective-permute-start.8 = (f32[2,2,2,32,128]{4,3,2,0,1:T(8,128)S(1)}, f32[2,2,2,32,128]{4,3,2,0,1:T(8,128)S(1)}, u32[]{:S(2)}, u32[]{:S(2)}) collective-permute-start(f32[2,2,2,32,128]{4,3,2,0,1:T(8,128)S(1)} %pad_maximum_fusion.1), channel_id=1, source_target_pairs={{0,4},{1,7},{2,6},{3,5},{4,0},{5,3},{6,2},{7,1},{8,12},{9,15},{10,... | collective-permute-start | bytes 393224 | tf_op jit(solution)/shard_map/ppermute | solution.py:352
  19.9 6.5 %collective-permute-start.9 = (f32[2,2,32,128]{3,2,1,0:T(8,128)S(1)}, f32[2,2,32,128]{3,2,1,0:T(8,128)S(1)}, u32[]{:S(2)}, u32[]{:S(2)}) collective-permute-start(f32[2,2,32,128]{3,2,1,0:T(8,128)S(1)} %pad_maximum_fusion.2), channel_id=1, source_target_pairs={{0,2},{1,3},{2,0},{3,1},{4,6},{5,7},{6,4},{7,5},{8,10},{9,11},{10,... | collective-permute-start | bytes 196616 | tf_op jit(solution)/shard_map/ppermute | solution.py:352
  20.9 10.6 %collective-permute-start.11 = (f32[2,2,32,128]{3,2,1,0:T(8,128)S(1)}, f32[2,2,32,128]{3,2,1,0:T(8,128)S(1)}, u32[]{:S(2)}, u32[]{:S(2)}) collective-permute-start(f32[2,2,32,128]{3,2,1,0:T(8,128)S(1)} %get-tuple-element.39), channel_id=1, source_target_pairs={{0,12},{1,15},{2,14},{3,13},{4,8},{5,11},{6,10},{7,9},{8,4},{9,7},... | collective-permute-start | bytes 196616 | tf_op jit(solution)/shard_map/ppermute | solution.py:352
  23.2 9.2 %collective-permute-start.12 = (f32[2,2,32,128]{3,2,1,0:T(8,128)S(1)}, f32[2,2,32,128]{3,2,1,0:T(8,128)S(1)}, u32[]{:S(2)}, u32[]{:S(2)}) collective-permute-start(f32[2,2,32,128]{3,2,1,0:T(8,128)S(1)} %get-tuple-element.40), channel_id=1, source_target_pairs={{0,13},{1,14},{2,15},{3,12},{4,9},{5,10},{6,11},{7,8},{8,5},{9,6},... | collective-permute-start | bytes 196616 | tf_op jit(solution)/shard_map/ppermute | solution.py:352
  27.3 5.2 %collective-permute-start.10 = (f32[4,2,32,128]{3,2,1,0:T(8,128)S(1)}, f32[4,2,32,128]{3,2,1,0:T(8,128)S(1)}, u32[]{:S(2)}, u32[]{:S(2)}) collective-permute-start(f32[4,2,32,128]{3,2,1,0:T(8,128)S(1)} %get-tuple-element.38), channel_id=1, source_target_pairs={{0,1},{1,0},{2,3},{3,2},{4,5},{5,4},{6,7},{7,6},{8,9},{9,8},{10,11... | collective-permute-start | bytes 393224 | tf_op jit(solution)/shard_map/ppermute | solution.py:352

commit v5 on v4

--- a/solution.py
+++ b/solution.py
@@ -172,12 +172,25 @@
         return self.mh[k], self.ml[k]
 
 
+class Given:
+    def __init__(self, mh, ml, indices):
+        self.mh, self.ml, self.indices = mh, ml, indices
+
+    def __getitem__(self, g):
+        k = self.indices.index(g)
+        return self.mh[k], self.ml[k]
+
+
+def prepare_all(source, indices, mh, ml):
+    for k, g in enumerate(indices):
+        prepare(source.at[:, g], g % 4 == 1, mh.at[k], ml.at[k])
+
+
 class Ready:
     def __init__(self, source, scratch, indices):
         self.mh, self.ml = scratch
         self.indices = indices
-        for k, g in enumerate(indices):
-            prepare(source.at[:, g], g % 4 == 1, self.mh.at[k], self.ml.at[k])
+        prepare_all(source, indices, self.mh, self.ml)
 
     def __getitem__(self, g):
         k = self.indices.index(g)
@@ -228,13 +241,14 @@
     lower_blocks(s, g, (own0, recv.at[0], own3, recv.at[1]), (*split(p0), *split(p3)))
 
 
-def after_lower(indices, r1, r2, gates, keep, send1, send2, s, mh, ml):
+def after_lower(indices, r1, r2, gates, keep, send1, send2, wh, wl, s, mh, ml):
+    prepare_all(gates, (6, 7), wh, wl)
     g = Ready(gates, (mh, ml), indices)
     lower_blocks(s, g, (*split(r1), *split(r2)), (keep.at[0], send1, keep.at[1], send2))
 
 
-def second_kernel(indices, me_ref, p0, near, r3, post1, post2, gates, own, give, y1, self0, s, mh, ml):
-    g = Ready(gates, (mh, ml), indices)
+def second_kernel(indices, me_ref, p0, near, r3, post1, post2, wh, wl, own, give, y1, self0, s, mh, ml):
+    g = Given(wh, wl, indices)
     me = me_ref[0]
     low3, core = me & 7, me & 1
     blocks = (*split(p0), near.at[0], post1, near.at[1], post2, *split(r3))
@@ -275,7 +289,8 @@
     gate_nine(s, g, (*split(own), *split(recv)), [out.at[src] for src in range(2) for out in (out0, out1)])
 
 
-def after_kernel(indices, a0, a1, y1, self0, other, gates, keep, send, s, mh, ml):
+def after_kernel(indices, a0, a1, y1, self0, other, gates, keep, send, wh, wl, s, mh, ml):
+    prepare_all(gates, (10, 11), wh, wl)
     g = Ready(gates, (mh, ml), indices)
     blocks = [a.at[f, src] for f in range(2) for a in (a0, a1) for src in range(2)]
     blocks = blocks[:4] + [y1.at[0], y1.at[1], self0, other] + blocks[4:]
@@ -288,8 +303,8 @@
             out[n, c] = block[c]
 
 
-def third_kernel(indices, me_ref, keep, early, far, gates, out, s, mh, ml, y, ysems):
-    g = Ready(gates, (mh, ml), indices)
+def third_kernel(indices, me_ref, keep, early, far, wh, wl, out, s, mh, ml, y, ysems):
+    g = Given(wh, wl, indices)
     me = me_ref[0]
     core = me & 1
 
@@ -374,7 +389,8 @@
     r1, r2 = flipped(q1, 2), flipped(q2, 4)
     p0, p3 = call(before_lower, (4, 5, 8), [two, two], 4 * eighth, [own0, own3, recv, gates], [VMEM] * 4)
     r3 = flipped(p3, 6)
-    near, send1, send2 = call(after_lower, (4, 5, 8), [two, one, one], 4 * eighth, [r1, r2, gates], [VMEM] * 3)
+    weights = [jax.ShapeDtypeStruct((2, PAIR, PAIR), BF16)] * 2
+    near, send1, send2, *w = call(after_lower, (4, 5, 8), [two, one, one, *weights], 4 * eighth, [r1, r2, gates], [VMEM] * 3)
     post1, post2 = flipped(send1, 1), flipped(send2, 1)
     block = (2, part16, LANES)
     own, give, y1, self0 = call(
@@ -382,8 +398,8 @@
         (6, 7),
         [shape(3, 2, *block), shape(8, *block), shape(*block), shape(*block)],
         rows,
-        [me, p0, near, r3, post1, post2, gates],
-        [SMEM] + [VMEM] * 6,
+        [me, p0, near, r3, post1, post2, *w],
+        [SMEM] + [VMEM] * 7,
     )
     recv = flipped(give, 1)
     ready = call(
@@ -393,10 +409,10 @@
     a0, a1 = [flipped(payload, 2 * base, 2) for base, payload in zip(PORTS, payloads)]
     mine, late = [flipped(payload, 2 * PORTS[2] + f, 2) for f, payload in enumerate(ready)]
     y1 = flipped(jnp.stack([y1, recv[6]]), 2)
-    keep, send = call(
+    keep, send, *w = call(
         after_kernel,
         (9,),
-        [shape(8, *block), shape(4, *block)],
+        [shape(8, *block), shape(4, *block), *weights],
         12 * part16,
         [a0, a1, y1, self0, recv[7], gates],
         [VMEM] * 6,
@@ -408,8 +424,8 @@
         (10, 11),
         [shape(2 * rows, LANES)],
         rows,
-        [me, keep, early, far, gates],
-        [SMEM] + [VMEM] * 4,
+        [me, keep, early, far, *w],
+        [SMEM] + [VMEM] * 5,
         interleaved,
         [HBM],
     )[0]

time: 34.7 us -> 34.7 us (level)
  transfers between devices with their start and end apart: 13 -> 13, of which waited for: 9 -> 9; matrix products, arithmetic and copies ran while one was open for 0% -> 0% of each run, Pallas kernels for 13% -> 14%
where the time goes in v5:
time: 34.7 us; the launch traced here: 34 us
  starting transfers between devices  12.4 us (36%)
  Pallas kernels  10.8 us (31%)
  waiting for transfers between devices  10.6 us (31%)
    ppermute x13, starting transfers between devices, flipped(): return lax.ppermute(block, 'node', route)  12.4 us
    pallas_call x8, Pallas kernels, call(): pl.pallas_call(functools.partial(kernel, indices), out_shape=outs, in_spe...  10.8 us
    ppermute x13, waiting for transfers between devices, flipped(): return lax.ppermute(block, 'node', route)  10.6 us
  transfers between devices with their start and end apart: 13, of which 9 were waited for; matrix products, arithmetic and copies ran while one was open for 0% of the time, Pallas kernels for 14%

profile of v5, /device:TPU:19, one launch (start us, length us, event | category | flops | bytes accessed | tf_op | source)
XLA Modules:
  0.0 34.0 jit_solution(1635717716208769414)
XLA Ops:
  0.0 3.7 %first_kernel.1 = (f32[2,2,64,128]{3,2,1,0:T(8,128)S(1)}, f32[2,2,64,128]{3,2,1,0:T(8,128)S(1)}, f32[2,64,128]{2,1,0:T(8,128)S(1)}, f32[2,64,128]{2,1,0:T(8,128)S(1)}, f32[2,2,64,128]{3,2,1,0:T(8,128)S(1)}) custom-call(s32[1]{0:T(128)} %bitcast.me_ref, f32[1024,128]{1,0:T(8,128)} %bitcast.25, f32[2,12,128,128]{3,2,1,0:T(8,128)} %gates.9), custom_call_target="tpu_custom_call" | custom-call | tf_op jit(solution)/shard_map/first_kernel/pallas_call | solution.py:347
  3.7 0.7 %collective-permute-start = (f32[2,2,64,128]{3,2,1,0:T(8,128)S(1)}, f32[2,2,64,128]{3,2,1,0:T(8,128)S(1)}, u32[]{:S(2)}, u32[]{:S(2)}) collective-permute-start(f32[2,2,64,128]{3,2,1,0:T(8,128)S(1)} %get-tuple-element.29), channel_id=1, source_target_pairs={{0,1},{1,0},{2,3},{3,2},{4,5},{5,4},{6,7},{7,6},{8,9},{9,8},{10,11... | collective-permute-start | bytes 393224 | tf_op jit(solution)/shard_map/ppermute | solution.py:367
  4.5 1.3 %collective-permute-start.1 = (f32[2,2,64,128]{3,2,1,0:T(8,128)S(1)}, f32[2,2,64,128]{3,2,1,0:T(8,128)S(1)}, u32[]{:S(2)}, u32[]{:S(2)}) collective-permute-start(f32[2,2,64,128]{3,2,1,0:T(8,128)S(1)} %get-tuple-element.31), channel_id=1, source_target_pairs={{0,2},{1,3},{2,0},{3,1},{4,6},{5,7},{6,4},{7,5},{8,10},{9,11},{10,... | collective-permute-start | bytes 393224 | tf_op jit(solution)/shard_map/ppermute | solution.py:367
  5.7 1.3 %collective-permute-start.2 = (f32[2,2,64,128]{3,2,1,0:T(8,128)S(1)}, f32[2,2,64,128]{3,2,1,0:T(8,128)S(1)}, u32[]{:S(2)}, u32[]{:S(2)}) collective-permute-start(f32[2,2,64,128]{3,2,1,0:T(8,128)S(1)} %get-tuple-element.32), channel_id=1, source_target_pairs={{0,4},{1,5},{2,6},{3,7},{4,0},{5,1},{6,2},{7,3},{8,12},{9,13},{10,... | collective-permute-start | bytes 393224 | tf_op jit(solution)/shard_map/ppermute | solution.py:367
  7.0 0.0 collective-permute-done.recv
  7.0 1.5 %before_lower.1 = (f32[2,2,64,128]{3,2,1,0:T(8,128)S(1)}, f32[2,2,64,128]{3,2,1,0:T(8,128)S(1)}) custom-call(f32[2,64,128]{2,1,0:T(8,128)S(1)} %get-tuple-element.27.own0, f32[2,64,128]{2,1,0:T(8,128)S(1)} %get-tuple-element.28.own3, f32[2,2,64,128]{3,2,1,0:T(8,128)S(1)} %collective-permute-done.recv, f32[2,12,128,128]{3,2,1,0:T(8,128)S(1)} %copy-done), custom_call_target="tpu_custom_call" | custom-call | flops 2000000000 | bytes 262144 | tf_op jit(solution)/shard_map/before_lower/pallas_call | solution.py:347
  8.5 0.7 %collective-permute-start.3 = (f32[2,2,64,128]{3,2,1,0:T(8,128)S(1)}, f32[2,2,64,128]{3,2,1,0:T(8,128)S(1)}, u32[]{:S(2)}, u32[]{:S(2)}) collective-permute-start(f32[2,2,64,128]{3,2,1,0:T(8,128)S(1)} %get-tuple-element.34), channel_id=1, source_target_pairs={{0,6},{1,7},{2,4},{3,5},{4,2},{5,3},{6,0},{7,1},{8,14},{9,15},{10,... | collective-permute-start | bytes 393224 | tf_op jit(solution)/shard_map/ppermute | solution.py:367
  9.3 0.3 collective-permute-done.1.r1
  9.6 0.9 %collective-permute-done.2.r2 = f32[2,2,64,128]{3,2,1,0:T(8,128)S(1)} collective-permute-done((f32[2,2,64,128]{3,2,1,0:T(8,128)S(1)}, f32[2,2,64,128]{3,2,1,0:T(8,128)S(1)}, u32[]{:S(2)}, u32[]{:S(2)}) %collective-permute-start.2) | collective-permute-done | bytes 131104 | tf_op jit(solution)/shard_map/ppermute | solution.py:367
  10.5 1.6 %after_lower.1 = (f32[2,2,64,128]{3,2,1,0:T(8,128)S(1)}, f32[2,64,128]{2,1,0:T(8,128)S(1)}, f32[2,64,128]{2,1,0:T(8,128)S(1)}, bf16[2,256,256]{2,1,0:T(8,128)(2,1)S(1)}, bf16[2,256,256]{2,1,0:T(8,128)(2,1)S(1)}) custom-call(f32[2,2,64,128]{3,2,1,0:T(8,128)S(1)} %collective-permute-done.1.r1, f32[2,2,64,128]{3,2,1,0:T(8,128)S(1)} %collective-permute-done.2.r2, ...), custom_call_target="tpu_custom_call" | custom-call | flops 2000000000 | bytes 262144 | tf_op jit(solution)/shard_map/after_lower/pallas_call | solution.py:347
  12.0 1.2 %collective-permute-start.4 = (f32[2,64,128]{2,1,0:T(8,128)S(1)}, f32[2,64,128]{2,1,0:T(8,128)S(1)}, u32[]{:S(2)}, u32[]{:S(2)}) collective-permute-start(f32[2,64,128]{2,1,0:T(8,128)S(1)} %get-tuple-element.35), channel_id=1, source_target_pairs={{0,1},{1,0},{2,3},{3,2},{4,5},{5,4},{6,7},{7,6},{8,9},{9,8},{10,11... | collective-permute-start | bytes 196616 | tf_op jit(solution)/shard_map/ppermute | solution.py:367
  13.3 0.1 collective-permute-start.5
  13.4 0.8 %collective-permute-done.4.post1 = f32[2,64,128]{2,1,0:T(8,128)S(1)} collective-permute-done((f32[2,64,128]{2,1,0:T(8,128)S(1)}, f32[2,64,128]{2,1,0:T(8,128)S(1)}, u32[]{:S(2)}, u32[]{:S(2)}) %collective-permute-start.4) | collective-permute-done | bytes 65568 | tf_op jit(solution)/shard_map/ppermute | solution.py:367
  14.2 0.4 %collective-permute-done.5.post2 = f32[2,64,128]{2,1,0:T(8,128)S(1)} collective-permute-done((f32[2,64,128]{2,1,0:T(8,128)S(1)}, f32[2,64,128]{2,1,0:T(8,128)S(1)}, u32[]{:S(2)}, u32[]{:S(2)}) %collective-permute-start.5) | collective-permute-done | bytes 65568 | tf_op jit(solution)/shard_map/ppermute | solution.py:367
  14.5 0.0 collective-permute-done.3.r3
  14.5 0.8 %second_kernel.1 = (f32[3,2,2,32,128]{4,3,2,1,0:T(8,128)S(1)}, f32[8,2,32,128]{3,2,1,0:T(8,128)S(1)}, f32[2,32,128]{2,1,0:T(8,128)S(1)}, f32[2,32,128]{2,1,0:T(8,128)S(1)}) custom-call(s32[1]{0:T(128)} %bitcast.me_ref, f32[2,2,64,128]{3,2,1,0:T(8,128)S(1)} %get-tuple-element.30.p0, f32[2,2,64,128]{3,2,1,0:T(8,128)S(1)} %get-tuple-element.33.near, ...), custom_call_target="tpu_custom_call" | custom-call | tf_op jit(solution)/shard_map/second_kernel/pallas_call | solution.py:347
  15.4 0.9 %collective-permute-start.6 = (f32[8,2,32,128]{3,2,1,0:T(8,128)S(1)}, f32[8,2,32,128]{3,2,1,0:T(8,128)S(1)}, u32[]{:S(2)}, u32[]{:S(2)}) collective-permute-start(f32[8,2,32,128]{3,2,1,0:T(8,128)S(1)} %get-tuple-element.40), channel_id=1, source_target_pairs={{0,1},{1,0},{2,3},{3,2},{4,5},{5,4},{6,7},{7,6},{8,9},{9,8},{10,11... | collective-permute-start | bytes 786440 | tf_op jit(solution)/shard_map/ppermute | solution.py:367
  16.3 1.1 %collective-permute-done.6 = f32[8,2,32,128]{3,2,1,0:T(8,128)S(1)} collective-permute-done((f32[8,2,32,128]{3,2,1,0:T(8,128)S(1)}, f32[8,2,32,128]{3,2,1,0:T(8,128)S(1)}, u32[]{:S(2)}, u32[]{:S(2)}) %collective-permute-start.6) | collective-permute-done | bytes 262176 | tf_op jit(solution)/shard_map/ppermute | solution.py:367
  17.5 0.1 collective-permute-start.7
  17.6 2.3 %collective-permute-start.8 = (f32[2,2,2,32,128]{4,3,2,0,1:T(8,128)S(1)}, f32[2,2,2,32,128]{4,3,2,0,1:T(8,128)S(1)}, u32[]{:S(2)}, u32[]{:S(2)}) collective-permute-start(f32[2,2,2,32,128]{4,3,2,0,1:T(8,128)S(1)} %pad_maximum_fusion.1), channel_id=1, source_target_pairs={{0,4},{1,7},{2,6},{3,5},{4,0},{5,3},{6,2},{7,1},{8,12},{9,15},{10,... | collective-permute-start | bytes 393224 | tf_op jit(solution)/shard_map/ppermute | solution.py:367
  19.9 0.3 collective-permute-start.9
  20.2 0.7 %before_kernel.1 = (f32[2,2,32,128]{3,2,1,0:T(8,128)S(1)}, f32[2,2,32,128]{3,2,1,0:T(8,128)S(1)}) custom-call(f32[2,2,32,128]{3,2,1,0:T(8,128)S(1)} %get-tuple-element.54.own, f32[2,2,32,128]{3,2,1,0:T(8,128)S(1)} %get-tuple-element.49.recv, f32[2,12,128,128]{3,2,1,0:T(8,128)S(1)} %copy-done), custom_call_target="tpu_custom_call" | custom-call | flops 1000000000 | bytes 262144 | tf_op jit(solution)/shard_map/before_kernel/pallas_call | solution.py:347
  20.9 2.3 %collective-permute-start.11 = (f32[2,2,32,128]{3,2,1,0:T(8,128)S(1)}, f32[2,2,32,128]{3,2,1,0:T(8,128)S(1)}, u32[]{:S(2)}, u32[]{:S(2)}) collective-permute-start(f32[2,2,32,128]{3,2,1,0:T(8,128)S(1)} %get-tuple-element.45), channel_id=1, source_target_pairs={{0,12},{1,15},{2,14},{3,13},{4,8},{5,11},{6,10},{7,9},{8,4},{9,7},... | collective-permute-start | bytes 196616 | tf_op jit(solution)/shard_map/ppermute | solution.py:367
  23.2 0.4 %collective-permute-start.12 = (f32[2,2,32,128]{3,2,1,0:T(8,128)S(1)}, f32[2,2,32,128]{3,2,1,0:T(8,128)S(1)}, u32[]{:S(2)}, u32[]{:S(2)}) collective-permute-start(f32[2,2,32,128]{3,2,1,0:T(8,128)S(1)} %get-tuple-element.46), channel_id=1, source_target_pairs={{0,13},{1,14},{2,15},{3,12},{4,9},{5,10},{6,11},{7,8},{8,5},{9,6},... | collective-permute-start | bytes 196616 | tf_op jit(solution)/shard_map/ppermute | solution.py:367
  23.6 1.1 %collective-permute-done.7 = f32[2,2,2,32,128]{4,3,2,0,1:T(8,128)S(1)} collective-permute-done((f32[2,2,2,32,128]{4,3,2,0,1:T(8,128)S(1)}, f32[2,2,2,32,128]{4,3,2,0,1:T(8,128)S(1)}, u32[]{:S(2)}, u32[]{:S(2)}) %collective-permute-start.7) | collective-permute-done | bytes 131104 | tf_op jit(solution)/shard_map/ppermute | solution.py:367
  24.8 1.6 %collective-permute-done.8 = f32[2,2,2,32,128]{4,3,2,0,1:T(8,128)S(1)} collective-permute-done((f32[2,2,2,32,128]{4,3,2,0,1:T(8,128)S(1)}, f32[2,2,2,32,128]{4,3,2,0,1:T(8,128)S(1)}, u32[]{:S(2)}, u32[]{:S(2)}) %collective-permute-start.8) | collective-permute-done | bytes 131104 | tf_op jit(solution)/shard_map/ppermute | solution.py:367
  26.4 0.0 collective-permute-done.9.y1
  26.4 0.9 %after_kernel.1 = (f32[8,2,32,128]{3,2,1,0:T(8,128)S(1)}, f32[4,2,32,128]{3,2,1,0:T(8,128)S(1)}, bf16[2,256,256]{2,1,0:T(8,128)(2,1)S(1)}, bf16[2,256,256]{2,1,0:T(8,128)(2,1)S(1)}) custom-call(f32[2,2,2,32,128]{4,3,2,1,0:T(8,128)S(1)} %copy.4.a0, f32[2,2,2,32,128]{4,3,2,1,0:T(8,128)S(1)} %copy.5.a1, f32[2,2,32,128]{3,2,1,0:T(8,128)S(1)} %collective-permute-done.9.y1, ...), custom_call_target="tpu_custom_call" | custom-call | flops 2000000000 | bytes 262144 | tf_op jit(solution)/shard_map/after_kernel/pallas_call | solution.py:347
  27.3 0.7 %collective-permute-start.10 = (f32[4,2,32,128]{3,2,1,0:T(8,128)S(1)}, f32[4,2,32,128]{3,2,1,0:T(8,128)S(1)}, u32[]{:S(2)}, u32[]{:S(2)}) collective-permute-start(f32[4,2,32,128]{3,2,1,0:T(8,128)S(1)} %get-tuple-element.44), channel_id=1, source_target_pairs={{0,1},{1,0},{2,3},{3,2},{4,5},{5,4},{6,7},{7,6},{8,9},{9,8},{10,11... | collective-permute-start | bytes 393224 | tf_op jit(solution)/shard_map/ppermute | solution.py:367
  28.0 3.5 %collective-permute-done.11.mine = f32[2,2,32,128]{3,2,1,0:T(8,128)S(1)} collective-permute-done((f32[2,2,32,128]{3,2,1,0:T(8,128)S(1)}, f32[2,2,32,128]{3,2,1,0:T(8,128)S(1)}, u32[]{:S(2)}, u32[]{:S(2)}) %collective-permute-start.11) | collective-permute-done | bytes 65568 | tf_op jit(solution)/shard_map/ppermute | solution.py:367
  31.5 0.9 %collective-permute-done.12.late = f32[2,2,32,128]{3,2,1,0:T(8,128)S(1)} collective-permute-done((f32[2,2,32,128]{3,2,1,0:T(8,128)S(1)}, f32[2,2,32,128]{3,2,1,0:T(8,128)S(1)}, u32[]{:S(2)}, u32[]{:S(2)}) %collective-permute-start.12) | collective-permute-done | bytes 65568 | tf_op jit(solution)/shard_map/ppermute | solution.py:367
  32.4 1.6 %third_kernel.1 = f32[1024,128]{1,0:T(8,128)} custom-call(s32[1]{0:T(128)} %bitcast.me_ref, f32[8,2,32,128]{3,2,1,0:T(8,128)S(1)} %get-tuple-element.43.keep, f32[4,2,32,128]{3,2,1,0:T(8,128)S(1)} %collective-permute-done.10.early, f32[4,2,32,128]{3,2,1,0:T(8,128)S(1)} %join_kernel.1.far, bf16[2,256,256]{2,1,0:T(8,128)(2,1)S(1)} %get-tuple-element.47.wh, ...), custom_call_target="tpu_custom_call" | custom-call | tf_op jit(solution)/shard_map/third_kernel/pallas_call | solution.py:347
  (12 shorter events, 0.1 us)
Async XLA Ops:
  0.0 7.0 %copy-start = (f32[2,12,128,128]{3,2,1,0:T(8,128)S(1)}, f32[2,12,128,128]{3,2,1,0:T(8,128)}, u32[]{:S(2)}) copy-start(f32[2,12,128,128]{3,2,1,0:T(8,128)} %gates.9) | copy-start | bytes 4718596
  3.7 3.3 %collective-permute-start = (f32[2,2,64,128]{3,2,1,0:T(8,128)S(1)}, f32[2,2,64,128]{3,2,1,0:T(8,128)S(1)}, u32[]{:S(2)}, u32[]{:S(2)}) collective-permute-start(f32[2,2,64,128]{3,2,1,0:T(8,128)S(1)} %get-tuple-element.29), channel_id=1, source_target_pairs={{0,1},{1,0},{2,3},{3,2},{4,5},{5,4},{6,7},{7,6},{8,9},{9,8},{10,11... | collective-permute-start | bytes 393224 | tf_op jit(solution)/shard_map/ppermute | solution.py:367
  4.5 5.1 %collective-permute-start.1 = (f32[2,2,64,128]{3,2,1,0:T(8,128)S(1)}, f32[2,2,64,128]{3,2,1,0:T(8,128)S(1)}, u32[]{:S(2)}, u32[]{:S(2)}) collective-permute-start(f32[2,2,64,128]{3,2,1,0:T(8,128)S(1)} %get-tuple-element.31), channel_id=1, source_target_pairs={{0,2},{1,3},{2,0},{3,1},{4,6},{5,7},{6,4},{7,5},{8,10},{9,11},{10,... | collective-permute-start | bytes 393224 | tf_op jit(solution)/shard_map/ppermute | solution.py:367
  5.7 4.7 %collective-permute-start.2 = (f32[2,2,64,128]{3,2,1,0:T(8,128)S(1)}, f32[2,2,64,128]{3,2,1,0:T(8,128)S(1)}, u32[]{:S(2)}, u32[]{:S(2)}) collective-permute-start(f32[2,2,64,128]{3,2,1,0:T(8,128)S(1)} %get-tuple-element.32), channel_id=1, source_target_pairs={{0,4},{1,5},{2,6},{3,7},{4,0},{5,1},{6,2},{7,3},{8,12},{9,13},{10,... | collective-permute-start | bytes 393224 | tf_op jit(solution)/shard_map/ppermute | solution.py:367
  8.5 6.0 %collective-permute-start.3 = (f32[2,2,64,128]{3,2,1,0:T(8,128)S(1)}, f32[2,2,64,128]{3,2,1,0:T(8,128)S(1)}, u32[]{:S(2)}, u32[]{:S(2)}) collective-permute-start(f32[2,2,64,128]{3,2,1,0:T(8,128)S(1)} %get-tuple-element.34), channel_id=1, source_target_pairs={{0,6},{1,7},{2,4},{3,5},{4,2},{5,3},{6,0},{7,1},{8,14},{9,15},{10,... | collective-permute-start | bytes 393224 | tf_op jit(solution)/shard_map/ppermute | solution.py:367
  12.0 2.1 %collective-permute-start.4 = (f32[2,64,128]{2,1,0:T(8,128)S(1)}, f32[2,64,128]{2,1,0:T(8,128)S(1)}, u32[]{:S(2)}, u32[]{:S(2)}) collective-permute-start(f32[2,64,128]{2,1,0:T(8,128)S(1)} %get-tuple-element.35), channel_id=1, source_target_pairs={{0,1},{1,0},{2,3},{3,2},{4,5},{5,4},{6,7},{7,6},{8,9},{9,8},{10,11... | collective-permute-start | bytes 196616 | tf_op jit(solution)/shard_map/ppermute | solution.py:367
  13.3 1.3 %collective-permute-start.5 = (f32[2,64,128]{2,1,0:T(8,128)S(1)}, f32[2,64,128]{2,1,0:T(8,128)S(1)}, u32[]{:S(2)}, u32[]{:S(2)}) collective-permute-start(f32[2,64,128]{2,1,0:T(8,128)S(1)} %get-tuple-element.36), channel_id=1, source_target_pairs={{0,1},{1,0},{2,3},{3,2},{4,5},{5,4},{6,7},{7,6},{8,9},{9,8},{10,11... | collective-permute-start | bytes 196616 | tf_op jit(solution)/shard_map/ppermute | solution.py:367
  15.4 2.1 %collective-permute-start.6 = (f32[8,2,32,128]{3,2,1,0:T(8,128)S(1)}, f32[8,2,32,128]{3,2,1,0:T(8,128)S(1)}, u32[]{:S(2)}, u32[]{:S(2)}) collective-permute-start(f32[8,2,32,128]{3,2,1,0:T(8,128)S(1)} %get-tuple-element.40), channel_id=1, source_target_pairs={{0,1},{1,0},{2,3},{3,2},{4,5},{5,4},{6,7},{7,6},{8,9},{9,8},{10,11... | collective-permute-start | bytes 786440 | tf_op jit(solution)/shard_map/ppermute | solution.py:367
  17.5 7.3 %collective-permute-start.7 = (f32[2,2,2,32,128]{4,3,2,0,1:T(8,128)S(1)}, f32[2,2,2,32,128]{4,3,2,0,1:T(8,128)S(1)}, u32[]{:S(2)}, u32[]{:S(2)}) collective-permute-start(f32[2,2,2,32,128]{4,3,2,0,1:T(8,128)S(1)} %pad_maximum_fusion), channel_id=1, source_target_pairs={{0,8},{1,11},{2,10},{3,9},{4,12},{5,15},{6,14},{7,13},{8,0},{9,3},... | collective-permute-start | bytes 393224 | tf_op jit(solution)/shard_map/ppermute | solution.py:367
  17.6 8.7 %collective-permute-start.8 = (f32[2,2,2,32,128]{4,3,2,0,1:T(8,128)S(1)}, f32[2,2,2,32,128]{4,3,2,0,1:T(8,128)S(1)}, u32[]{:S(2)}, u32[]{:S(2)}) collective-permute-start(f32[2,2,2,32,128]{4,3,2,0,1:T(8,128)S(1)} %pad_maximum_fusion.1), channel_id=1, source_target_pairs={{0,4},{1,7},{2,6},{3,5},{4,0},{5,3},{6,2},{7,1},{8,12},{9,15},{10,... | collective-permute-start | bytes 393224 | tf_op jit(solution)/shard_map/ppermute | solution.py:367
  19.9 6.4 %collective-permute-start.9 = (f32[2,2,32,128]{3,2,1,0:T(8,128)S(1)}, f32[2,2,32,128]{3,2,1,0:T(8,128)S(1)}, u32[]{:S(2)}, u32[]{:S(2)}) collective-permute-start(f32[2,2,32,128]{3,2,1,0:T(8,128)S(1)} %pad_maximum_fusion.2), channel_id=1, source_target_pairs={{0,2},{1,3},{2,0},{3,1},{4,6},{5,7},{6,4},{7,5},{8,10},{9,11},{10,... | collective-permute-start | bytes 196616 | tf_op jit(solution)/shard_map/ppermute | solution.py:367
  20.9 10.6 %collective-permute-start.11 = (f32[2,2,32,128]{3,2,1,0:T(8,128)S(1)}, f32[2,2,32,128]{3,2,1,0:T(8,128)S(1)}, u32[]{:S(2)}, u32[]{:S(2)}) collective-permute-start(f32[2,2,32,128]{3,2,1,0:T(8,128)S(1)} %get-tuple-element.45), channel_id=1, source_target_pairs={{0,12},{1,15},{2,14},{3,13},{4,8},{5,11},{6,10},{7,9},{8,4},{9,7},... | collective-permute-start | bytes 196616 | tf_op jit(solution)/shard_map/ppermute | solution.py:367
  23.2 9.2 %collective-permute-start.12 = (f32[2,2,32,128]{3,2,1,0:T(8,128)S(1)}, f32[2,2,32,128]{3,2,1,0:T(8,128)S(1)}, u32[]{:S(2)}, u32[]{:S(2)}) collective-permute-start(f32[2,2,32,128]{3,2,1,0:T(8,128)S(1)} %get-tuple-element.46), channel_id=1, source_target_pairs={{0,13},{1,14},{2,15},{3,12},{4,9},{5,10},{6,11},{7,8},{8,5},{9,6},... | collective-permute-start | bytes 196616 | tf_op jit(solution)/shard_map/ppermute | solution.py:367
  27.3 5.1 %collective-permute-start.10 = (f32[4,2,32,128]{3,2,1,0:T(8,128)S(1)}, f32[4,2,32,128]{3,2,1,0:T(8,128)S(1)}, u32[]{:S(2)}, u32[]{:S(2)}) collective-permute-start(f32[4,2,32,128]{3,2,1,0:T(8,128)S(1)} %get-tuple-element.44), channel_id=1, source_target_pairs={{0,1},{1,0},{2,3},{3,2},{4,5},{5,4},{6,7},{7,6},{8,9},{9,8},{10,11... | collective-permute-start | bytes 393224 | tf_op jit(solution)/shard_map/ppermute | solution.py:367

commit v6 on v5

--- a/solution.py
+++ b/solution.py
@@ -297,7 +297,7 @@
     gate_nine(s, g, blocks, [keep.at[n] for n in range(8)] + [send.at[n] for n in range(4)])
 
 
-def join_kernel(indices, mine, late, out, s, mh, ml):
+def join_kernel(indices, late, mine, out, s, mh, ml):
     for n, block in enumerate((*split(mine), *split(late))):
         for c in range(2):
             out[n, c] = block[c]
@@ -418,7 +418,7 @@
         [VMEM] * 6,
     )
     early = flipped(send, 1)
-    far = call(join_kernel, (9,), [shape(4, *block)], 8, [mine, late], [VMEM] * 2)[0]
+    far = call(join_kernel, (9,), [shape(4, *block)], 8, [late, mine], [VMEM] * 2)[0]
     out = call(
         third_kernel,
         (10, 11),

time: 34.7 us -> 34.7 us (level); the launches traced: 34 us -> 34.5 us
  waiting for transfers between devices: 10.6 us -> 11.2 us
    ppermute x13, waiting for transfers between devices: 10.6 us -> 11.2 us  [flipped(): return lax.ppermute(block, 'node', route)]
where the time goes in v6:
time: 34.7 us; the launch traced here: 34.5 us
  starting transfers between devices  12.3 us (35%)
  waiting for transfers between devices  11.2 us (32%)
  Pallas kernels  10.8 us (31%)
    ppermute x13, starting transfers between devices, flipped(): return lax.ppermute(block, 'node', route)  12.3 us
    ppermute x13, waiting for transfers between devices, flipped(): return lax.ppermute(block, 'node', route)  11.2 us
    pallas_call x8, Pallas kernels, call(): pl.pallas_call(functools.partial(kernel, indices), out_shape=outs, in_spe...  10.8 us
  transfers between devices with their start and end apart: 13, of which 9 were waited for; matrix products, arithmetic and copies ran while one was open for 0% of the time, Pallas kernels for 14%

profile of v6, /device:TPU:19, one launch (start us, length us, event | category | flops | bytes accessed | tf_op | source)
XLA Modules:
  0.0 34.5 jit_solution(6673211188354052409)
XLA Ops:
  0.0 3.7 %first_kernel.1 = (f32[2,2,64,128]{3,2,1,0:T(8,128)S(1)}, f32[2,2,64,128]{3,2,1,0:T(8,128)S(1)}, f32[2,64,128]{2,1,0:T(8,128)S(1)}, f32[2,64,128]{2,1,0:T(8,128)S(1)}, f32[2,2,64,128]{3,2,1,0:T(8,128)S(1)}) custom-call(s32[1]{0:T(128)} %bitcast.me_ref, f32[1024,128]{1,0:T(8,128)} %bitcast.25, f32[2,12,128,128]{3,2,1,0:T(8,128)} %gates.9), custom_call_target="tpu_custom_call" | custom-call | tf_op jit(solution)/shard_map/first_kernel/pallas_call | solution.py:347
  3.7 0.7 %collective-permute-start = (f32[2,2,64,128]{3,2,1,0:T(8,128)S(1)}, f32[2,2,64,128]{3,2,1,0:T(8,128)S(1)}, u32[]{:S(2)}, u32[]{:S(2)}) collective-permute-start(f32[2,2,64,128]{3,2,1,0:T(8,128)S(1)} %get-tuple-element.29), channel_id=1, source_target_pairs={{0,1},{1,0},{2,3},{3,2},{4,5},{5,4},{6,7},{7,6},{8,9},{9,8},{10,11... | collective-permute-start | bytes 393224 | tf_op jit(solution)/shard_map/ppermute | solution.py:367
  4.5 1.3 %collective-permute-start.1 = (f32[2,2,64,128]{3,2,1,0:T(8,128)S(1)}, f32[2,2,64,128]{3,2,1,0:T(8,128)S(1)}, u32[]{:S(2)}, u32[]{:S(2)}) collective-permute-start(f32[2,2,64,128]{3,2,1,0:T(8,128)S(1)} %get-tuple-element.31), channel_id=1, source_target_pairs={{0,2},{1,3},{2,0},{3,1},{4,6},{5,7},{6,4},{7,5},{8,10},{9,11},{10,... | collective-permute-start | bytes 393224 | tf_op jit(solution)/shard_map/ppermute | solution.py:367
  5.7 1.3 %collective-permute-start.2 = (f32[2,2,64,128]{3,2,1,0:T(8,128)S(1)}, f32[2,2,64,128]{3,2,1,0:T(8,128)S(1)}, u32[]{:S(2)}, u32[]{:S(2)}) collective-permute-start(f32[2,2,64,128]{3,2,1,0:T(8,128)S(1)} %get-tuple-element.32), channel_id=1, source_target_pairs={{0,4},{1,5},{2,6},{3,7},{4,0},{5,1},{6,2},{7,3},{8,12},{9,13},{10,... | collective-permute-start | bytes 393224 | tf_op jit(solution)/shard_map/ppermute | solution.py:367
  7.0 0.0 collective-permute-done.recv
  7.0 1.5 %before_lower.1 = (f32[2,2,64,128]{3,2,1,0:T(8,128)S(1)}, f32[2,2,64,128]{3,2,1,0:T(8,128)S(1)}) custom-call(f32[2,64,128]{2,1,0:T(8,128)S(1)} %get-tuple-element.27.own0, f32[2,64,128]{2,1,0:T(8,128)S(1)} %get-tuple-element.28.own3, f32[2,2,64,128]{3,2,1,0:T(8,128)S(1)} %collective-permute-done.recv, f32[2,12,128,128]{3,2,1,0:T(8,128)S(1)} %copy-done), custom_call_target="tpu_custom_call" | custom-call | flops 2000000000 | bytes 262144 | tf_op jit(solution)/shard_map/before_lower/pallas_call | solution.py:347
  8.5 0.7 %collective-permute-start.3 = (f32[2,2,64,128]{3,2,1,0:T(8,128)S(1)}, f32[2,2,64,128]{3,2,1,0:T(8,128)S(1)}, u32[]{:S(2)}, u32[]{:S(2)}) collective-permute-start(f32[2,2,64,128]{3,2,1,0:T(8,128)S(1)} %get-tuple-element.34), channel_id=1, source_target_pairs={{0,6},{1,7},{2,4},{3,5},{4,2},{5,3},{6,0},{7,1},{8,14},{9,15},{10,... | collective-permute-start | bytes 393224 | tf_op jit(solution)/shard_map/ppermute | solution.py:367
  9.3 0.3 collective-permute-done.1.r1
  9.6 0.9 %collective-permute-done.2.r2 = f32[2,2,64,128]{3,2,1,0:T(8,128)S(1)} collective-permute-done((f32[2,2,64,128]{3,2,1,0:T(8,128)S(1)}, f32[2,2,64,128]{3,2,1,0:T(8,128)S(1)}, u32[]{:S(2)}, u32[]{:S(2)}) %collective-permute-start.2) | collective-permute-done | bytes 131104 | tf_op jit(solution)/shard_map/ppermute | solution.py:367
  10.5 1.6 %after_lower.1 = (f32[2,2,64,128]{3,2,1,0:T(8,128)S(1)}, f32[2,64,128]{2,1,0:T(8,128)S(1)}, f32[2,64,128]{2,1,0:T(8,128)S(1)}, bf16[2,256,256]{2,1,0:T(8,128)(2,1)S(1)}, bf16[2,256,256]{2,1,0:T(8,128)(2,1)S(1)}) custom-call(f32[2,2,64,128]{3,2,1,0:T(8,128)S(1)} %collective-permute-done.1.r1, f32[2,2,64,128]{3,2,1,0:T(8,128)S(1)} %collective-permute-done.2.r2, ...), custom_call_target="tpu_custom_call" | custom-call | flops 2000000000 | bytes 262144 | tf_op jit(solution)/shard_map/after_lower/pallas_call | solution.py:347
  12.0 1.2 %collective-permute-start.4 = (f32[2,64,128]{2,1,0:T(8,128)S(1)}, f32[2,64,128]{2,1,0:T(8,128)S(1)}, u32[]{:S(2)}, u32[]{:S(2)}) collective-permute-start(f32[2,64,128]{2,1,0:T(8,128)S(1)} %get-tuple-element.35), channel_id=1, source_target_pairs={{0,1},{1,0},{2,3},{3,2},{4,5},{5,4},{6,7},{7,6},{8,9},{9,8},{10,11... | collective-permute-start | bytes 196616 | tf_op jit(solution)/shard_map/ppermute | solution.py:367
  13.3 0.1 collective-permute-start.5
  13.4 0.8 %collective-permute-done.4.post1 = f32[2,64,128]{2,1,0:T(8,128)S(1)} collective-permute-done((f32[2,64,128]{2,1,0:T(8,128)S(1)}, f32[2,64,128]{2,1,0:T(8,128)S(1)}, u32[]{:S(2)}, u32[]{:S(2)}) %collective-permute-start.4) | collective-permute-done | bytes 65568 | tf_op jit(solution)/shard_map/ppermute | solution.py:367
  14.2 0.4 %collective-permute-done.5.post2 = f32[2,64,128]{2,1,0:T(8,128)S(1)} collective-permute-done((f32[2,64,128]{2,1,0:T(8,128)S(1)}, f32[2,64,128]{2,1,0:T(8,128)S(1)}, u32[]{:S(2)}, u32[]{:S(2)}) %collective-permute-start.5) | collective-permute-done | bytes 65568 | tf_op jit(solution)/shard_map/ppermute | solution.py:367
  14.5 0.0 collective-permute-done.3.r3
  14.5 0.8 %second_kernel.1 = (f32[3,2,2,32,128]{4,3,2,1,0:T(8,128)S(1)}, f32[8,2,32,128]{3,2,1,0:T(8,128)S(1)}, f32[2,32,128]{2,1,0:T(8,128)S(1)}, f32[2,32,128]{2,1,0:T(8,128)S(1)}) custom-call(s32[1]{0:T(128)} %bitcast.me_ref, f32[2,2,64,128]{3,2,1,0:T(8,128)S(1)} %get-tuple-element.30.p0, f32[2,2,64,128]{3,2,1,0:T(8,128)S(1)} %get-tuple-element.33.near, ...), custom_call_target="tpu_custom_call" | custom-call | tf_op jit(solution)/shard_map/second_kernel/pallas_call | solution.py:347
  15.4 0.9 %collective-permute-start.6 = (f32[8,2,32,128]{3,2,1,0:T(8,128)S(1)}, f32[8,2,32,128]{3,2,1,0:T(8,128)S(1)}, u32[]{:S(2)}, u32[]{:S(2)}) collective-permute-start(f32[8,2,32,128]{3,2,1,0:T(8,128)S(1)} %get-tuple-element.40), channel_id=1, source_target_pairs={{0,1},{1,0},{2,3},{3,2},{4,5},{5,4},{6,7},{7,6},{8,9},{9,8},{10,11... | collective-permute-start | bytes 786440 | tf_op jit(solution)/shard_map/ppermute | solution.py:367
  16.3 1.1 %collective-permute-done.6 = f32[8,2,32,128]{3,2,1,0:T(8,128)S(1)} collective-permute-done((f32[8,2,32,128]{3,2,1,0:T(8,128)S(1)}, f32[8,2,32,128]{3,2,1,0:T(8,128)S(1)}, u32[]{:S(2)}, u32[]{:S(2)}) %collective-permute-start.6) | collective-permute-done | bytes 262176 | tf_op jit(solution)/shard_map/ppermute | solution.py:367
  17.5 0.1 collective-permute-start.7
  17.6 2.3 %collective-permute-start.8 = (f32[2,2,2,32,128]{4,3,2,0,1:T(8,128)S(1)}, f32[2,2,2,32,128]{4,3,2,0,1:T(8,128)S(1)}, u32[]{:S(2)}, u32[]{:S(2)}) collective-permute-start(f32[2,2,2,32,128]{4,3,2,0,1:T(8,128)S(1)} %pad_maximum_fusion.1), channel_id=1, source_target_pairs={{0,4},{1,7},{2,6},{3,5},{4,0},{5,3},{6,2},{7,1},{8,12},{9,15},{10,... | collective-permute-start | bytes 393224 | tf_op jit(solution)/shard_map/ppermute | solution.py:367
  19.9 0.3 collective-permute-start.9
  20.2 0.7 %before_kernel.1 = (f32[2,2,32,128]{3,2,1,0:T(8,128)S(1)}, f32[2,2,32,128]{3,2,1,0:T(8,128)S(1)}) custom-call(f32[2,2,32,128]{3,2,1,0:T(8,128)S(1)} %get-tuple-element.54.own, f32[2,2,32,128]{3,2,1,0:T(8,128)S(1)} %get-tuple-element.49.recv, f32[2,12,128,128]{3,2,1,0:T(8,128)S(1)} %copy-done), custom_call_target="tpu_custom_call" | custom-call | flops 1000000000 | bytes 262144 | tf_op jit(solution)/shard_map/before_kernel/pallas_call | solution.py:347
  20.9 2.5 %collective-permute-start.11 = (f32[2,2,32,128]{3,2,1,0:T(8,128)S(1)}, f32[2,2,32,128]{3,2,1,0:T(8,128)S(1)}, u32[]{:S(2)}, u32[]{:S(2)}) collective-permute-start(f32[2,2,32,128]{3,2,1,0:T(8,128)S(1)} %get-tuple-element.45), channel_id=1, source_target_pairs={{0,13},{1,14},{2,15},{3,12},{4,9},{5,10},{6,11},{7,8},{8,5},{9,6},... | collective-permute-start | bytes 196616 | tf_op jit(solution)/shard_map/ppermute | solution.py:367
  23.4 0.1 collective-permute-start.12
  23.5 1.2 %collective-permute-done.7 = f32[2,2,2,32,128]{4,3,2,0,1:T(8,128)S(1)} collective-permute-done((f32[2,2,2,32,128]{4,3,2,0,1:T(8,128)S(1)}, f32[2,2,2,32,128]{4,3,2,0,1:T(8,128)S(1)}, u32[]{:S(2)}, u32[]{:S(2)}) %collective-permute-start.7) | collective-permute-done | bytes 131104 | tf_op jit(solution)/shard_map/ppermute | solution.py:367
  24.8 1.6 %collective-permute-done.8 = f32[2,2,2,32,128]{4,3,2,0,1:T(8,128)S(1)} collective-permute-done((f32[2,2,2,32,128]{4,3,2,0,1:T(8,128)S(1)}, f32[2,2,2,32,128]{4,3,2,0,1:T(8,128)S(1)}, u32[]{:S(2)}, u32[]{:S(2)}) %collective-permute-start.8) | collective-permute-done | bytes 131104 | tf_op jit(solution)/shard_map/ppermute | solution.py:367
  26.4 0.0 collective-permute-done.9.y1
  26.4 0.9 %after_kernel.1 = (f32[8,2,32,128]{3,2,1,0:T(8,128)S(1)}, f32[4,2,32,128]{3,2,1,0:T(8,128)S(1)}, bf16[2,256,256]{2,1,0:T(8,128)(2,1)S(1)}, bf16[2,256,256]{2,1,0:T(8,128)(2,1)S(1)}) custom-call(f32[2,2,2,32,128]{4,3,2,1,0:T(8,128)S(1)} %copy.4.a0, f32[2,2,2,32,128]{4,3,2,1,0:T(8,128)S(1)} %copy.5.a1, f32[2,2,32,128]{3,2,1,0:T(8,128)S(1)} %collective-permute-done.9.y1, ...), custom_call_target="tpu_custom_call" | custom-call | flops 2000000000 | bytes 262144 | tf_op jit(solution)/shard_map/after_kernel/pallas_call | solution.py:347
  27.3 0.7 %collective-permute-start.10 = (f32[4,2,32,128]{3,2,1,0:T(8,128)S(1)}, f32[4,2,32,128]{3,2,1,0:T(8,128)S(1)}, u32[]{:S(2)}, u32[]{:S(2)}) collective-permute-start(f32[4,2,32,128]{3,2,1,0:T(8,128)S(1)} %get-tuple-element.44), channel_id=1, source_target_pairs={{0,1},{1,0},{2,3},{3,2},{4,5},{5,4},{6,7},{7,6},{8,9},{9,8},{10,11... | collective-permute-start | bytes 393224 | tf_op jit(solution)/shard_map/ppermute | solution.py:367
  28.0 3.1 %collective-permute-done.11.late = f32[2,2,32,128]{3,2,1,0:T(8,128)S(1)} collective-permute-done((f32[2,2,32,128]{3,2,1,0:T(8,128)S(1)}, f32[2,2,32,128]{3,2,1,0:T(8,128)S(1)}, u32[]{:S(2)}, u32[]{:S(2)}) %collective-permute-start.11) | collective-permute-done | bytes 65568 | tf_op jit(solution)/shard_map/ppermute | solution.py:367
  31.1 1.8 %collective-permute-done.12.mine = f32[2,2,32,128]{3,2,1,0:T(8,128)S(1)} collective-permute-done((f32[2,2,32,128]{3,2,1,0:T(8,128)S(1)}, f32[2,2,32,128]{3,2,1,0:T(8,128)S(1)}, u32[]{:S(2)}, u32[]{:S(2)}) %collective-permute-start.12) | collective-permute-done | bytes 65568 | tf_op jit(solution)/shard_map/ppermute | solution.py:367
  32.9 1.6 %third_kernel.1 = f32[1024,128]{1,0:T(8,128)} custom-call(s32[1]{0:T(128)} %bitcast.me_ref, f32[8,2,32,128]{3,2,1,0:T(8,128)S(1)} %get-tuple-element.43.keep, f32[4,2,32,128]{3,2,1,0:T(8,128)S(1)} %collective-permute-done.10.early, f32[4,2,32,128]{3,2,1,0:T(8,128)S(1)} %join_kernel.1.far, bf16[2,256,256]{2,1,0:T(8,128)(2,1)S(1)} %get-tuple-element.47.wh, ...), custom_call_target="tpu_custom_call" | custom-call | tf_op jit(solution)/shard_map/third_kernel/pallas_call | solution.py:347
  (12 shorter events, 0.1 us)
Async XLA Ops:
  0.0 7.0 %copy-start = (f32[2,12,128,128]{3,2,1,0:T(8,128)S(1)}, f32[2,12,128,128]{3,2,1,0:T(8,128)}, u32[]{:S(2)}) copy-start(f32[2,12,128,128]{3,2,1,0:T(8,128)} %gates.9) | copy-start | bytes 4718596
  3.7 3.3 %collective-permute-start = (f32[2,2,64,128]{3,2,1,0:T(8,128)S(1)}, f32[2,2,64,128]{3,2,1,0:T(8,128)S(1)}, u32[]{:S(2)}, u32[]{:S(2)}) collective-permute-start(f32[2,2,64,128]{3,2,1,0:T(8,128)S(1)} %get-tuple-element.29), channel_id=1, source_target_pairs={{0,1},{1,0},{2,3},{3,2},{4,5},{5,4},{6,7},{7,6},{8,9},{9,8},{10,11... | collective-permute-start | bytes 393224 | tf_op jit(solution)/shard_map/ppermute | solution.py:367
  4.5 5.1 %collective-permute-start.1 = (f32[2,2,64,128]{3,2,1,0:T(8,128)S(1)}, f32[2,2,64,128]{3,2,1,0:T(8,128)S(1)}, u32[]{:S(2)}, u32[]{:S(2)}) collective-permute-start(f32[2,2,64,128]{3,2,1,0:T(8,128)S(1)} %get-tuple-element.31), channel_id=1, source_target_pairs={{0,2},{1,3},{2,0},{3,1},{4,6},{5,7},{6,4},{7,5},{8,10},{9,11},{10,... | collective-permute-start | bytes 393224 | tf_op jit(solution)/shard_map/ppermute | solution.py:367
  5.7 4.7 %collective-permute-start.2 = (f32[2,2,64,128]{3,2,1,0:T(8,128)S(1)}, f32[2,2,64,128]{3,2,1,0:T(8,128)S(1)}, u32[]{:S(2)}, u32[]{:S(2)}) collective-permute-start(f32[2,2,64,128]{3,2,1,0:T(8,128)S(1)} %get-tuple-element.32), channel_id=1, source_target_pairs={{0,4},{1,5},{2,6},{3,7},{4,0},{5,1},{6,2},{7,3},{8,12},{9,13},{10,... | collective-permute-start | bytes 393224 | tf_op jit(solution)/shard_map/ppermute | solution.py:367
  8.5 6.0 %collective-permute-start.3 = (f32[2,2,64,128]{3,2,1,0:T(8,128)S(1)}, f32[2,2,64,128]{3,2,1,0:T(8,128)S(1)}, u32[]{:S(2)}, u32[]{:S(2)}) collective-permute-start(f32[2,2,64,128]{3,2,1,0:T(8,128)S(1)} %get-tuple-element.34), channel_id=1, source_target_pairs={{0,6},{1,7},{2,4},{3,5},{4,2},{5,3},{6,0},{7,1},{8,14},{9,15},{10,... | collective-permute-start | bytes 393224 | tf_op jit(solution)/shard_map/ppermute | solution.py:367
  12.0 2.1 %collective-permute-start.4 = (f32[2,64,128]{2,1,0:T(8,128)S(1)}, f32[2,64,128]{2,1,0:T(8,128)S(1)}, u32[]{:S(2)}, u32[]{:S(2)}) collective-permute-start(f32[2,64,128]{2,1,0:T(8,128)S(1)} %get-tuple-element.35), channel_id=1, source_target_pairs={{0,1},{1,0},{2,3},{3,2},{4,5},{5,4},{6,7},{7,6},{8,9},{9,8},{10,11... | collective-permute-start | bytes 196616 | tf_op jit(solution)/shard_map/ppermute | solution.py:367
  13.3 1.3 %collective-permute-start.5 = (f32[2,64,128]{2,1,0:T(8,128)S(1)}, f32[2,64,128]{2,1,0:T(8,128)S(1)}, u32[]{:S(2)}, u32[]{:S(2)}) collective-permute-start(f32[2,64,128]{2,1,0:T(8,128)S(1)} %get-tuple-element.36), channel_id=1, source_target_pairs={{0,1},{1,0},{2,3},{3,2},{4,5},{5,4},{6,7},{7,6},{8,9},{9,8},{10,11... | collective-permute-start | bytes 196616 | tf_op jit(solution)/shard_map/ppermute | solution.py:367
  15.4 2.1 %collective-permute-start.6 = (f32[8,2,32,128]{3,2,1,0:T(8,128)S(1)}, f32[8,2,32,128]{3,2,1,0:T(8,128)S(1)}, u32[]{:S(2)}, u32[]{:S(2)}) collective-permute-start(f32[8,2,32,128]{3,2,1,0:T(8,128)S(1)} %get-tuple-element.40), channel_id=1, source_target_pairs={{0,1},{1,0},{2,3},{3,2},{4,5},{5,4},{6,7},{7,6},{8,9},{9,8},{10,11... | collective-permute-start | bytes 786440 | tf_op jit(solution)/shard_map/ppermute | solution.py:367
  17.5 7.3 %collective-permute-start.7 = (f32[2,2,2,32,128]{4,3,2,0,1:T(8,128)S(1)}, f32[2,2,2,32,128]{4,3,2,0,1:T(8,128)S(1)}, u32[]{:S(2)}, u32[]{:S(2)}) collective-permute-start(f32[2,2,2,32,128]{4,3,2,0,1:T(8,128)S(1)} %pad_maximum_fusion), channel_id=1, source_target_pairs={{0,8},{1,11},{2,10},{3,9},{4,12},{5,15},{6,14},{7,13},{8,0},{9,3},... | collective-permute-start | bytes 393224 | tf_op jit(solution)/shard_map/ppermute | solution.py:367
  17.6 8.7 %collective-permute-start.8 = (f32[2,2,2,32,128]{4,3,2,0,1:T(8,128)S(1)}, f32[2,2,2,32,128]{4,3,2,0,1:T(8,128)S(1)}, u32[]{:S(2)}, u32[]{:S(2)}) collective-permute-start(f32[2,2,2,32,128]{4,3,2,0,1:T(8,128)S(1)} %pad_maximum_fusion.1), channel_id=1, source_target_pairs={{0,4},{1,7},{2,6},{3,5},{4,0},{5,3},{6,2},{7,1},{8,12},{9,15},{10,... | collective-permute-start | bytes 393224 | tf_op jit(solution)/shard_map/ppermute | solution.py:367
  19.9 6.4 %collective-permute-start.9 = (f32[2,2,32,128]{3,2,1,0:T(8,128)S(1)}, f32[2,2,32,128]{3,2,1,0:T(8,128)S(1)}, u32[]{:S(2)}, u32[]{:S(2)}) collective-permute-start(f32[2,2,32,128]{3,2,1,0:T(8,128)S(1)} %pad_maximum_fusion.2), channel_id=1, source_target_pairs={{0,2},{1,3},{2,0},{3,1},{4,6},{5,7},{6,4},{7,5},{8,10},{9,11},{10,... | collective-permute-start | bytes 196616 | tf_op jit(solution)/shard_map/ppermute | solution.py:367
  20.9 10.1 %collective-permute-start.11 = (f32[2,2,32,128]{3,2,1,0:T(8,128)S(1)}, f32[2,2,32,128]{3,2,1,0:T(8,128)S(1)}, u32[]{:S(2)}, u32[]{:S(2)}) collective-permute-start(f32[2,2,32,128]{3,2,1,0:T(8,128)S(1)} %get-tuple-element.45), channel_id=1, source_target_pairs={{0,13},{1,14},{2,15},{3,12},{4,9},{5,10},{6,11},{7,8},{8,5},{9,6},... | collective-permute-start | bytes 196616 | tf_op jit(solution)/shard_map/ppermute | solution.py:367
  23.4 9.5 %collective-permute-start.12 = (f32[2,2,32,128]{3,2,1,0:T(8,128)S(1)}, f32[2,2,32,128]{3,2,1,0:T(8,128)S(1)}, u32[]{:S(2)}, u32[]{:S(2)}) collective-permute-start(f32[2,2,32,128]{3,2,1,0:T(8,128)S(1)} %get-tuple-element.46), channel_id=1, source_target_pairs={{0,12},{1,15},{2,14},{3,13},{4,8},{5,11},{6,10},{7,9},{8,4},{9,7},... | collective-permute-start | bytes 196616 | tf_op jit(solution)/shard_map/ppermute | solution.py:367
  27.3 5.6 %collective-permute-start.10 = (f32[4,2,32,128]{3,2,1,0:T(8,128)S(1)}, f32[4,2,32,128]{3,2,1,0:T(8,128)S(1)}, u32[]{:S(2)}, u32[]{:S(2)}) collective-permute-start(f32[4,2,32,128]{3,2,1,0:T(8,128)S(1)} %get-tuple-element.44), channel_id=1, source_target_pairs={{0,1},{1,0},{2,3},{3,2},{4,5},{5,4},{6,7},{7,6},{8,9},{9,8},{10,11... | collective-permute-start | bytes 393224 | tf_op jit(solution)/shard_map/ppermute | solution.py:367

commit v7 on v5

--- a/solution.py
+++ b/solution.py
@@ -94,8 +94,8 @@
         bs = (2 * pair, 2 * pair + 1)
         x = [jnp.concatenate([s[c, pl.ds(b * LANES, LANES), :] for b in bs], 1) for c in range(2)]
         y = left_gate(*x, m)
-        for c in range(2):
-            for k, b in enumerate(bs):
+        for k, b in enumerate(bs):
+            for c in range(2):
                 store(c, b * LANES, y[c][:, k * LANES : (k + 1) * LANES])
 
 
@@ -324,8 +324,8 @@
 
     def store(c, row, value):
         y[pl.ds(2 * row + c, LANES, stride=2), :] = value
-        if c == 1 and row % PAIR == LANES:
-            at = pl.ds(2 * (row - LANES), 2 * PAIR)
+        if c == 1:
+            at = pl.ds(2 * row, PAIR)
             copies.append(pltpu.make_async_copy(y.at[at], out.at[at], ysems.at[len(copies)]))
             copies[-1].start()
 
@@ -426,7 +426,7 @@
         rows,
         [me, keep, early, far, *w],
         [SMEM] + [VMEM] * 5,
-        interleaved,
+        (interleaved[0], pltpu.SemaphoreType.DMA((4,))),
         [HBM],
     )[0]
     return out.reshape(rows, 2, LANES).transpose(1, 0, 2).reshape(2, total)

time: 34.7 us -> 34.7 us (level)
  no operation moved by 1% of the time
where the time goes in v7:
time: 34.7 us; the launch traced here: 34 us
  starting transfers between devices  12.4 us (36%)
  Pallas kernels  10.9 us (31%)
  waiting for transfers between devices  10.6 us (31%)
    ppermute x13, starting transfers between devices, flipped(): return lax.ppermute(block, 'node', route)  12.4 us
    pallas_call x8, Pallas kernels, call(): pl.pallas_call(functools.partial(kernel, indices), out_shape=outs, in_spe...  10.9 us
    ppermute x13, waiting for transfers between devices, flipped(): return lax.ppermute(block, 'node', route)  10.6 us
  transfers between devices with their start and end apart: 13, of which 9 were waited for; matrix products, arithmetic and copies ran while one was open for 0% of the time, Pallas kernels for 14%

profile of v7, /device:TPU:19, one launch (start us, length us, event | category | flops | bytes accessed | tf_op | source)
XLA Modules:
  0.0 34.0 jit_solution(3992348597276701910)
XLA Ops:
  0.0 3.7 %first_kernel.1 = (f32[2,2,64,128]{3,2,1,0:T(8,128)S(1)}, f32[2,2,64,128]{3,2,1,0:T(8,128)S(1)}, f32[2,64,128]{2,1,0:T(8,128)S(1)}, f32[2,64,128]{2,1,0:T(8,128)S(1)}, f32[2,2,64,128]{3,2,1,0:T(8,128)S(1)}) custom-call(s32[1]{0:T(128)} %bitcast.me_ref, f32[1024,128]{1,0:T(8,128)} %bitcast.25, f32[2,12,128,128]{3,2,1,0:T(8,128)} %gates.9), custom_call_target="tpu_custom_call" | custom-call | tf_op jit(solution)/shard_map/first_kernel/pallas_call | solution.py:347
  3.7 0.7 %collective-permute-start = (f32[2,2,64,128]{3,2,1,0:T(8,128)S(1)}, f32[2,2,64,128]{3,2,1,0:T(8,128)S(1)}, u32[]{:S(2)}, u32[]{:S(2)}) collective-permute-start(f32[2,2,64,128]{3,2,1,0:T(8,128)S(1)} %get-tuple-element.29), channel_id=1, source_target_pairs={{0,1},{1,0},{2,3},{3,2},{4,5},{5,4},{6,7},{7,6},{8,9},{9,8},{10,11... | collective-permute-start | bytes 393224 | tf_op jit(solution)/shard_map/ppermute | solution.py:367
  4.5 1.3 %collective-permute-start.1 = (f32[2,2,64,128]{3,2,1,0:T(8,128)S(1)}, f32[2,2,64,128]{3,2,1,0:T(8,128)S(1)}, u32[]{:S(2)}, u32[]{:S(2)}) collective-permute-start(f32[2,2,64,128]{3,2,1,0:T(8,128)S(1)} %get-tuple-element.31), channel_id=1, source_target_pairs={{0,2},{1,3},{2,0},{3,1},{4,6},{5,7},{6,4},{7,5},{8,10},{9,11},{10,... | collective-permute-start | bytes 393224 | tf_op jit(solution)/shard_map/ppermute | solution.py:367
  5.7 1.3 %collective-permute-start.2 = (f32[2,2,64,128]{3,2,1,0:T(8,128)S(1)}, f32[2,2,64,128]{3,2,1,0:T(8,128)S(1)}, u32[]{:S(2)}, u32[]{:S(2)}) collective-permute-start(f32[2,2,64,128]{3,2,1,0:T(8,128)S(1)} %get-tuple-element.32), channel_id=1, source_target_pairs={{0,4},{1,5},{2,6},{3,7},{4,0},{5,1},{6,2},{7,3},{8,12},{9,13},{10,... | collective-permute-start | bytes 393224 | tf_op jit(solution)/shard_map/ppermute | solution.py:367
  7.0 0.0 collective-permute-done.recv
  7.0 1.5 %before_lower.1 = (f32[2,2,64,128]{3,2,1,0:T(8,128)S(1)}, f32[2,2,64,128]{3,2,1,0:T(8,128)S(1)}) custom-call(f32[2,64,128]{2,1,0:T(8,128)S(1)} %get-tuple-element.27.own0, f32[2,64,128]{2,1,0:T(8,128)S(1)} %get-tuple-element.28.own3, f32[2,2,64,128]{3,2,1,0:T(8,128)S(1)} %collective-permute-done.recv, f32[2,12,128,128]{3,2,1,0:T(8,128)S(1)} %copy-done), custom_call_target="tpu_custom_call" | custom-call | flops 2000000000 | bytes 262144 | tf_op jit(solution)/shard_map/before_lower/pallas_call | solution.py:347
  8.5 0.7 %collective-permute-start.3 = (f32[2,2,64,128]{3,2,1,0:T(8,128)S(1)}, f32[2,2,64,128]{3,2,1,0:T(8,128)S(1)}, u32[]{:S(2)}, u32[]{:S(2)}) collective-permute-start(f32[2,2,64,128]{3,2,1,0:T(8,128)S(1)} %get-tuple-element.34), channel_id=1, source_target_pairs={{0,6},{1,7},{2,4},{3,5},{4,2},{5,3},{6,0},{7,1},{8,14},{9,15},{10,... | collective-permute-start | bytes 393224 | tf_op jit(solution)/shard_map/ppermute | solution.py:367
  9.3 0.3 collective-permute-done.1.r1
  9.6 0.9 %collective-permute-done.2.r2 = f32[2,2,64,128]{3,2,1,0:T(8,128)S(1)} collective-permute-done((f32[2,2,64,128]{3,2,1,0:T(8,128)S(1)}, f32[2,2,64,128]{3,2,1,0:T(8,128)S(1)}, u32[]{:S(2)}, u32[]{:S(2)}) %collective-permute-start.2) | collective-permute-done | bytes 131104 | tf_op jit(solution)/shard_map/ppermute | solution.py:367
  10.5 1.6 %after_lower.1 = (f32[2,2,64,128]{3,2,1,0:T(8,128)S(1)}, f32[2,64,128]{2,1,0:T(8,128)S(1)}, f32[2,64,128]{2,1,0:T(8,128)S(1)}, bf16[2,256,256]{2,1,0:T(8,128)(2,1)S(1)}, bf16[2,256,256]{2,1,0:T(8,128)(2,1)S(1)}) custom-call(f32[2,2,64,128]{3,2,1,0:T(8,128)S(1)} %collective-permute-done.1.r1, f32[2,2,64,128]{3,2,1,0:T(8,128)S(1)} %collective-permute-done.2.r2, ...), custom_call_target="tpu_custom_call" | custom-call | flops 2000000000 | bytes 262144 | tf_op jit(solution)/shard_map/after_lower/pallas_call | solution.py:347
  12.0 1.2 %collective-permute-start.4 = (f32[2,64,128]{2,1,0:T(8,128)S(1)}, f32[2,64,128]{2,1,0:T(8,128)S(1)}, u32[]{:S(2)}, u32[]{:S(2)}) collective-permute-start(f32[2,64,128]{2,1,0:T(8,128)S(1)} %get-tuple-element.35), channel_id=1, source_target_pairs={{0,1},{1,0},{2,3},{3,2},{4,5},{5,4},{6,7},{7,6},{8,9},{9,8},{10,11... | collective-permute-start | bytes 196616 | tf_op jit(solution)/shard_map/ppermute | solution.py:367
  13.3 0.1 collective-permute-start.5
  13.4 0.8 %collective-permute-done.4.post1 = f32[2,64,128]{2,1,0:T(8,128)S(1)} collective-permute-done((f32[2,64,128]{2,1,0:T(8,128)S(1)}, f32[2,64,128]{2,1,0:T(8,128)S(1)}, u32[]{:S(2)}, u32[]{:S(2)}) %collective-permute-start.4) | collective-permute-done | bytes 65568 | tf_op jit(solution)/shard_map/ppermute | solution.py:367
  14.2 0.4 %collective-permute-done.5.post2 = f32[2,64,128]{2,1,0:T(8,128)S(1)} collective-permute-done((f32[2,64,128]{2,1,0:T(8,128)S(1)}, f32[2,64,128]{2,1,0:T(8,128)S(1)}, u32[]{:S(2)}, u32[]{:S(2)}) %collective-permute-start.5) | collective-permute-done | bytes 65568 | tf_op jit(solution)/shard_map/ppermute | solution.py:367
  14.5 0.0 collective-permute-done.3.r3
  14.5 0.8 %second_kernel.1 = (f32[3,2,2,32,128]{4,3,2,1,0:T(8,128)S(1)}, f32[8,2,32,128]{3,2,1,0:T(8,128)S(1)}, f32[2,32,128]{2,1,0:T(8,128)S(1)}, f32[2,32,128]{2,1,0:T(8,128)S(1)}) custom-call(s32[1]{0:T(128)} %bitcast.me_ref, f32[2,2,64,128]{3,2,1,0:T(8,128)S(1)} %get-tuple-element.30.p0, f32[2,2,64,128]{3,2,1,0:T(8,128)S(1)} %get-tuple-element.33.near, ...), custom_call_target="tpu_custom_call" | custom-call | tf_op jit(solution)/shard_map/second_kernel/pallas_call | solution.py:347
  15.4 0.9 %collective-permute-start.6 = (f32[8,2,32,128]{3,2,1,0:T(8,128)S(1)}, f32[8,2,32,128]{3,2,1,0:T(8,128)S(1)}, u32[]{:S(2)}, u32[]{:S(2)}) collective-permute-start(f32[8,2,32,128]{3,2,1,0:T(8,128)S(1)} %get-tuple-element.40), channel_id=1, source_target_pairs={{0,1},{1,0},{2,3},{3,2},{4,5},{5,4},{6,7},{7,6},{8,9},{9,8},{10,11... | collective-permute-start | bytes 786440 | tf_op jit(solution)/shard_map/ppermute | solution.py:367
  16.3 1.1 %collective-permute-done.6 = f32[8,2,32,128]{3,2,1,0:T(8,128)S(1)} collective-permute-done((f32[8,2,32,128]{3,2,1,0:T(8,128)S(1)}, f32[8,2,32,128]{3,2,1,0:T(8,128)S(1)}, u32[]{:S(2)}, u32[]{:S(2)}) %collective-permute-start.6) | collective-permute-done | bytes 262176 | tf_op jit(solution)/shard_map/ppermute | solution.py:367
  17.5 0.1 collective-permute-start.7
  17.6 2.3 %collective-permute-start.8 = (f32[2,2,2,32,128]{4,3,2,0,1:T(8,128)S(1)}, f32[2,2,2,32,128]{4,3,2,0,1:T(8,128)S(1)}, u32[]{:S(2)}, u32[]{:S(2)}) collective-permute-start(f32[2,2,2,32,128]{4,3,2,0,1:T(8,128)S(1)} %pad_maximum_fusion.1), channel_id=1, source_target_pairs={{0,4},{1,7},{2,6},{3,5},{4,0},{5,3},{6,2},{7,1},{8,12},{9,15},{10,... | collective-permute-start | bytes 393224 | tf_op jit(solution)/shard_map/ppermute | solution.py:367
  19.9 0.3 collective-permute-start.9
  20.2 0.7 %before_kernel.1 = (f32[2,2,32,128]{3,2,1,0:T(8,128)S(1)}, f32[2,2,32,128]{3,2,1,0:T(8,128)S(1)}) custom-call(f32[2,2,32,128]{3,2,1,0:T(8,128)S(1)} %get-tuple-element.54.own, f32[2,2,32,128]{3,2,1,0:T(8,128)S(1)} %get-tuple-element.49.recv, f32[2,12,128,128]{3,2,1,0:T(8,128)S(1)} %copy-done), custom_call_target="tpu_custom_call" | custom-call | flops 1000000000 | bytes 262144 | tf_op jit(solution)/shard_map/before_kernel/pallas_call | solution.py:347
  20.9 2.3 %collective-permute-start.11 = (f32[2,2,32,128]{3,2,1,0:T(8,128)S(1)}, f32[2,2,32,128]{3,2,1,0:T(8,128)S(1)}, u32[]{:S(2)}, u32[]{:S(2)}) collective-permute-start(f32[2,2,32,128]{3,2,1,0:T(8,128)S(1)} %get-tuple-element.45), channel_id=1, source_target_pairs={{0,12},{1,15},{2,14},{3,13},{4,8},{5,11},{6,10},{7,9},{8,4},{9,7},... | collective-permute-start | bytes 196616 | tf_op jit(solution)/shard_map/ppermute | solution.py:367
  23.2 0.4 %collective-permute-start.12 = (f32[2,2,32,128]{3,2,1,0:T(8,128)S(1)}, f32[2,2,32,128]{3,2,1,0:T(8,128)S(1)}, u32[]{:S(2)}, u32[]{:S(2)}) collective-permute-start(f32[2,2,32,128]{3,2,1,0:T(8,128)S(1)} %get-tuple-element.46), channel_id=1, source_target_pairs={{0,13},{1,14},{2,15},{3,12},{4,9},{5,10},{6,11},{7,8},{8,5},{9,6},... | collective-permute-start | bytes 196616 | tf_op jit(solution)/shard_map/ppermute | solution.py:367
  23.6 1.1 %collective-permute-done.7 = f32[2,2,2,32,128]{4,3,2,0,1:T(8,128)S(1)} collective-permute-done((f32[2,2,2,32,128]{4,3,2,0,1:T(8,128)S(1)}, f32[2,2,2,32,128]{4,3,2,0,1:T(8,128)S(1)}, u32[]{:S(2)}, u32[]{:S(2)}) %collective-permute-start.7) | collective-permute-done | bytes 131104 | tf_op jit(solution)/shard_map/ppermute | solution.py:367
  24.8 1.6 %collective-permute-done.8 = f32[2,2,2,32,128]{4,3,2,0,1:T(8,128)S(1)} collective-permute-done((f32[2,2,2,32,128]{4,3,2,0,1:T(8,128)S(1)}, f32[2,2,2,32,128]{4,3,2,0,1:T(8,128)S(1)}, u32[]{:S(2)}, u32[]{:S(2)}) %collective-permute-start.8) | collective-permute-done | bytes 131104 | tf_op jit(solution)/shard_map/ppermute | solution.py:367
  26.4 0.0 collective-permute-done.9.y1
  26.4 0.9 %after_kernel.1 = (f32[8,2,32,128]{3,2,1,0:T(8,128)S(1)}, f32[4,2,32,128]{3,2,1,0:T(8,128)S(1)}, bf16[2,256,256]{2,1,0:T(8,128)(2,1)S(1)}, bf16[2,256,256]{2,1,0:T(8,128)(2,1)S(1)}) custom-call(f32[2,2,2,32,128]{4,3,2,1,0:T(8,128)S(1)} %copy.4.a0, f32[2,2,2,32,128]{4,3,2,1,0:T(8,128)S(1)} %copy.5.a1, f32[2,2,32,128]{3,2,1,0:T(8,128)S(1)} %collective-permute-done.9.y1, ...), custom_call_target="tpu_custom_call" | custom-call | flops 2000000000 | bytes 262144 | tf_op jit(solution)/shard_map/after_kernel/pallas_call | solution.py:347
  27.3 0.7 %collective-permute-start.10 = (f32[4,2,32,128]{3,2,1,0:T(8,128)S(1)}, f32[4,2,32,128]{3,2,1,0:T(8,128)S(1)}, u32[]{:S(2)}, u32[]{:S(2)}) collective-permute-start(f32[4,2,32,128]{3,2,1,0:T(8,128)S(1)} %get-tuple-element.44), channel_id=1, source_target_pairs={{0,1},{1,0},{2,3},{3,2},{4,5},{5,4},{6,7},{7,6},{8,9},{9,8},{10,11... | collective-permute-start | bytes 393224 | tf_op jit(solution)/shard_map/ppermute | solution.py:367
  28.0 3.5 %collective-permute-done.11.mine = f32[2,2,32,128]{3,2,1,0:T(8,128)S(1)} collective-permute-done((f32[2,2,32,128]{3,2,1,0:T(8,128)S(1)}, f32[2,2,32,128]{3,2,1,0:T(8,128)S(1)}, u32[]{:S(2)}, u32[]{:S(2)}) %collective-permute-start.11) | collective-permute-done | bytes 65568 | tf_op jit(solution)/shard_map/ppermute | solution.py:367
  31.5 0.9 %collective-permute-done.12.late = f32[2,2,32,128]{3,2,1,0:T(8,128)S(1)} collective-permute-done((f32[2,2,32,128]{3,2,1,0:T(8,128)S(1)}, f32[2,2,32,128]{3,2,1,0:T(8,128)S(1)}, u32[]{:S(2)}, u32[]{:S(2)}) %collective-permute-start.12) | collective-permute-done | bytes 65568 | tf_op jit(solution)/shard_map/ppermute | solution.py:367
  32.4 1.6 %third_kernel.1 = f32[1024,128]{1,0:T(8,128)} custom-call(s32[1]{0:T(128)} %bitcast.me_ref, f32[8,2,32,128]{3,2,1,0:T(8,128)S(1)} %get-tuple-element.43.keep, f32[4,2,32,128]{3,2,1,0:T(8,128)S(1)} %collective-permute-done.10.early, f32[4,2,32,128]{3,2,1,0:T(8,128)S(1)} %join_kernel.1.far, bf16[2,256,256]{2,1,0:T(8,128)(2,1)S(1)} %get-tuple-element.47.wh, ...), custom_call_target="tpu_custom_call" | custom-call | tf_op jit(solution)/shard_map/third_kernel/pallas_call | solution.py:347
  (12 shorter events, 0.1 us)
Async XLA Ops:
  0.0 7.0 %copy-start = (f32[2,12,128,128]{3,2,1,0:T(8,128)S(1)}, f32[2,12,128,128]{3,2,1,0:T(8,128)}, u32[]{:S(2)}) copy-start(f32[2,12,128,128]{3,2,1,0:T(8,128)} %gates.9) | copy-start | bytes 4718596
  3.7 3.3 %collective-permute-start = (f32[2,2,64,128]{3,2,1,0:T(8,128)S(1)}, f32[2,2,64,128]{3,2,1,0:T(8,128)S(1)}, u32[]{:S(2)}, u32[]{:S(2)}) collective-permute-start(f32[2,2,64,128]{3,2,1,0:T(8,128)S(1)} %get-tuple-element.29), channel_id=1, source_target_pairs={{0,1},{1,0},{2,3},{3,2},{4,5},{5,4},{6,7},{7,6},{8,9},{9,8},{10,11... | collective-permute-start | bytes 393224 | tf_op jit(solution)/shard_map/ppermute | solution.py:367
  4.5 5.1 %collective-permute-start.1 = (f32[2,2,64,128]{3,2,1,0:T(8,128)S(1)}, f32[2,2,64,128]{3,2,1,0:T(8,128)S(1)}, u32[]{:S(2)}, u32[]{:S(2)}) collective-permute-start(f32[2,2,64,128]{3,2,1,0:T(8,128)S(1)} %get-tuple-element.31), channel_id=1, source_target_pairs={{0,2},{1,3},{2,0},{3,1},{4,6},{5,7},{6,4},{7,5},{8,10},{9,11},{10,... | collective-permute-start | bytes 393224 | tf_op jit(solution)/shard_map/ppermute | solution.py:367
  5.7 4.7 %collective-permute-start.2 = (f32[2,2,64,128]{3,2,1,0:T(8,128)S(1)}, f32[2,2,64,128]{3,2,1,0:T(8,128)S(1)}, u32[]{:S(2)}, u32[]{:S(2)}) collective-permute-start(f32[2,2,64,128]{3,2,1,0:T(8,128)S(1)} %get-tuple-element.32), channel_id=1, source_target_pairs={{0,4},{1,5},{2,6},{3,7},{4,0},{5,1},{6,2},{7,3},{8,12},{9,13},{10,... | collective-permute-start | bytes 393224 | tf_op jit(solution)/shard_map/ppermute | solution.py:367
  8.5 6.0 %collective-permute-start.3 = (f32[2,2,64,128]{3,2,1,0:T(8,128)S(1)}, f32[2,2,64,128]{3,2,1,0:T(8,128)S(1)}, u32[]{:S(2)}, u32[]{:S(2)}) collective-permute-start(f32[2,2,64,128]{3,2,1,0:T(8,128)S(1)} %get-tuple-element.34), channel_id=1, source_target_pairs={{0,6},{1,7},{2,4},{3,5},{4,2},{5,3},{6,0},{7,1},{8,14},{9,15},{10,... | collective-permute-start | bytes 393224 | tf_op jit(solution)/shard_map/ppermute | solution.py:367
  12.0 2.1 %collective-permute-start.4 = (f32[2,64,128]{2,1,0:T(8,128)S(1)}, f32[2,64,128]{2,1,0:T(8,128)S(1)}, u32[]{:S(2)}, u32[]{:S(2)}) collective-permute-start(f32[2,64,128]{2,1,0:T(8,128)S(1)} %get-tuple-element.35), channel_id=1, source_target_pairs={{0,1},{1,0},{2,3},{3,2},{4,5},{5,4},{6,7},{7,6},{8,9},{9,8},{10,11... | collective-permute-start | bytes 196616 | tf_op jit(solution)/shard_map/ppermute | solution.py:367
  13.3 1.3 %collective-permute-start.5 = (f32[2,64,128]{2,1,0:T(8,128)S(1)}, f32[2,64,128]{2,1,0:T(8,128)S(1)}, u32[]{:S(2)}, u32[]{:S(2)}) collective-permute-start(f32[2,64,128]{2,1,0:T(8,128)S(1)} %get-tuple-element.36), channel_id=1, source_target_pairs={{0,1},{1,0},{2,3},{3,2},{4,5},{5,4},{6,7},{7,6},{8,9},{9,8},{10,11... | collective-permute-start | bytes 196616 | tf_op jit(solution)/shard_map/ppermute | solution.py:367
  15.4 2.1 %collective-permute-start.6 = (f32[8,2,32,128]{3,2,1,0:T(8,128)S(1)}, f32[8,2,32,128]{3,2,1,0:T(8,128)S(1)}, u32[]{:S(2)}, u32[]{:S(2)}) collective-permute-start(f32[8,2,32,128]{3,2,1,0:T(8,128)S(1)} %get-tuple-element.40), channel_id=1, source_target_pairs={{0,1},{1,0},{2,3},{3,2},{4,5},{5,4},{6,7},{7,6},{8,9},{9,8},{10,11... | collective-permute-start | bytes 786440 | tf_op jit(solution)/shard_map/ppermute | solution.py:367
  17.5 7.3 %collective-permute-start.7 = (f32[2,2,2,32,128]{4,3,2,0,1:T(8,128)S(1)}, f32[2,2,2,32,128]{4,3,2,0,1:T(8,128)S(1)}, u32[]{:S(2)}, u32[]{:S(2)}) collective-permute-start(f32[2,2,2,32,128]{4,3,2,0,1:T(8,128)S(1)} %pad_maximum_fusion), channel_id=1, source_target_pairs={{0,8},{1,11},{2,10},{3,9},{4,12},{5,15},{6,14},{7,13},{8,0},{9,3},... | collective-permute-start | bytes 393224 | tf_op jit(solution)/shard_map/ppermute | solution.py:367
  17.6 8.7 %collective-permute-start.8 = (f32[2,2,2,32,128]{4,3,2,0,1:T(8,128)S(1)}, f32[2,2,2,32,128]{4,3,2,0,1:T(8,128)S(1)}, u32[]{:S(2)}, u32[]{:S(2)}) collective-permute-start(f32[2,2,2,32,128]{4,3,2,0,1:T(8,128)S(1)} %pad_maximum_fusion.1), channel_id=1, source_target_pairs={{0,4},{1,7},{2,6},{3,5},{4,0},{5,3},{6,2},{7,1},{8,12},{9,15},{10,... | collective-permute-start | bytes 393224 | tf_op jit(solution)/shard_map/ppermute | solution.py:367
  19.9 6.4 %collective-permute-start.9 = (f32[2,2,32,128]{3,2,1,0:T(8,128)S(1)}, f32[2,2,32,128]{3,2,1,0:T(8,128)S(1)}, u32[]{:S(2)}, u32[]{:S(2)}) collective-permute-start(f32[2,2,32,128]{3,2,1,0:T(8,128)S(1)} %pad_maximum_fusion.2), channel_id=1, source_target_pairs={{0,2},{1,3},{2,0},{3,1},{4,6},{5,7},{6,4},{7,5},{8,10},{9,11},{10,... | collective-permute-start | bytes 196616 | tf_op jit(solution)/shard_map/ppermute | solution.py:367
  20.9 10.6 %collective-permute-start.11 = (f32[2,2,32,128]{3,2,1,0:T(8,128)S(1)}, f32[2,2,32,128]{3,2,1,0:T(8,128)S(1)}, u32[]{:S(2)}, u32[]{:S(2)}) collective-permute-start(f32[2,2,32,128]{3,2,1,0:T(8,128)S(1)} %get-tuple-element.45), channel_id=1, source_target_pairs={{0,12},{1,15},{2,14},{3,13},{4,8},{5,11},{6,10},{7,9},{8,4},{9,7},... | collective-permute-start | bytes 196616 | tf_op jit(solution)/shard_map/ppermute | solution.py:367
  23.2 9.2 %collective-permute-start.12 = (f32[2,2,32,128]{3,2,1,0:T(8,128)S(1)}, f32[2,2,32,128]{3,2,1,0:T(8,128)S(1)}, u32[]{:S(2)}, u32[]{:S(2)}) collective-permute-start(f32[2,2,32,128]{3,2,1,0:T(8,128)S(1)} %get-tuple-element.46), channel_id=1, source_target_pairs={{0,13},{1,14},{2,15},{3,12},{4,9},{5,10},{6,11},{7,8},{8,5},{9,6},... | collective-permute-start | bytes 196616 | tf_op jit(solution)/shard_map/ppermute | solution.py:367
  27.3 5.1 %collective-permute-start.10 = (f32[4,2,32,128]{3,2,1,0:T(8,128)S(1)}, f32[4,2,32,128]{3,2,1,0:T(8,128)S(1)}, u32[]{:S(2)}, u32[]{:S(2)}) collective-permute-start(f32[4,2,32,128]{3,2,1,0:T(8,128)S(1)} %get-tuple-element.44), channel_id=1, source_target_pairs={{0,1},{1,0},{2,3},{3,2},{4,5},{5,4},{6,7},{7,6},{8,9},{9,8},{10,11... | collective-permute-start | bytes 393224 | tf_op jit(solution)/shard_map/ppermute | solution.py:367
